TPU v7x, 128 devices: a whole 4x4x4 slice. The times are simulated.
128 devices in a mesh: rep: 16 (over z, x_hi, core), fsdp: 8 (over y, x_lo).
Axes of the slice: x: 4 (x_hi: 2, x_lo: 2; x = x_hi * 2 + x_lo), y: 4, z: 4, core: 2. Of those that a mesh axis runs over, the one named last changes fastest.
Arguments:
- tokens: bfloat16 [16, 2, 1024, 8192], P('rep', None, 'fsdp'), may hold values from -6 to 6
- targets: bfloat16 [16, 2, 1024, 1024], P('rep', None, 'fsdp'), may hold values from -6 to 6
- params: float32 [16, 8192, 1024], P('rep', 'fsdp'), may hold values from -6 to 6
- moment1: bfloat16 [16, 8192, 1024], P('rep', 'fsdp'), may hold values from -2 to 2
- moment2: bfloat16 [16, 8192, 1024], P('rep', 'fsdp'), may hold values from 0.0099487305 to 1
- stale_delta: float32 [16, 8192, 512], P('rep', 'fsdp'), may hold values from -6 to 6
- anchor: float32 [2, 8, 1024, 512], P(None, 'fsdp', 'rep'), may hold values from -6 to 6
- momentum: float32 [2, 8, 1024, 512], P(None, 'fsdp', 'rep'), may hold values from -4 to 4
- plan: int32 [1], replicated, may hold values from 0 to 1
Outputs:
- params_out: float32 [16, 8192, 1024], P('rep', 'fsdp')
- moment1_out: bfloat16 [16, 8192, 1024], P('rep', 'fsdp')
- moment2_out: bfloat16 [16, 8192, 1024], P('rep', 'fsdp')
- anchor_out: float32 [2, 8, 1024, 512], P(None, 'fsdp', 'rep')
- momentum_out: float32 [2, 8, 1024, 512], P(None, 'fsdp', 'rep')
All inputs are finite; a program needn't handle non-finite values.
Results may differ from a plain program's by a relative error of at most 0.011.
Values may be sent and summed in bfloat16 or wider, within the bound.
No kernel may reach another device: no remote copies, remote signals or barrier semaphores. Data moves between devices by JAX's collectives and lax.ppermute only.
A program may use at most 128 MiB of HBM per device.

v0:
```python
import math

import jax
import jax.numpy as jnp
from jax import lax
from jax.sharding import PartitionSpec as P

beta_one = 0.9
beta_two = 0.95
inner_rate = 0.02
decay_rate = 0.1
adam_eps = 1e-08
outer_rate = 0.7
outer_mu = 0.9
mix_weight = 0.5


def stored(value):
    return lax.optimization_barrier(value.astype(jnp.bfloat16))


def on_device(tokens, targets, params, moment1, moment2, stale_delta, anchor, momentum, plan):
    width = tokens.shape[3]
    inv_root = 1.0 / math.sqrt(width)
    replicas = lax.axis_size("rep")
    weights = params[0]
    first_b = moment1[0]
    second_b = moment2[0]
    first = first_b.astype(jnp.float32)
    second = second_b.astype(jnp.float32)
    own_rows = weights.shape[0]
    key_width = weights.shape[1]
    tok_rows = tokens.shape[2]
    fragment = plan[0]
    frag_cols = stale_delta.shape[2]
    delta = stale_delta[0]
    anchor_rows = lax.dynamic_index_in_dim(anchor, fragment, 0, keepdims=False)[0]
    moment_rows = lax.dynamic_index_in_dim(momentum, fragment, 0, keepdims=False)[0]
    slice_rows = anchor_rows.shape[0]
    total = lax.psum(delta.astype(jnp.bfloat16), "rep").astype(jnp.float32)
    anchor_old, moment_old = (
        lax.all_gather(anchor_rows.astype(jnp.bfloat16), "rep", axis=0, tiled=True).astype(
            anchor_rows.dtype
        ),
        lax.all_gather(moment_rows.astype(jnp.bfloat16), "rep", axis=0, tiled=True).astype(
            moment_rows.dtype
        ),
    )
    mean_full = total / replicas
    moment_all = outer_mu * moment_old + mean_full
    anchor_full = anchor_old - outer_rate * (mean_full + outer_mu * moment_all)
    offset = lax.axis_index("rep") * slice_rows
    moment_new = lax.dynamic_slice_in_dim(moment_all, offset, slice_rows, 0)
    anchor_new = lax.dynamic_slice_in_dim(anchor_full, offset, slice_rows, 0)
    for step in range(tokens.shape[1]):
        sliced = lax.all_to_all(tokens[0, step], "fsdp", split_axis=1, concat_axis=0, tiled=True)
        narrow = weights.astype(jnp.bfloat16)

        def partial_keys(start, count, sliced=sliced, narrow=narrow):
            return jnp.dot(sliced, narrow, preferred_element_type=jnp.float32)

        keys = (
            lax.psum_scatter(
                partial_keys(jnp.int32(0), lax.axis_size("fsdp") * tok_rows),
                "fsdp",
                scatter_dimension=0,
                tiled=True,
            )
            * inv_root
        )
        resid = (keys - targets[0, step].astype(jnp.float32)).astype(jnp.bfloat16)

        def add_grad(carry, piece, start, sliced=sliced):
            return lax.dot_general(
                sliced, piece, (((0,), (0,)), ((), ())), preferred_element_type=jnp.float32
            )

        empty = jnp.zeros((own_rows, key_width), jnp.float32)
        grad = (
            add_grad(empty, lax.all_gather(resid, "fsdp", axis=0, tiled=True), jnp.int32(0))
            * inv_root
        )
        first = beta_one * first + (1.0 - beta_one) * grad
        second = beta_two * second + (1.0 - beta_two) * grad * grad
        weights = weights - inner_rate * (
            first / (jnp.sqrt(second) + adam_eps) + decay_rate * weights
        )
        first_b = stored(first)
        second_b = stored(second)
        first = first_b.astype(jnp.float32)
        second = second_b.astype(jnp.float32)
    column = fragment * frag_cols
    local_cols = lax.dynamic_slice_in_dim(weights, column, frag_cols, 1)
    mixed = mix_weight * local_cols + (1.0 - mix_weight) * anchor_full
    weights = lax.dynamic_update_slice_in_dim(weights, mixed, column, 1)
    anchor_out = lax.dynamic_update_index_in_dim(anchor, anchor_new[None], fragment, 0)
    momentum_out = lax.dynamic_update_index_in_dim(momentum, moment_new[None], fragment, 0)
    return (weights[None], first_b[None], second_b[None], anchor_out, momentum_out)


def solution(mesh):
    return jax.shard_map(
        on_device,
        mesh=mesh,
        in_specs=(
            P("rep", None, "fsdp", None),
            P("rep", None, "fsdp", None),
            P("rep", "fsdp", None),
            P("rep", "fsdp", None),
            P("rep", "fsdp", None),
            P("rep", "fsdp", None),
            P(None, "fsdp", "rep", None),
            P(None, "fsdp", "rep", None),
            P(),
        ),
        out_specs=(
            P("rep", "fsdp", None),
            P("rep", "fsdp", None),
            P("rep", "fsdp", None),
            P(None, "fsdp", "rep", None),
            P(None, "fsdp", "rep", None),
        ),
        check_vma=False,
    )
```

profile of v0, /device:TPU:0, one launch (start us, length us, event | category | flops | bytes accessed | tf_op | source)
XLA Modules:
  0.0 597.8 jit_solution(7033476439077851119)
XLA Ops:
  9.9 4.7 fusion.12
  14.6 3.2 copy.67
  17.8 32.6 %all_to_all.38 = bf16[128,8,1024]{0,2,1:T(8,128)(2,1)} all-to-all(bf16[128,8,1024]{0,2,1:T(8,128)(2,1)S(1)} %bitcast.97), channel_id=1, replica_groups=mesh['rep'=16,'fsdp'=8] {'fsdp'}, dimensions={1} | all-to-all | bytes 4194304 | tf_op jit(solution)/shard_map/all_to_all | solution.py:56
  50.5 2.9 copy.53
  53.3 7.3 %fusion.4 = f32[1024,1024]{1,0:T(8,128)} fusion(bf16[1024,1024]{1,0:T(8,128)(2,1)S(1)} %bitcast.102, f32[1,1024,1024]{2,1,0:T(8,128)} %param.11), kind=kOutput, calls=%fused_computation.15 | convolution fusion | flops 2148532224 | bytes 10485760 | tf_op jit(solution)/shard_map/dot_general | solution.py:60
  60.7 91.3 %reduce-scatter.3.cloned.1.call-done = f32[128,1024]{1,0:T(8,128)} async-done(((f32[1024,1024]{1,0:T(8,128)}), f32[128,1024]{1,0:T(8,128)}) %reduce-scatter.3.cloned.1.call-update) | async-done | bytes 524304 | tf_op jit(solution)/shard_map/reduce_scatter | solution.py:63
  152.0 1.8 fusion.11
  153.9 2.5 copy.68
  156.3 3.9 all-to-all-start.1
  160.5 5.4 copy.50
  165.8 3.9 copy.51
  169.8 3.9 copy.54
  173.7 35.3 %all-to-all-done.1 = bf16[128,8,1024]{0,2,1:T(8,128)(2,1)S(1)} async-done(((bf16[128,8,1024]{0,2,1:T(8,128)(2,1)}), bf16[128,8,1024]{0,2,1:T(8,128)(2,1)S(1)}, u32[]{:S(2)}, u32[]{:S(2)}) %all-to-all-start.1) | async-done | bytes 2097184 | tf_op jit(solution)/shard_map/all_to_all | solution.py:56
  209.0 2.6 copy.56
  211.6 14.8 %all-gather.7.cloned.1.call-done = bf16[1024,1024]{1,0:T(8,128)(2,1)} async-done(((bf16[128,1024]{1,0:T(8,128)(2,1)}), bf16[1024,1024]{1,0:T(8,128)(2,1)}) %all-gather.7.cloned.1.call-update) | async-done | bytes 2097168 | tf_op jit(solution)/shard_map/all_gather | solution.py:80
  226.5 12.1 %fusion.8 = (bf16[1024,1024]{0,1:T(8,128)(2,1)}, f32[1024,1024]{0,1:T(8,128)S(1)}, bf16[1024,1024]{0,1:T(8,128)(2,1)}) fusion(bf16[1,1024,1024]{1,2,0:T(8,128)(2,1)} %copy.54, bf16[1,1024,1024]{1,2,0:T(8,128)(2,1)} %copy.51, f32[1,1024,1024]{1,2,0:T(8,128)} %copy.50, bf16[1024,1024]{1,0:T(8,128)(2,1)} %all-gather.7.cloned.1.call-done, ...), kind=kOutput, calls=%fused_computation.20 | convolution fusion | flops 2166358016 | bytes 20971520 | tf_op jit(solution)/shard_map/dot_general | solution.py:74
  238.6 2.0 copy-done.9
  240.6 4.4 convolution_bitcast_fusion
  249.0 91.3 %reduce-scatter.5.cloned.1.call-done = f32[128,1024]{1,0:T(8,128)} async-done(((f32[1024,1024]{1,0:T(8,128)}), f32[128,1024]{1,0:T(8,128)}) %reduce-scatter.5.cloned.1.call-update) | async-done | bytes 524304 | tf_op jit(solution)/shard_map/reduce_scatter | solution.py:63
  340.3 1.8 fusion.10
  342.2 1.5 copy.60
  343.7 20.2 %all-gather.11.cloned.1.call-done = bf16[1,1,1024,512]{3,2,1,0:T(8,128)(2,1)} async-done(((bf16[1,1,64,512]{3,2,1,0:T(8,128)(2,1)}), bf16[1,1,1024,512]{3,2,1,0:T(8,128)(2,1)}) %all-gather.11.cloned.1.call-update) | async-done | bytes 1048592 | tf_op jit(solution)/shard_map/all_gather | solution.py:42
  363.9 1.5 copy.58
  365.4 139.8 %all-reduce.2.cloned.1.call-done = bf16[1024,512]{0,1:T(8,128)(2,1)} async-done(((bf16[1024,512]{0,1:T(8,128)(2,1)}), bf16[1024,512]{0,1:T(8,128)(2,1)}) %all-reduce.2.cloned.1.call-update) | async-done | bytes 1048592 | tf_op jit(solution)/shard_map/psum | solution.py:40
  505.1 3.0 bitcast_add_fusion.4
  508.2 52.4 %all-gather.9.cloned.1.call-done = bf16[1024,1024]{1,0:T(8,128)(2,1)} async-done(((bf16[128,1024]{1,0:T(8,128)(2,1)}), bf16[1024,1024]{1,0:T(8,128)(2,1)}) %all-gather.9.cloned.1.call-update) | async-done | bytes 2097168 | tf_op jit(solution)/shard_map/all_gather | solution.py:80
  560.6 12.1 %fusion.6 = (bf16[1024,1024]{0,1:T(8,128)(2,1)}, f32[1024,1024]{0,1:T(8,128)S(1)}, bf16[1024,1024]{0,1:T(8,128)(2,1)}) fusion(bf16[1024,1024]{0,1:T(8,128)(2,1)} %get-tuple-element.30, f32[1024,1024]{0,1:T(8,128)} %copy-done.9, bf16[1024,1024]{0,1:T(8,128)(2,1)} %get-tuple-element.32, bf16[1024,1024]{1,0:T(8,128)(2,1)} %all-gather.9.cloned.1.call-done, ...), kind=kOutput, calls=%fused_computation.18 | convolution fusion | flops 2166358016 | bytes 20971520 | tf_op jit(solution)/shard_map/dot_general | solution.py:74
  572.7 2.0 copy.70
  574.7 2.2 bitcast_dynamic-update-slice_fusion
  578.3 5.4 copy.63
  583.8 4.1 copy.64
  587.9 2.5 copy.65
  (44 shorter events, 6.9 us)
Async XLA Ops:
  8.0 144.0 %reduce-scatter.3.cloned.1.call-start = ((), (), s32[]{:S(2)}) async-start(), calls=%async_computation.4 | async-start | bytes 4718592 | tf_op jit(solution)/shard_map/reduce_scatter | solution.py:63
  53.3 7.3 %copy-start.4 = (bf16[8,128,1024]{2,1,0:T(8,128)(2,1)}, bf16[8,128,1024]{2,1,0:T(8,128)(2,1)S(1)}, u32[]{:S(2)}) copy-start(bf16[8,128,1024]{2,1,0:T(8,128)(2,1)S(1)} %copy.53) | copy-start | bytes 6291460
  60.6 91.4 %copy-start.6 = (bf16[1,2,128,1024]{3,2,1,0:T(8,128)(2,1)S(1)}, bf16[1,2,128,1024]{3,2,1,0:T(8,128)(2,1)}, u32[]{:S(2)}) copy-start(bf16[1,2,128,1024]{3,2,1,0:T(8,128)(2,1)} %param.10) | copy-start | bytes 1572868
  60.6 93.2 %copy-start = (bf16[1,1,128,8192]{3,2,1,0:T(8,128)(2,1)S(1)}, bf16[1,1,128,8192]{3,2,1,0:T(8,128)(2,1)}, u32[]{:S(2)}) copy-start(bf16[1,1,128,8192]{3,2,1,0:T(8,128)(2,1)} %get-tuple-element.33) | copy-start | bytes 6291460
  60.7 165.8 %all-gather.7.cloned.1.call-start = ((), (), s32[]{:S(2)}) async-start(), calls=%async_computation.5 | async-start | bytes 2359296 | tf_op jit(solution)/shard_map/all_gather | solution.py:80
  156.3 52.7 %all-to-all-start.1 = ((bf16[128,8,1024]{0,2,1:T(8,128)(2,1)}), bf16[128,8,1024]{0,2,1:T(8,128)(2,1)S(1)}, u32[]{:S(2)}, u32[]{:S(2)}) async-start(bf16[128,8,1024]{0,2,1:T(8,128)(2,1)} %bitcast.96), calls=%async_computation.2 | async-start | bytes 4194304 | tf_op jit(solution)/shard_map/all_to_all | solution.py:56
  160.2 180.1 %reduce-scatter.5.cloned.1.call-start = ((), (), s32[]{:S(2)}) async-start(), calls=%async_computation.6 | async-start | bytes 4718592 | tf_op jit(solution)/shard_map/reduce_scatter | solution.py:63
  211.6 29.0 %copy-start.3 = (bf16[8,128,1024]{2,1,0:T(8,128)(2,1)S(1)}, bf16[8,128,1024]{2,1,0:T(8,128)(2,1)}, u32[]{:S(2)}) copy-start(bf16[8,128,1024]{2,1,0:T(8,128)(2,1)} %copy.56) | copy-start | bytes 6291460
  238.6 2.0 copy-start.9
  244.9 2.3 copy-start.2
  245.0 97.2 %all-gather.13.cloned.1.call-start = ((), (), s32[]{:S(2)}) async-start(), calls=%async_computation.10 | async-start | bytes 1114112 | tf_op jit(solution)/shard_map/all_gather | solution.py:45
  246.5 117.4 %all-gather.11.cloned.1.call-start = ((), (), s32[]{:S(2)}) async-start(), calls=%async_computation.9 | async-start | bytes 1114112 | tf_op jit(solution)/shard_map/all_gather | solution.py:42
  247.2 258.0 %all-reduce.2.cloned.1.call-start = ((), (), s32[]{:S(2)}) async-start(), calls=%async_computation.8 | async-start | bytes 2097152 | tf_op jit(solution)/shard_map/psum | solution.py:40
  248.7 311.9 %all-gather.9.cloned.1.call-start = ((), (), s32[]{:S(2)}) async-start(), calls=%async_computation.7 | async-start | bytes 2359296 | tf_op jit(solution)/shard_map/all_gather | solution.py:80
  572.7 2.0 copy-start.1
  578.2 5.6 copy-start.8
  578.3 5.5 copy-start.7
  583.8 4.1 copy-start.5
Sparse Core Ops, SparseCore 0:
  60.8 91.1 reduce-scatter.2
  154.2 72.1 all-gather.6
  245.1 95.1 reduce-scatter.4
Sparse Core Ops, SparseCore 1:
  248.5 60.0 all-gather.12
  310.8 53.0 all-gather.10
  366.2 138.9 all-reduce.1
  507.5 53.0 all-gather.8
where the time goes:
time: 599 us; the launch traced here: 598 us
  waiting for transfers between devices  445 us (74%)
  local copies, waits for them, and re-layouts  54.1 us (9%)
  matrix products  35.9 us (6%)
  blocking collectives  32.6 us (5%)
  between operations  16.4 us (3%)
  other arithmetic  8.85 us (1%)
    reduce_scatter x2, waiting for transfers between devices, on_device(): lax.psum_scatter(partial_keys(jnp.int32(0), lax.axis_size('fsdp') * tok_r...  183 us
    psum x1, waiting for transfers between devices, on_device(): total = lax.psum(delta.astype(jnp.bfloat16), 'rep').astype(jnp.float32)  140 us
    all_gather x2, waiting for transfers between devices, on_device(): lax.all_gather(resid, 'fsdp', axis=0, tiled=True)  67.3 us
    unnamed x32, local copies, waits for them, and re-layouts  38.3 us
    all_to_all x1, waiting for transfers between devices, on_device(): lax.all_to_all(tokens[0, step], 'fsdp', split_axis=1, concat_axis=0, tile...  35.3 us
    all_to_all x1, blocking collectives, on_device(): lax.all_to_all(tokens[0, step], 'fsdp', split_axis=1, concat_axis=0, tile...  32.6 us
    dot_general x2, matrix products, add_grad(): lax.dot_general(sliced, piece, (((0,), (0,)), ((), ())), preferred_elemen...  24.2 us
    all_gather x1, waiting for transfers between devices, on_device(): lax.all_gather(anchor_rows.astype(jnp.bfloat16), 'rep', axis=0, tiled=True)  20.2 us
  transfers between devices with their start and end apart: 8, of which 7 were waited for; matrix products, arithmetic and copies ran while one was open for 5% of the time, Pallas kernels for 0%

commit v1 on v0

v1 whole, which is shorter than its diff:
```python
import math

import jax
import jax.numpy as jnp
from jax import lax
from jax.experimental import pallas as pl
from jax.experimental.pallas import tpu as pltpu
from jax.sharding import PartitionSpec as P

beta_one = 0.9
beta_two = 0.95
inner_rate = 0.02
decay_rate = 0.1
adam_eps = 1e-08
outer_rate = 0.7
outer_mu = 0.9
mix_weight = 0.5

f32 = jnp.float32
bf16 = jnp.bfloat16
VMEM_LIMIT = 48 * 1024 * 1024

N_Y = 4
N_X = 2


def swap_x(value):
    return lax.ppermute(value, "fsdp", [(i, i ^ 1) for i in range(N_Y * N_X)])


def shift_y(value, hops):
    size = N_Y * N_X
    return lax.ppermute(value, "fsdp", [(i, (i + N_X * hops) % size) for i in range(size)])


def regroup_tokens(tokens, step):
    _, _, rows, width = tokens.shape
    parts = N_Y * N_X
    cols = width // parts

    def body(src, dst, sems):
        copies = [
            pltpu.make_async_copy(
                src.at[0, step, :, pl.ds(part * cols, cols)], dst.at[part], sems.at[part]
            )
            for part in range(parts)
        ]
        for copy in copies:
            copy.start()
        for copy in copies:
            copy.wait()

    return pl.pallas_call(
        body,
        out_shape=jax.ShapeDtypeStruct((parts, rows, cols), tokens.dtype),
        in_specs=[pl.BlockSpec(memory_space=pl.ANY)],
        out_specs=pl.BlockSpec(memory_space=pl.ANY),
        scratch_shapes=[pltpu.SemaphoreType.DMA((parts,))],
        cost_estimate=pl.CostEstimate(flops=0, bytes_accessed=4 * rows * width, transcendentals=0),
        name="regroup_tokens",
    )(tokens)


def pair_rows(y_pos, hops, pair):
    return pl.multiple_of(lax.rem(y_pos + hops, N_Y) * pair, pair)


def first_keys(y_pos, toks, weights, chain, cols):
    rows, width = toks.shape
    pair = rows // N_Y

    def body(y_ref, tok_ref, w_ref, own_ref, *out_refs):
        narrow = w_ref[0].astype(bf16)
        for hops in (1, 2, 3, 0):
            at = pair_rows(y_ref[0], hops, pair)
            part = jnp.dot(tok_ref[pl.ds(at, pair), :], narrow, preferred_element_type=f32)
            if hops:
                out_refs[hops - 1][...] = part.astype(bf16)
            else:
                own_ref[...] = part

    whole = lambda i, y: (0, 0)
    return pl.pallas_call(
        body,
        grid_spec=pltpu.PrefetchScalarGridSpec(
            num_scalar_prefetch=1,
            grid=(1,),
            in_specs=[
                pl.BlockSpec((rows, width), whole),
                pl.BlockSpec((1, width, cols), lambda i, y: (0, 0, chain)),
            ],
            out_specs=[pl.BlockSpec((pair, cols), whole)] * N_Y,
        ),
        out_shape=[jax.ShapeDtypeStruct((pair, cols), f32)]
        + [jax.ShapeDtypeStruct((pair, cols), bf16)] * (N_Y - 1),
        compiler_params=pltpu.CompilerParams(vmem_limit_bytes=VMEM_LIMIT),
        cost_estimate=pl.CostEstimate(
            flops=2 * rows * width * cols,
            bytes_accessed=2 * rows * width + 4 * width * cols + 2 * rows * cols,
            transcendentals=0,
        ),
        name="first_keys",
    )(y_pos, toks, weights)


def adam(grad, first, second, weights):
    first = beta_one * first.astype(f32) + (1.0 - beta_one) * grad
    second = beta_two * second.astype(f32) + (1.0 - beta_two) * grad * grad
    weights = weights - inner_rate * (
        first / (jnp.sqrt(second) + adam_eps) + decay_rate * weights
    )
    return first, second, weights


def gather_resid(y_ref, resid_refs, full, pair):
    for hops in range(N_Y):
        at = pair_rows(y_ref[0], (N_Y - hops) % N_Y, pair)
        full[pl.ds(at, pair), :] = resid_refs[hops][...]


def grad_block(tok, resid, inv_root):
    return (
        lax.dot_general(tok, resid, (((0,), (0,)), ((), ())), preferred_element_type=f32)
        * inv_root
    )


def middle_step(y_pos, toks, next_toks, resids, weights, first, second, chain, cols, inv_root):
    rows, width = toks.shape
    pair = rows // N_Y
    tile = 256
    tiles = width // tile

    def body(y_ref, tok_ref, next_ref, r0, r1, r2, r3, w_ref, m_ref, v_ref,
             w_out, m_out, v_out, own_ref, k1, k2, k3, full, narrow):
        step = pl.program_id(0)

        @pl.when(step == 0)
        def _():
            gather_resid(y_ref, (r0, r1, r2, r3), full, pair)

        grad = grad_block(tok_ref[...], full[...], inv_root)
        m_new, v_new, w_new = adam(grad, m_ref[0], v_ref[0], w_ref[0])
        w_out[...] = w_new
        m_out[...] = m_new.astype(bf16)
        v_out[...] = v_new.astype(bf16)
        narrow[pl.ds(pl.multiple_of(step * tile, tile), tile), :] = w_new.astype(bf16)

        @pl.when(step == tiles - 1)
        def _():
            for hops in (1, 2, 3, 0):
                at = pair_rows(y_ref[0], hops, pair)
                part = jnp.dot(
                    next_ref[pl.ds(at, pair), :], narrow[...], preferred_element_type=f32
                )
                if hops:
                    (k1, k2, k3)[hops - 1][...] = part.astype(bf16)
                else:
                    own_ref[...] = part

    whole = lambda i, y: (0, 0)
    state = lambda i, y: (0, i, chain)
    return pl.pallas_call(
        body,
        grid_spec=pltpu.PrefetchScalarGridSpec(
            num_scalar_prefetch=1,
            grid=(tiles,),
            in_specs=[
                pl.BlockSpec((rows, tile), lambda i, y: (0, i)),
                pl.BlockSpec((rows, width), whole),
            ]
            + [pl.BlockSpec((pair, cols), whole)] * N_Y
            + [pl.BlockSpec((1, tile, cols), state)] * 3,
            out_specs=[pl.BlockSpec((tile, cols), lambda i, y: (i, 0))] * 3
            + [pl.BlockSpec((pair, cols), whole)] * N_Y,
            scratch_shapes=[pltpu.VMEM((rows, cols), bf16), pltpu.VMEM((width, cols), bf16)],
        ),
        out_shape=[
            jax.ShapeDtypeStruct((width, cols), f32),
            jax.ShapeDtypeStruct((width, cols), bf16),
            jax.ShapeDtypeStruct((width, cols), bf16),
            jax.ShapeDtypeStruct((pair, cols), f32),
        ]
        + [jax.ShapeDtypeStruct((pair, cols), bf16)] * (N_Y - 1),
        compiler_params=pltpu.CompilerParams(vmem_limit_bytes=VMEM_LIMIT),
        cost_estimate=pl.CostEstimate(
            flops=4 * rows * width * cols,
            bytes_accessed=4 * rows * width + 18 * width * cols + 4 * rows * cols,
            transcendentals=width * cols,
        ),
        name="middle_step",
    )(y_pos, toks, next_toks, *resids, weights, first, second)


def last_step(y_pos, fragment, toks, resids, weights, first, second, anchor_new, chain, cols,
              inv_root, outs):
    rows, width = toks.shape
    pair = rows // N_Y
    tile = 256
    tiles = width // tile
    total = outs[0].shape[2] if outs is not None else 2 * cols

    def body(y_ref, f_ref, tok_ref, r0, r1, r2, r3, w_ref, m_ref, v_ref, a_ref, *rest):
        w_out, m_out, v_out, full = rest[-4:]

        @pl.when(pl.program_id(0) == 0)
        def _():
            gather_resid(y_ref, (r0, r1, r2, r3), full, pair)

        grad = grad_block(tok_ref[...], full[...], inv_root)
        m_new, v_new, w_new = adam(grad, m_ref[...], v_ref[...], w_ref[...])
        m_out[0] = m_new.astype(bf16)
        v_out[0] = v_new.astype(bf16)
        mixed = mix_weight * w_new + (1.0 - mix_weight) * a_ref[...].astype(f32)
        w_out[0] = jnp.where(f_ref[0] == chain, mixed, w_new)

    whole = lambda i, y, f: (0, 0)
    by_tile = lambda i, y, f: (i, 0)
    place = lambda i, y, f: (0, i, chain)
    in_specs = (
        [pl.BlockSpec((rows, tile), lambda i, y, f: (0, i))]
        + [pl.BlockSpec((pair, cols), whole)] * N_Y
        + [pl.BlockSpec((tile, cols), by_tile)] * 4
    )
    args = [y_pos, fragment, toks, *resids, weights, first, second, anchor_new]
    aliases = {}
    if outs is not None:
        in_specs = in_specs + [pl.BlockSpec(memory_space=pl.ANY)] * 3
        aliases = {len(args) + i: i for i in range(3)}
        args = args + list(outs)
    return pl.pallas_call(
        body,
        grid_spec=pltpu.PrefetchScalarGridSpec(
            num_scalar_prefetch=2,
            grid=(tiles,),
            in_specs=in_specs,
            out_specs=[pl.BlockSpec((1, tile, cols), place)] * 3,
            scratch_shapes=[pltpu.VMEM((rows, cols), bf16)],
        ),
        out_shape=[
            jax.ShapeDtypeStruct((1, width, total), f32),
            jax.ShapeDtypeStruct((1, width, total), bf16),
            jax.ShapeDtypeStruct((1, width, total), bf16),
        ],
        input_output_aliases=aliases,
        compiler_params=pltpu.CompilerParams(vmem_limit_bytes=VMEM_LIMIT),
        cost_estimate=pl.CostEstimate(
            flops=2 * rows * width * cols,
            bytes_accessed=2 * rows * width + 18 * width * cols + 2 * rows * cols,
            transcendentals=width * cols,
        ),
        name="last_step",
    )(*args)


def outer_step(shares, anchor, momentum, fragment, replicas):
    mean = jnp.sum(shares.astype(f32), axis=0) / replicas
    anchor_old = lax.dynamic_index_in_dim(anchor, fragment, 0, keepdims=False)[0]
    moment_old = lax.dynamic_index_in_dim(momentum, fragment, 0, keepdims=False)[0]
    moment_new = outer_mu * moment_old + mean
    anchor_new = anchor_old - outer_rate * (mean + outer_mu * moment_new)
    anchor_out = lax.dynamic_update_index_in_dim(anchor, anchor_new[None], fragment, 0)
    momentum_out = lax.dynamic_update_index_in_dim(momentum, moment_new[None], fragment, 0)
    return anchor_new, anchor_out, momentum_out


def on_device(tokens, targets, params, moment1, moment2, stale_delta, anchor, momentum, plan):
    inv_root = 1.0 / math.sqrt(tokens.shape[3])
    replicas = lax.axis_size("rep")
    place = lax.axis_index("fsdp")
    y_pos = jnp.full((1,), place // N_X, jnp.int32)
    x_pos = place % N_X
    cols = stale_delta.shape[2]
    chains = params.shape[2] // cols
    slice_rows = anchor.shape[2]

    def exchange(blocks, axis):
        return lax.all_to_all(blocks, axis, split_axis=0, concat_axis=0, tiled=True)

    flat = lambda blocks: blocks.reshape(-1, blocks.shape[-1])
    toks = [flat(exchange(regroup_tokens(tokens, step), "fsdp")) for step in range(2)]

    other = swap_x(targets[0])
    pair_targets = jnp.where(
        x_pos == 0,
        jnp.concatenate([targets[0], other], axis=1),
        jnp.concatenate([other, targets[0]], axis=1),
    )

    shares = exchange(
        stale_delta[0].astype(bf16).reshape(replicas, slice_rows, cols), "rep"
    )
    anchor_new, anchor_out, momentum_out = outer_step(shares, anchor, momentum, plan[0], replicas)
    spread = jnp.broadcast_to(anchor_new.astype(bf16)[None], (replicas, slice_rows, cols))
    anchor_full = flat(exchange(spread, "rep"))

    def resid_of(parts, step, chain):
        own, *sent = parts
        got = [shift_y(sent[hops - 1], hops) for hops in (1, 2, 3)]
        half = (own + got[0].astype(f32) + got[1].astype(f32) + got[2].astype(f32)).astype(bf16)
        keys = (half.astype(f32) + swap_x(half).astype(f32)) * inv_root
        goal = pair_targets[step, :, chain * cols : (chain + 1) * cols].astype(f32)
        resid = (keys - goal).astype(bf16)
        return [resid] + [shift_y(resid, hops) for hops in (1, 2, 3)]

    parts = [first_keys(y_pos, toks[0], params, chain, cols) for chain in range(chains)]
    state = []
    for chain in range(chains):
        resids = resid_of(parts[chain], 0, chain)
        w, m, v, *parts[chain] = middle_step(
            y_pos, toks[0], toks[1], resids, params, moment1, moment2, chain, cols, inv_root
        )
        state.append((w, m, v))
    outs = None
    for chain in range(chains):
        resids = resid_of(parts[chain], 1, chain)
        outs = last_step(
            y_pos, plan, toks[1], resids, *state[chain], anchor_full, chain, cols, inv_root, outs
        )
    return (*outs, anchor_out, momentum_out)


def solution(mesh):
    return jax.shard_map(
        on_device,
        mesh=mesh,
        in_specs=(
            P("rep", None, "fsdp", None),
            P("rep", None, "fsdp", None),
            P("rep", "fsdp", None),
            P("rep", "fsdp", None),
            P("rep", "fsdp", None),
            P("rep", "fsdp", None),
            P(None, "fsdp", "rep", None),
            P(None, "fsdp", "rep", None),
            P(),
        ),
        out_specs=(
            P("rep", "fsdp", None),
            P("rep", "fsdp", None),
            P("rep", "fsdp", None),
            P(None, "fsdp", "rep", None),
            P(None, "fsdp", "rep", None),
        ),
        check_vma=False,
    )
```

time: 599 us -> 317 us (0.53)
  waiting for transfers between devices: 445 us -> 57.8 us
  Pallas kernels: 0 us -> 167 us
  starting transfers between devices: 4.62 us -> 64.4 us
  local copies, waits for them, and re-layouts: 54.1 us -> 13.1 us
  matrix products: 35.9 us -> 0 us
  blocking collectives: 32.6 us -> 0 us
  between operations: 16.4 us -> 1.56 us
    reduce_scatter x2 -> x0, waiting for transfers between devices: 183 us -> none  [on_device(): lax.psum_scatter(partial_keys(jnp.int32(0), lax.axis_size('fsdp') * tok_r...]
    pallas_call x0 -> x8, Pallas kernels: none -> 167 us  [the longest x2 129 us: regroup_tokens(): pl.pallas_call(body, out_shape=jax.ShapeDtypeStruct((parts, rows, cols),...]
    psum x1 -> x0, waiting for transfers between devices: 140 us -> none  [on_device(): total = lax.psum(delta.astype(jnp.bfloat16), 'rep').astype(jnp.float32)]
    all_gather x4 -> x0, waiting for transfers between devices: 87.5 us -> none  [the longest x2 67.3 us: on_device(): lax.all_gather(resid, 'fsdp', axis=0, tiled=True)]
    ppermute x0 -> x29, waiting for transfers between devices: none -> 57.8 us  [the longest x24 57.8 us: shift_y(): lax.ppermute(value, 'fsdp', [(i, (i + N_X * hops) % size) for i in range(...]
    ppermute x0 -> x29, starting transfers between devices: none -> 37.8 us  [the longest x24 33.4 us: shift_y(): lax.ppermute(value, 'fsdp', [(i, (i + N_X * hops) % size) for i in range(...]
    dot_general x4 -> x0, matrix products: 35.9 us -> none  [the longest x2 24.2 us: add_grad(): lax.dot_general(sliced, piece, (((0,), (0,)), ((), ())), preferred_elemen...]
    all_to_all x1 -> x4, waiting for transfers between devices: 35.3 us -> 0.01 us  [exchange(): return lax.all_to_all(blocks, axis, split_axis=0, concat_axis=0, tiled=True)]
  transfers between devices with their start and end apart: 8 -> 33, of which waited for: 7 -> 11; matrix products, arithmetic and copies ran while one was open for 5% -> 4% of each run, Pallas kernels for 0% -> 30%
where the time goes in v1:
time: 317 us; the launch traced here: 315 us
  Pallas kernels  167 us (53%)
  starting transfers between devices  64.4 us (20%)
  waiting for transfers between devices  57.8 us (18%)
  local copies, waits for them, and re-layouts  13.1 us (4%)
  other arithmetic  11.7 us (4%)
    pallas_call x2, Pallas kernels, regroup_tokens(): pl.pallas_call(body, out_shape=jax.ShapeDtypeStruct((parts, rows, cols),...  129 us
    ppermute x24, waiting for transfers between devices, shift_y(): lax.ppermute(value, 'fsdp', [(i, (i + N_X * hops) % size) for i in range(...  57.8 us
    ppermute x24, starting transfers between devices, shift_y(): lax.ppermute(value, 'fsdp', [(i, (i + N_X * hops) % size) for i in range(...  33.4 us
    all_to_all x4, starting transfers between devices, exchange(): return lax.all_to_all(blocks, axis, split_axis=0, concat_axis=0, tiled=True)  26.6 us
    pallas_call x2, Pallas kernels, middle_step(): pl.pallas_call(body, grid_spec=pltpu.PrefetchScalarGridSpec(num_scalar_pr...  17.6 us
    pallas_call x2, Pallas kernels, last_step(): pl.pallas_call(body, grid_spec=pltpu.PrefetchScalarGridSpec(num_scalar_pr...  13.9 us
    unnamed x38, local copies, waits for them, and re-layouts  12 us
  transfers between devices with their start and end apart: 33, of which 11 were waited for; matrix products, arithmetic and copies ran while one was open for 4% of the time, Pallas kernels for 30%

profile of v1, /device:TPU:0, one launch (start us, length us, event | category | flops | bytes accessed | tf_op | source)
XLA Modules:
  0.0 315.3 jit_solution(14296039198627189942)
XLA Ops:
  0.6 1.7 copy.25
  2.3 1.7 copy.26
  4.0 64.7 %regroup_tokens.3 = bf16[8,128,1024]{2,1,0:T(8,128)(2,1)} custom-call(bf16[1,2,128,8192]{3,2,1,0:T(8,128)(2,1)} %src.3), custom_call_target="tpu_custom_call" | custom-call | bytes 4194304 | tf_op jit(solution)/shard_map/regroup_tokens/pallas_call | solution.py:53
  68.7 5.5 %all-to-all-start.1 = ((bf16[8,128,1024]{2,1,0:T(8,128)(2,1)}), bf16[8,128,1024]{2,1,0:T(8,128)(2,1)S(1)}, u32[]{:S(2)}, u32[]{:S(2)}) async-start(bf16[8,128,1024]{2,1,0:T(8,128)(2,1)} %regroup_tokens.3), calls=%async_computation.1 | async-start | bytes 4194304 | tf_op jit(solution)/shard_map/all_to_all | solution.py:278
  74.2 64.7 %regroup_tokens.2 = bf16[8,128,1024]{2,1,0:T(8,128)(2,1)} custom-call(bf16[1,2,128,8192]{3,2,1,0:T(8,128)(2,1)} %src.3), custom_call_target="tpu_custom_call" | custom-call | bytes 4194304 | tf_op jit(solution)/shard_map/regroup_tokens/pallas_call | solution.py:53
  138.9 5.7 %all-to-all-start = ((bf16[8,128,1024]{2,1,0:T(8,128)(2,1)}), bf16[8,128,1024]{2,1,0:T(8,128)(2,1)}, u32[]{:S(2)}, u32[]{:S(2)}) async-start(bf16[8,128,1024]{2,1,0:T(8,128)(2,1)} %regroup_tokens.2), calls=%async_computation | async-start | bytes 4194304 | tf_op jit(solution)/shard_map/all_to_all | solution.py:278
  144.6 2.9 first_keys.3
  147.5 2.1 collective-permute-start.15
  149.6 2.7 collective-permute-start.16
  155.2 2.8 first_keys.2
  158.7 24.4 %collective-permute-done.15 = bf16[256,512]{1,0:T(8,128)(2,1)S(1)} collective-permute-done((bf16[256,512]{1,0:T(8,128)(2,1)S(1)}, bf16[256,512]{1,0:T(8,128)(2,1)S(1)}, u32[]{:S(2)}, u32[]{:S(2)}) %collective-permute-start.15) | collective-permute-done | bytes 262176 | tf_op jit(solution)/shard_map/ppermute | solution.py:33
  185.4 3.3 %collective-permute-done = bf16[256,512]{1,0:T(8,128)(2,1)S(1)} collective-permute-done((bf16[256,512]{1,0:T(8,128)(2,1)S(1)}, bf16[256,512]{1,0:T(8,128)(2,1)S(1)}, u32[]{:S(2)}, u32[]{:S(2)}) %collective-permute-start) | collective-permute-done | bytes 262176 | tf_op jit(solution)/shard_map/ppermute | solution.py:33
  188.7 4.2 %collective-permute-done.1 = bf16[256,512]{1,0:T(8,128)(2,1)S(1)} collective-permute-done((bf16[256,512]{1,0:T(8,128)(2,1)S(1)}, bf16[256,512]{1,0:T(8,128)(2,1)S(1)}, u32[]{:S(2)}, u32[]{:S(2)}) %collective-permute-start.1) | collective-permute-done | bytes 262176 | tf_op jit(solution)/shard_map/ppermute | solution.py:33
  195.7 7.6 %all-to-all-start.2 = ((bf16[16,64,512]{2,1,0:T(8,128)(2,1)}), bf16[16,64,512]{2,1,0:T(8,128)(2,1)}, u32[]{:S(2)}, u32[]{:S(2)}) async-start(bf16[16,64,512]{2,1,0:T(8,128)(2,1)} %bitcast.8), calls=%async_computation.2 | async-start | bytes 2097152 | tf_op jit(solution)/shard_map/all_to_all | solution.py:278
  207.9 2.6 collective-permute-start.7
  212.8 1.7 collective-permute-done.21.r3
  217.9 5.0 %collective-permute-done.19.r1 = bf16[256,512]{1,0:T(8,128)(2,1)S(1)} collective-permute-done((bf16[256,512]{1,0:T(8,128)(2,1)S(1)}, bf16[256,512]{1,0:T(8,128)(2,1)S(1)}, u32[]{:S(2)}, u32[]{:S(2)}) %collective-permute-start.19) | collective-permute-done | bytes 262176 | tf_op jit(solution)/shard_map/ppermute | solution.py:33
  226.4 8.9 %middle_step.3 = (f32[1024,512]{1,0:T(8,128)}, bf16[1024,512]{1,0:T(8,128)(2,1)S(1)}, bf16[1024,512]{1,0:T(8,128)(2,1)S(1)}, f32[256,512]{1,0:T(8,128)S(1)}, bf1...) custom-call(s32[1]{0:T(128)} %bitcast.y_ref, bf16[1024,1024]{1,0:T(8,128)(2,1)} %bitcast.59, ...), custom_call_target="tpu_custom_call" | custom-call | flops 2147483648 | bytes 15728640 | tf_op jit(solution)/shard_map/middle_step/pallas_call | solution.py:163
  235.3 2.1 collective-permute-start.23
  237.5 2.5 collective-permute-start.24
  241.4 8.7 %middle_step.2 = (f32[1024,512]{1,0:T(8,128)}, bf16[1024,512]{1,0:T(8,128)(2,1)S(1)}, bf16[1024,512]{1,0:T(8,128)(2,1)S(1)}, f32[256,512]{1,0:T(8,128)S(1)}, bf1...) custom-call(s32[1]{0:T(128)} %bitcast.y_ref, bf16[1024,1024]{1,0:T(8,128)(2,1)} %bitcast.60, ...), custom_call_target="tpu_custom_call" | custom-call | flops 2147483648 | bytes 15728640 | tf_op jit(solution)/shard_map/middle_step/pallas_call | solution.py:163
  253.7 2.6 collective-permute-start.10
  257.7 7.7 %collective-permute-done.8 = bf16[256,512]{1,0:T(8,128)(2,1)S(1)} collective-permute-done((bf16[256,512]{1,0:T(8,128)(2,1)S(1)}, bf16[256,512]{1,0:T(8,128)(2,1)S(1)}, u32[]{:S(2)}, u32[]{:S(2)}) %collective-permute-start.8) | collective-permute-done | bytes 262176 | tf_op jit(solution)/shard_map/ppermute | solution.py:33
  268.6 7.8 %all-to-all-start.3 = ((bf16[16,64,512]{2,1,0:T(8,128)(2,1)}), bf16[16,64,512]{2,1,0:T(8,128)(2,1)S(1)}, u32[]{:S(2)}, u32[]{:S(2)}) async-start(bf16[16,64,512]{2,1,0:T(8,128)(2,1)} %broadcast_in_dim.8), calls=%async_computation.3 | async-start | bytes 2097152 | tf_op jit(solution)/shard_map/all_to_all | solution.py:278
  276.4 2.3 fusion
  278.6 2.6 collective-permute-start.28
  282.3 3.2 %collective-permute-start.14 = (bf16[256,512]{1,0:T(8,128)(2,1)S(1)}, bf16[256,512]{1,0:T(8,128)(2,1)}, u32[]{:S(2)}, u32[]{:S(2)}) collective-permute-start(bf16[256,512]{1,0:T(8,128)(2,1)S(1)} %get-tuple-element.62.r0), channel_id=1, source_target_pairs={{0,6},{1,7},{2,0},{3,1},{4,2},{5,3},{6,4},{7,5},{8,14},{9,15},{10,... | collective-permute-start | bytes 786440 | tf_op jit(solution)/shard_map/ppermute | solution.py:33
  286.8 6.9 %collective-permute-done.28.r3 = bf16[256,512]{1,0:T(8,128)(2,1)S(1)} collective-permute-done((bf16[256,512]{1,0:T(8,128)(2,1)}, bf16[256,512]{1,0:T(8,128)(2,1)S(1)}, u32[]{:S(2)}, u32[]{:S(2)}) %collective-permute-start.28) | collective-permute-done | bytes 262176 | tf_op jit(solution)/shard_map/ppermute | solution.py:33
  295.8 1.7 fusion.12
  298.8 7.0 %last_step.2 = (f32[1,1024,1024]{2,1,0:T(8,128)}, bf16[1,1024,1024]{2,1,0:T(8,128)(2,1)}, bf16[1,1024,1024]{2,1,0:T(8,128)(2,1)}) custom-call(s32[1]{0:T(128)} %bitcast.y_ref, s32[1]{0:T(128)} %copy.24.f_ref, bf16[1024,1024]{1,0:T(8,128)(2,1)} %bitcast.1.next_ref.tok_ref, bf16[256,512]{1,0:T(8,128)(2,1)} %get-tuple-element.61.r0, ...), custom_call_target="tpu_custom_call" | custom-call | flops 1073741824 | bytes 12582912 | tf_op jit(solution)/shard_map/last_step/pallas_call | solution.py:231
  305.8 2.5 collective-permute-done.12.r1
  308.4 6.9 %last_step.3 = (f32[1,1024,1024]{2,1,0:T(8,128)}, bf16[1,1024,1024]{2,1,0:T(8,128)(2,1)}, bf16[1,1024,1024]{2,1,0:T(8,128)(2,1)}) custom-call(s32[1]{0:T(128)} %bitcast.y_ref, s32[1]{0:T(128)} %copy.24.f_ref, bf16[1024,1024]{1,0:T(8,128)(2,1)} %bitcast.1.next_ref.tok_ref, ...), custom_call_target="tpu_custom_call", output_to_operand_aliasing={{0}: (11, {}), {1}: (12, {}), {2}: (13, {})} | custom-call | flops 1073741824 | bytes 12582912 | tf_op jit(solution)/shard_map/last_step/pallas_call | solution.py:231
  (92 shorter events, 37.0 us)
Async XLA Ops:
  68.7 70.2 %all-to-all-start.1 = ((bf16[8,128,1024]{2,1,0:T(8,128)(2,1)}), bf16[8,128,1024]{2,1,0:T(8,128)(2,1)S(1)}, u32[]{:S(2)}, u32[]{:S(2)}) async-start(bf16[8,128,1024]{2,1,0:T(8,128)(2,1)} %regroup_tokens.3), calls=%async_computation.1 | async-start | bytes 4194304 | tf_op jit(solution)/shard_map/all_to_all | solution.py:278
  138.9 56.8 %all-to-all-start = ((bf16[8,128,1024]{2,1,0:T(8,128)(2,1)}), bf16[8,128,1024]{2,1,0:T(8,128)(2,1)}, u32[]{:S(2)}, u32[]{:S(2)}) async-start(bf16[8,128,1024]{2,1,0:T(8,128)(2,1)} %regroup_tokens.2), calls=%async_computation | async-start | bytes 4194304 | tf_op jit(solution)/shard_map/all_to_all | solution.py:278
  147.5 35.5 %collective-permute-start.15 = (bf16[256,512]{1,0:T(8,128)(2,1)S(1)}, bf16[256,512]{1,0:T(8,128)(2,1)S(1)}, u32[]{:S(2)}, u32[]{:S(2)}) collective-permute-start(bf16[256,512]{1,0:T(8,128)(2,1)S(1)} %get-tuple-element.45), channel_id=1, source_target_pairs={{0,2},{1,3},{2,4},{3,5},{4,6},{5,7},{6,0},{7,1},{8,10},{9,11},{10,... | collective-permute-start | bytes 786440 | tf_op jit(solution)/shard_map/ppermute | solution.py:33
  149.6 34.4 %collective-permute-start.16 = (bf16[256,512]{1,0:T(8,128)(2,1)S(1)}, bf16[256,512]{1,0:T(8,128)(2,1)S(1)}, u32[]{:S(2)}, u32[]{:S(2)}) collective-permute-start(bf16[256,512]{1,0:T(8,128)(2,1)S(1)} %get-tuple-element.46), channel_id=1, source_target_pairs={{0,4},{1,5},{2,6},{3,7},{4,0},{5,1},{6,2},{7,3},{8,12},{9,13},{10,... | collective-permute-start | bytes 786440 | tf_op jit(solution)/shard_map/ppermute | solution.py:33
  152.3 31.7 %collective-permute-start.17 = (bf16[256,512]{1,0:T(8,128)(2,1)S(1)}, bf16[256,512]{1,0:T(8,128)(2,1)S(1)}, u32[]{:S(2)}, u32[]{:S(2)}) collective-permute-start(bf16[256,512]{1,0:T(8,128)(2,1)S(1)} %get-tuple-element.47), channel_id=1, source_target_pairs={{0,6},{1,7},{2,0},{3,1},{4,2},{5,3},{6,4},{7,5},{8,14},{9,15},{10,... | collective-permute-start | bytes 786440 | tf_op jit(solution)/shard_map/ppermute | solution.py:33
  153.8 49.6 %collective-permute-start.4 = (bf16[2,128,1024]{2,1,0:T(8,128)(2,1)S(1)}, bf16[2,128,1024]{2,1,0:T(8,128)(2,1)}, u32[]{:S(2)}, u32[]{:S(2)}) collective-permute-start(bf16[2,128,1024]{2,1,0:T(8,128)(2,1)S(1)} %bitcast.63), channel_id=1, source_target_pairs={{0,1},{1,0},{2,3},{3,2},{4,5},{5,4},{6,7},{7,6},{8,9},{9,8},{10,11... | collective-permute-start | bytes 1572872 | tf_op jit(solution)/shard_map/ppermute | solution.py:28
  158.1 30.6 %collective-permute-start = (bf16[256,512]{1,0:T(8,128)(2,1)S(1)}, bf16[256,512]{1,0:T(8,128)(2,1)S(1)}, u32[]{:S(2)}, u32[]{:S(2)}) collective-permute-start(bf16[256,512]{1,0:T(8,128)(2,1)S(1)} %get-tuple-element.34), channel_id=1, source_target_pairs={{0,2},{1,3},{2,4},{3,5},{4,6},{5,7},{6,0},{7,1},{8,10},{9,11},{10,... | collective-permute-start | bytes 786440 | tf_op jit(solution)/shard_map/ppermute | solution.py:33
  183.1 9.8 %collective-permute-start.1 = (bf16[256,512]{1,0:T(8,128)(2,1)S(1)}, bf16[256,512]{1,0:T(8,128)(2,1)S(1)}, u32[]{:S(2)}, u32[]{:S(2)}) collective-permute-start(bf16[256,512]{1,0:T(8,128)(2,1)S(1)} %get-tuple-element.35), channel_id=1, source_target_pairs={{0,4},{1,5},{2,6},{3,7},{4,0},{5,1},{6,2},{7,3},{8,12},{9,13},{10,... | collective-permute-start | bytes 786440 | tf_op jit(solution)/shard_map/ppermute | solution.py:33
  184.1 20.9 %collective-permute-start.18 = (bf16[256,512]{1,0:T(8,128)(2,1)S(1)}, bf16[256,512]{1,0:T(8,128)(2,1)S(1)}, u32[]{:S(2)}, u32[]{:S(2)}) collective-permute-start(bf16[256,512]{1,0:T(8,128)(2,1)S(1)} %add_convert_fusion.1), channel_id=1, source_target_pairs={{0,1},{1,0},{2,3},{3,2},{4,5},{5,4},{6,7},{7,6},{8,9},{9,8},{10,11... | collective-permute-start | bytes 786440 | tf_op jit(solution)/shard_map/ppermute | solution.py:28
  193.0 12.0 %collective-permute-start.3 = (bf16[256,512]{1,0:T(8,128)(2,1)S(1)}, bf16[256,512]{1,0:T(8,128)(2,1)S(1)}, u32[]{:S(2)}, u32[]{:S(2)}) collective-permute-start(bf16[256,512]{1,0:T(8,128)(2,1)S(1)} %add_convert_fusion.3), channel_id=1, source_target_pairs={{0,1},{1,0},{2,3},{3,2},{4,5},{5,4},{6,7},{7,6},{8,9},{9,8},{10,11... | collective-permute-start | bytes 786440 | tf_op jit(solution)/shard_map/ppermute | solution.py:28
  195.7 44.3 %all-to-all-start.2 = ((bf16[16,64,512]{2,1,0:T(8,128)(2,1)}), bf16[16,64,512]{2,1,0:T(8,128)(2,1)}, u32[]{:S(2)}, u32[]{:S(2)}) async-start(bf16[16,64,512]{2,1,0:T(8,128)(2,1)} %bitcast.8), calls=%async_computation.2 | async-start | bytes 2097152 | tf_op jit(solution)/shard_map/all_to_all | solution.py:278
  205.3 9.2 %collective-permute-start.21 = (bf16[256,512]{1,0:T(8,128)(2,1)S(1)}, bf16[256,512]{1,0:T(8,128)(2,1)S(1)}, u32[]{:S(2)}, u32[]{:S(2)}) collective-permute-start(bf16[256,512]{1,0:T(8,128)(2,1)S(1)} %get-tuple-element.63.r0), channel_id=1, source_target_pairs={{0,6},{1,7},{2,0},{3,1},{4,2},{5,3},{6,4},{7,5},{8,14},{9,15},{10,... | collective-permute-start | bytes 786440 | tf_op jit(solution)/shard_map/ppermute | solution.py:33
  206.5 10.7 %collective-permute-start.20 = (bf16[256,512]{1,0:T(8,128)(2,1)S(1)}, bf16[256,512]{1,0:T(8,128)(2,1)S(1)}, u32[]{:S(2)}, u32[]{:S(2)}) collective-permute-start(bf16[256,512]{1,0:T(8,128)(2,1)S(1)} %get-tuple-element.63.r0), channel_id=1, source_target_pairs={{0,4},{1,5},{2,6},{3,7},{4,0},{5,1},{6,2},{7,3},{8,12},{9,13},{10,... | collective-permute-start | bytes 786440 | tf_op jit(solution)/shard_map/ppermute | solution.py:33
  207.3 15.5 %collective-permute-start.19 = (bf16[256,512]{1,0:T(8,128)(2,1)S(1)}, bf16[256,512]{1,0:T(8,128)(2,1)S(1)}, u32[]{:S(2)}, u32[]{:S(2)}) collective-permute-start(bf16[256,512]{1,0:T(8,128)(2,1)S(1)} %get-tuple-element.63.r0), channel_id=1, source_target_pairs={{0,2},{1,3},{2,4},{3,5},{4,6},{5,7},{6,0},{7,1},{8,10},{9,11},{10,... | collective-permute-start | bytes 786440 | tf_op jit(solution)/shard_map/ppermute | solution.py:33
  207.9 29.5 %collective-permute-start.7 = (bf16[256,512]{1,0:T(8,128)(2,1)S(1)}, bf16[256,512]{1,0:T(8,128)(2,1)S(1)}, u32[]{:S(2)}, u32[]{:S(2)}) collective-permute-start(bf16[256,512]{1,0:T(8,128)(2,1)S(1)} %get-tuple-element.64.r0), channel_id=1, source_target_pairs={{0,6},{1,7},{2,0},{3,1},{4,2},{5,3},{6,4},{7,5},{8,14},{9,15},{10,... | collective-permute-start | bytes 786440 | tf_op jit(solution)/shard_map/ppermute | solution.py:33
  211.2 30.2 %collective-permute-start.6 = (bf16[256,512]{1,0:T(8,128)(2,1)S(1)}, bf16[256,512]{1,0:T(8,128)(2,1)}, u32[]{:S(2)}, u32[]{:S(2)}) collective-permute-start(bf16[256,512]{1,0:T(8,128)(2,1)S(1)} %get-tuple-element.64.r0), channel_id=1, source_target_pairs={{0,4},{1,5},{2,6},{3,7},{4,0},{5,1},{6,2},{7,3},{8,12},{9,13},{10,... | collective-permute-start | bytes 786440 | tf_op jit(solution)/shard_map/ppermute | solution.py:33
  215.2 26.2 %collective-permute-start.5 = (bf16[256,512]{1,0:T(8,128)(2,1)S(1)}, bf16[256,512]{1,0:T(8,128)(2,1)}, u32[]{:S(2)}, u32[]{:S(2)}) collective-permute-start(bf16[256,512]{1,0:T(8,128)(2,1)S(1)} %get-tuple-element.64.r0), channel_id=1, source_target_pairs={{0,2},{1,3},{2,4},{3,5},{4,6},{5,7},{6,0},{7,1},{8,10},{9,11},{10,... | collective-permute-start | bytes 786440 | tf_op jit(solution)/shard_map/ppermute | solution.py:33
  235.3 18.4 %collective-permute-start.22 = (bf16[256,512]{1,0:T(8,128)(2,1)}, bf16[256,512]{1,0:T(8,128)(2,1)S(1)}, u32[]{:S(2)}, u32[]{:S(2)}) collective-permute-start(bf16[256,512]{1,0:T(8,128)(2,1)} %get-tuple-element.49), channel_id=1, source_target_pairs={{0,2},{1,3},{2,4},{3,5},{4,6},{5,7},{6,0},{7,1},{8,10},{9,11},{10,... | collective-permute-start | bytes 786440 | tf_op jit(solution)/shard_map/ppermute | solution.py:33
  235.3 21.0 %collective-permute-start.23 = (bf16[256,512]{1,0:T(8,128)(2,1)}, bf16[256,512]{1,0:T(8,128)(2,1)}, u32[]{:S(2)}, u32[]{:S(2)}) collective-permute-start(bf16[256,512]{1,0:T(8,128)(2,1)} %get-tuple-element.50), channel_id=1, source_target_pairs={{0,4},{1,5},{2,6},{3,7},{4,0},{5,1},{6,2},{7,3},{8,12},{9,13},{10,... | collective-permute-start | bytes 786440 | tf_op jit(solution)/shard_map/ppermute | solution.py:33
  237.5 18.9 %collective-permute-start.24 = (bf16[256,512]{1,0:T(8,128)(2,1)}, bf16[256,512]{1,0:T(8,128)(2,1)}, u32[]{:S(2)}, u32[]{:S(2)}) collective-permute-start(bf16[256,512]{1,0:T(8,128)(2,1)} %get-tuple-element.51), channel_id=1, source_target_pairs={{0,6},{1,7},{2,0},{3,1},{4,2},{5,3},{6,4},{7,5},{8,14},{9,15},{10,... | collective-permute-start | bytes 786440 | tf_op jit(solution)/shard_map/ppermute | solution.py:33
  252.2 13.2 %collective-permute-start.8 = (bf16[256,512]{1,0:T(8,128)(2,1)S(1)}, bf16[256,512]{1,0:T(8,128)(2,1)S(1)}, u32[]{:S(2)}, u32[]{:S(2)}) collective-permute-start(bf16[256,512]{1,0:T(8,128)(2,1)S(1)} %get-tuple-element.38), channel_id=1, source_target_pairs={{0,2},{1,3},{2,4},{3,5},{4,6},{5,7},{6,0},{7,1},{8,10},{9,11},{10,... | collective-permute-start | bytes 786440 | tf_op jit(solution)/shard_map/ppermute | solution.py:33
  252.2 13.2 %collective-permute-start.9 = (bf16[256,512]{1,0:T(8,128)(2,1)S(1)}, bf16[256,512]{1,0:T(8,128)(2,1)S(1)}, u32[]{:S(2)}, u32[]{:S(2)}) collective-permute-start(bf16[256,512]{1,0:T(8,128)(2,1)S(1)} %get-tuple-element.39), channel_id=1, source_target_pairs={{0,4},{1,5},{2,6},{3,7},{4,0},{5,1},{6,2},{7,3},{8,12},{9,13},{10,... | collective-permute-start | bytes 786440 | tf_op jit(solution)/shard_map/ppermute | solution.py:33
  253.7 11.9 %collective-permute-start.10 = (bf16[256,512]{1,0:T(8,128)(2,1)S(1)}, bf16[256,512]{1,0:T(8,128)(2,1)S(1)}, u32[]{:S(2)}, u32[]{:S(2)}) collective-permute-start(bf16[256,512]{1,0:T(8,128)(2,1)S(1)} %get-tuple-element.40), channel_id=1, source_target_pairs={{0,6},{1,7},{2,0},{3,1},{4,2},{5,3},{6,4},{7,5},{8,14},{9,15},{10,... | collective-permute-start | bytes 786440 | tf_op jit(solution)/shard_map/ppermute | solution.py:33
  257.6 18.7 %collective-permute-start.25 = (bf16[256,512]{1,0:T(8,128)(2,1)S(1)}, bf16[256,512]{1,0:T(8,128)(2,1)}, u32[]{:S(2)}, u32[]{:S(2)}) collective-permute-start(bf16[256,512]{1,0:T(8,128)(2,1)S(1)} %add_convert_fusion), channel_id=1, source_target_pairs={{0,1},{1,0},{2,3},{3,2},{4,5},{5,4},{6,7},{7,6},{8,9},{9,8},{10,11... | collective-permute-start | bytes 786440 | tf_op jit(solution)/shard_map/ppermute | solution.py:28
  266.4 9.9 %collective-permute-start.11 = (bf16[256,512]{1,0:T(8,128)(2,1)}, bf16[256,512]{1,0:T(8,128)(2,1)}, u32[]{:S(2)}, u32[]{:S(2)}) collective-permute-start(bf16[256,512]{1,0:T(8,128)(2,1)} %add_convert_fusion.2), channel_id=1, source_target_pairs={{0,1},{1,0},{2,3},{3,2},{4,5},{5,4},{6,7},{7,6},{8,9},{9,8},{10,11... | collective-permute-start | bytes 786440 | tf_op jit(solution)/shard_map/ppermute | solution.py:28
  268.6 28.9 %all-to-all-start.3 = ((bf16[16,64,512]{2,1,0:T(8,128)(2,1)}), bf16[16,64,512]{2,1,0:T(8,128)(2,1)S(1)}, u32[]{:S(2)}, u32[]{:S(2)}) async-start(bf16[16,64,512]{2,1,0:T(8,128)(2,1)} %broadcast_in_dim.8), calls=%async_computation.3 | async-start | bytes 2097152 | tf_op jit(solution)/shard_map/all_to_all | solution.py:278
  278.6 15.1 %collective-permute-start.28 = (bf16[256,512]{1,0:T(8,128)(2,1)}, bf16[256,512]{1,0:T(8,128)(2,1)S(1)}, u32[]{:S(2)}, u32[]{:S(2)}) collective-permute-start(bf16[256,512]{1,0:T(8,128)(2,1)} %get-tuple-element.61.r0), channel_id=1, source_target_pairs={{0,6},{1,7},{2,0},{3,1},{4,2},{5,3},{6,4},{7,5},{8,14},{9,15},{10,... | collective-permute-start | bytes 786440 | tf_op jit(solution)/shard_map/ppermute | solution.py:33
  281.3 16.2 %collective-permute-start.27 = (bf16[256,512]{1,0:T(8,128)(2,1)}, bf16[256,512]{1,0:T(8,128)(2,1)}, u32[]{:S(2)}, u32[]{:S(2)}) collective-permute-start(bf16[256,512]{1,0:T(8,128)(2,1)} %get-tuple-element.61.r0), channel_id=1, source_target_pairs={{0,4},{1,5},{2,6},{3,7},{4,0},{5,1},{6,2},{7,3},{8,12},{9,13},{10,... | collective-permute-start | bytes 786440 | tf_op jit(solution)/shard_map/ppermute | solution.py:33
  282.3 15.5 %collective-permute-start.26 = (bf16[256,512]{1,0:T(8,128)(2,1)}, bf16[256,512]{1,0:T(8,128)(2,1)}, u32[]{:S(2)}, u32[]{:S(2)}) collective-permute-start(bf16[256,512]{1,0:T(8,128)(2,1)} %get-tuple-element.61.r0), channel_id=1, source_target_pairs={{0,2},{1,3},{2,4},{3,5},{4,6},{5,7},{6,0},{7,1},{8,10},{9,11},{10,... | collective-permute-start | bytes 786440 | tf_op jit(solution)/shard_map/ppermute | solution.py:33
  282.3 23.5 %collective-permute-start.14 = (bf16[256,512]{1,0:T(8,128)(2,1)S(1)}, bf16[256,512]{1,0:T(8,128)(2,1)}, u32[]{:S(2)}, u32[]{:S(2)}) collective-permute-start(bf16[256,512]{1,0:T(8,128)(2,1)S(1)} %get-tuple-element.62.r0), channel_id=1, source_target_pairs={{0,6},{1,7},{2,0},{3,1},{4,2},{5,3},{6,4},{7,5},{8,14},{9,15},{10,... | collective-permute-start | bytes 786440 | tf_op jit(solution)/shard_map/ppermute | solution.py:33
  285.5 20.3 %collective-permute-start.13 = (bf16[256,512]{1,0:T(8,128)(2,1)S(1)}, bf16[256,512]{1,0:T(8,128)(2,1)}, u32[]{:S(2)}, u32[]{:S(2)}) collective-permute-start(bf16[256,512]{1,0:T(8,128)(2,1)S(1)} %get-tuple-element.62.r0), channel_id=1, source_target_pairs={{0,4},{1,5},{2,6},{3,7},{4,0},{5,1},{6,2},{7,3},{8,12},{9,13},{10,... | collective-permute-start | bytes 786440 | tf_op jit(solution)/shard_map/ppermute | solution.py:33
  294.4 14.0 %collective-permute-start.12 = (bf16[256,512]{1,0:T(8,128)(2,1)S(1)}, bf16[256,512]{1,0:T(8,128)(2,1)}, u32[]{:S(2)}, u32[]{:S(2)}) collective-permute-start(bf16[256,512]{1,0:T(8,128)(2,1)S(1)} %get-tuple-element.62.r0), channel_id=1, source_target_pairs={{0,2},{1,3},{2,4},{3,5},{4,6},{5,7},{6,0},{7,1},{8,10},{9,11},{10,... | collective-permute-start | bytes 786440 | tf_op jit(solution)/shard_map/ppermute | solution.py:33
  (19 other events, 115.2 us)

commit v2 on v0

v2 whole, which is shorter than its diff:
```python
import math

import jax
import jax.numpy as jnp
from jax import lax
from jax.experimental import pallas as pl
from jax.experimental.pallas import tpu as pltpu
from jax.sharding import PartitionSpec as P

beta_one = 0.9
beta_two = 0.95
inner_rate = 0.02
decay_rate = 0.1
adam_eps = 1e-08
outer_rate = 0.7
outer_mu = 0.9
mix_weight = 0.5

f32 = jnp.float32
bf16 = jnp.bfloat16

RING = 4
FSDP = 8
REP = 16
TILE = 256
ORDER = (('sides', 'A', 'B', 'outer', 'A', 'pairs', 'B', 'A', 'ring', 'B', 'join'), ('A', 'B', 'A', 'B'))
MODES = (
    (("up", "up"), ("down", "down")),
    (("direct", "direct"), ("direct", "direct")),
)


def swap_x(value):
    return lax.ppermute(value, "fsdp", [(i, i ^ 1) for i in range(FSDP)])


def shift_y(value, hops):
    return lax.ppermute(value, "fsdp", [(i, (i + 2 * hops) % FSDP) for i in range(FSDP)])


def swap_core(value):
    return lax.ppermute(value, "rep", [(i, i ^ 1) for i in range(REP)])


def swap_far(value):
    return lax.ppermute(value, "rep", [(i, i ^ 2) for i in range(REP)])


def shift_z(value, hops):
    return lax.ppermute(value, "rep", [(i, (i + 4 * hops) % REP) for i in range(REP)])


def in_vmem(value):
    return pltpu.with_memory_space_constraint(value, pltpu.VMEM)


def in_hbm(value):
    return pltpu.with_memory_space_constraint(value, pltpu.HBM)


def call(body, name, place, arrays, outs, scratch=(), limit=8, flops=0, apart=(), out_hbm=False,
         aliases=None):
    vmem = pl.BlockSpec(memory_space=pltpu.VMEM)
    hbm = pl.BlockSpec(memory_space=pl.ANY)
    out = pl.BlockSpec(memory_space=pltpu.HBM) if out_hbm else vmem
    moved = sum(math.prod(a.shape) * a.dtype.itemsize for a in list(arrays) + list(apart))
    moved += sum(math.prod(shape) * jnp.dtype(kind).itemsize for shape, kind in outs)
    return pl.pallas_call(
        body,
        in_specs=[pl.BlockSpec(memory_space=pltpu.SMEM)] * (place is not None)
        + [vmem] * len(arrays) + [hbm] * len(apart),
        out_specs=[out] * len(outs),
        out_shape=[
            (pltpu.HBM if out_hbm else pltpu.VMEM)(shape, kind)
            for shape, kind in outs
        ],
        scratch_shapes=list(scratch),
        input_output_aliases=aliases or {},
        compiler_params=pltpu.CompilerParams(vmem_limit_bytes=limit * 1024 * 1024),
        cost_estimate=pl.CostEstimate(flops=0, bytes_accessed=1024, transcendentals=0),
        name=name,
    )(*([] if place is None else [place]), *[in_vmem(array) for array in arrays], *apart)


def through_vmem(pairs, held, in_sems, out_sems):
    loads = [
        pltpu.make_async_copy(src, held.at[i], in_sems.at[i]) for i, (src, _) in enumerate(pairs)
    ]
    stores = [
        pltpu.make_async_copy(held.at[i], dst, out_sems.at[i]) for i, (_, dst) in enumerate(pairs)
    ]
    for load in loads:
        load.start()
    for load, store in zip(loads, stores):
        load.wait()
        store.start()
    for store in stores:
        store.wait()


def through_scratch(rows, cols, kind):
    return [pltpu.VMEM((FSDP, rows, cols), kind), pltpu.SemaphoreType.DMA((FSDP,)),
            pltpu.SemaphoreType.DMA((FSDP,))]


def regroup_tokens(tokens, step):
    _, _, rows, width = tokens.shape
    cols = width // FSDP

    def body(src, dst, held, in_sems, out_sems):
        through_vmem(
            [(src.at[0, step, :, pl.ds(part * cols, cols)], dst.at[part]) for part in range(FSDP)],
            held, in_sems, out_sems,
        )

    return call(body, "regroup_tokens", None, [], [((FSDP, rows, cols), tokens.dtype)],
                scratch=through_scratch(rows, cols, tokens.dtype), apart=[in_hbm(tokens)],
                out_hbm=True)[0]


def tokens_by_hops(place, tokens, step):
    _, _, rows, width = tokens.shape
    cols = width // FSDP
    groups = (((1, 0), (1, 1)), ((3, 0), (3, 1)), ((0, 1), (2, 1)), ((0, 0),), ((2, 0),))

    def body(place, src, g0, g1, g2, g3, g4, held, in_sems, out_sems):
        pairs = []
        for blocks, dst in zip(groups, (g0, g1, g2, g3, g4)):
            for index, (hops, other) in enumerate(blocks):
                x = 1 - place[1] if other else place[1]
                part = 2 * lax.rem(place[0] + hops, RING) + x
                block = pl.ds(pl.multiple_of(part * cols, cols), cols)
                pairs.append((src.at[0, step, :, block], dst.at[index]))
        through_vmem(pairs, held, in_sems, out_sems)

    return call(body, "tokens_by_hops", place, [],
                [((len(blocks), rows, cols), tokens.dtype) for blocks in groups],
                scratch=through_scratch(rows, cols, tokens.dtype), apart=[in_hbm(tokens)],
                out_hbm=True)


def join_blocks(place, one, one_at, two, two_at):
    _, rows, cols = one.shape

    def body(_, one_hbm, two_hbm, out, sems):
        copies = [
            pltpu.make_async_copy(one_hbm.at[one_at], out.at[0], sems.at[0]),
            pltpu.make_async_copy(two_hbm.at[two_at], out.at[1], sems.at[1]),
        ]
        for copy in copies:
            copy.start()
        for copy in copies:
            copy.wait()

    return call(body, "join_blocks", place, [], [((2, rows, cols), one.dtype)],
                scratch=[pltpu.SemaphoreType.DMA((2,))], apart=[one, two])[0]


def ring_rows(at, hops, count):
    return pl.ds(pl.multiple_of(lax.rem(at + (hops % RING), RING) * count, count), count)


def pair_at(place, tok_refs, hops, cols):
    hops = hops % RING
    if len(tok_refs) > 1:
        places = (((0, 0), (1, 0)), ((2, 0), (5, 0)), ((4, 0), (4, 1)), ((3, 0), (5, 1)))
        return jnp.concatenate(
            [tok_refs[ref][block, :, cols] for ref, block in places[(RING - hops) % RING]], axis=0
        )
    rows = tok_refs[0].shape[0] // FSDP
    first = 2 * lax.rem(place[0] + hops, RING)
    blocks = [
        tok_refs[0][pl.ds(pl.multiple_of((first + x) * rows, rows), rows), cols]
        for x in (place[1], 1 - place[1])
    ]
    return jnp.concatenate(blocks, axis=0)


def keys_outs(mode, rows, cols):
    pair = rows // RING
    if mode == "x":
        return [((rows // 2, cols), f32), ((rows // 2, cols), bf16)]
    kept = {"direct": (), "up": (1,), "down": (3,)}[mode]
    return [((pair, cols), f32)] + [
        ((pair, cols), f32 if hops in kept else bf16) for hops in (1, 2, 3)
    ]


def partial_keys(place, mode, tok_refs, narrow_ref, out_refs):
    every = slice(None)
    for hops in (2, 1, 3, 0):
        part = jnp.dot(
            pair_at(place, tok_refs, hops, every), narrow_ref[...], preferred_element_type=f32
        )
        if mode == "x":
            rows = part.shape[0] // 2
            block = slice(hops * rows, (hops + 1) * rows)
            out_refs[0][block, :] = part[:rows]
            out_refs[1][block, :] = part[rows:].astype(bf16)
        else:
            out_refs[hops][...] = part.astype(out_refs[hops].dtype)


def narrow_chains(place, params, cols):
    width, total = params.shape[1:]
    count = total // cols

    def body(_, w_ref, *out_refs):
        for chain, out_ref in enumerate(out_refs):
            out_ref[...] = w_ref[0, :, chain * cols : (chain + 1) * cols].astype(bf16)

    return call(body, "narrow_chains", place, [params], [((width, cols), bf16)] * count)


def first_keys(place, mode, toks, narrow):
    rows, width = toks.shape
    cols = narrow.shape[1]

    def body(place, tok_ref, narrow_ref, *out_refs):
        partial_keys(place, mode, (tok_ref,), narrow_ref, out_refs)

    return call(body, "first_keys", place, [toks, narrow], keys_outs(mode, rows, cols),
                flops=2 * rows * width * cols)


def add_keys(place, kept, got):
    def body(_, kept_ref, got_ref, out_ref):
        out_ref[...] = (kept_ref[...].astype(f32) + got_ref[...].astype(f32)).astype(bf16)

    return call(body, "add_keys", place, [kept, got], [(kept.shape, bf16)])[0]


def sum_keys(place, own, got, targets, step, chain, inv_root):
    cols = own.shape[1]
    rows = targets.shape[2]

    def body(place, own_ref, *refs):
        got_refs, goal_ref, out_ref = refs[:-2], refs[-2], refs[-1]
        at = slice(chain * cols, (chain + 1) * cols)
        for start in range(0, own.shape[0], rows):
            part = slice(start, start + rows)
            total = own_ref[part, :]
            for ref in got_refs:
                total = total + ref[part, :].astype(f32)
            total = total * inv_root
            if start == 0:
                total = total - goal_ref[0, step, :, at].astype(f32)
            out_ref[part, :] = total.astype(bf16)

    return call(body, "sum_keys", place, [own, *got, targets], [(own.shape, bf16)])[0]


def pair_resid(place, half, other):
    rows = half.shape[0] // 2

    def body(_, half_ref, other_ref, out_ref):
        for mine, theirs in ((slice(0, rows), slice(rows, None)), (slice(rows, None), slice(0, rows))):
            out_ref[mine, :] = (
                half_ref[mine, :].astype(f32) + other_ref[theirs, :].astype(f32)
            ).astype(bf16)

    return call(body, "pair_resid", place, [half, other], [(half.shape, bf16)])[0]


def add_far_keys(place, own, got):
    rows = own.shape[0] // RING
    cols = own.shape[1]

    def body(_, own_ref, got_ref, *out_refs):
        for hops, out_ref in enumerate(out_refs):
            block = slice(hops * rows, (hops + 1) * rows)
            total = own_ref[block, :] + got_ref[block, :].astype(f32)
            out_ref[...] = total.astype(out_ref.dtype)

    return call(body, "add_far_keys", place, [own, got],
                [((rows, cols), f32)] + [((rows, cols), bf16)] * (RING - 1))


def join_pair(place, near, far):
    rows, cols = near.shape

    def body(_, near_ref, far_ref, out_ref):
        out_ref[:rows, :] = near_ref[...]
        out_ref[rows:, :] = far_ref[...]

    return call(body, "join_pair", place, [near, far], [((2 * rows, cols), bf16)])[0]


def resid_at(resid_refs, hops):
    if len(resid_refs) == RING:
        return resid_refs[hops][...]
    return jnp.concatenate([resid_refs[hops][...], resid_refs[RING][hops]], axis=0)


def join_resids(place, resids):
    rows, cols = resids[0].shape

    def body(_, r0, r1, r2, r3, out_ref):
        for hops, ref in enumerate((r0, r1, r2, r3)):
            out_ref[hops] = ref[...]

    return call(body, "join_resids", place, resids, [((RING, rows, cols), bf16)])[0]


def grad_tile(place, tok_refs, resid_refs, tile, inv_root):
    total = None
    for hops in range(RING):
        part = lax.dot_general(
            pair_at(place, tok_refs, -hops, tile),
            resid_at(resid_refs, hops),
            (((0,), (0,)), ((), ())),
            preferred_element_type=f32,
        )
        total = part if total is None else total + part
    return total * inv_root


def adam(grad, first, second, weights):
    first = beta_one * first.astype(f32) + (1.0 - beta_one) * grad
    second = beta_two * second.astype(f32) + (1.0 - beta_two) * grad * grad
    weights = weights - inner_rate * (
        first / (jnp.sqrt(second) + adam_eps) + decay_rate * weights
    )
    return first, second, weights


def middle_step(place, mode, toks, next_toks, resids, params, moment1, moment2, chain, inv_root):
    rows, width = toks.shape
    cols = resids[0].shape[1]
    at = slice(chain * cols, (chain + 1) * cols)

    def body(place, tok_ref, n0, n1, n2, n3, n4, n5, w_ref, m_ref, v_ref, *rest):
        resid_refs, rest = rest[: len(resids)], rest[len(resids) :]
        w_out, m_out, v_out, *out_refs, narrow = rest
        for start in range(0, width, TILE):
            tile = slice(start, start + TILE)
            grad = grad_tile(place, (tok_ref,), resid_refs, tile, inv_root)
            m_new, v_new, w_new = adam(grad, m_ref[0, tile, at], v_ref[0, tile, at], w_ref[0, tile, at])
            w_out[tile, :] = w_new
            m_out[tile, :] = m_new.astype(bf16)
            v_out[tile, :] = v_new.astype(bf16)
            narrow[tile, :] = w_new.astype(bf16)
        partial_keys(place, mode, (n0, n1, n2, n3, n4, n5), narrow, out_refs)

    outs = [((width, cols), f32), ((width, cols), bf16), ((width, cols), bf16)]
    return call(body, "middle_step", place,
                [toks, *next_toks, params, moment1, moment2, *resids],
                outs + keys_outs(mode, rows, cols), scratch=[pltpu.VMEM((width, cols), bf16)],
                flops=4 * rows * width * cols)


def last_step(place, toks, resids, weights, first, second, anchors, chain, inv_root, outs):
    width, cols = weights.shape
    rows = FSDP * toks[0].shape[1]
    slice_rows = width // REP
    at = pl.ds(chain * cols, cols)
    total = 2 * cols

    def body(place, t0, t1, t2, t3, t4, t5, w_ref, m_ref, v_ref, same_ref, other_ref, *rest):
        resid_refs = rest[: len(resids)]
        w_hbm, m_hbm, v_hbm, w_out, m_out, v_out, sems = rest[-7:]
        copies = []
        for index, start in enumerate(range(0, width, TILE)):
            tile = pl.ds(start, TILE)
            grad = grad_tile(place, (t0, t1, t2, t3, t4, t5), resid_refs, tile, inv_root)
            m_new, v_new, w_new = adam(grad, m_ref[tile, :], v_ref[tile, :], w_ref[tile, :])
            m_out[tile, :] = m_new.astype(bf16)
            v_out[tile, :] = v_new.astype(bf16)
            w_out[tile, :] = w_new

            @pl.when(place[5] == chain)
            def _():
                for begin in range(start, start + TILE, slice_rows):
                    owner = begin // slice_rows
                    block = slice(begin, begin + slice_rows)
                    source = slice((owner // 2) * slice_rows, (owner // 2 + 1) * slice_rows)
                    fresh = jnp.where(
                        place[4] == owner % 2,
                        same_ref[source, :].astype(f32),
                        other_ref[source, :].astype(f32),
                    )
                    w_out[block, :] = mix_weight * w_out[block, :] + (1.0 - mix_weight) * fresh

            for which, (src, dst) in enumerate(((w_out, w_hbm), (m_out, m_hbm), (v_out, v_hbm))):
                copy = pltpu.make_async_copy(
                    src.at[tile, :], dst.at[0, tile, at], sems.at[which, index]
                )
                copy.start()
                copies.append(copy)
        for copy in copies:
            copy.wait()

    arrays = [*toks, weights, first, second, *anchors, *resids]
    results = [((1, width, total), f32), ((1, width, total), bf16), ((1, width, total), bf16)]
    aliases = {1 + len(arrays) + i: i for i in range(3)} if outs else {}
    return call(body, "last_step", place, arrays, results, apart=outs, out_hbm=True,
                scratch=[pltpu.VMEM((width, cols), f32), pltpu.VMEM((width, cols), bf16),
                         pltpu.VMEM((width, cols), bf16),
                         pltpu.SemaphoreType.DMA((3, width // TILE))],
                limit=16, flops=2 * rows * width * cols, aliases=aliases)


def delta_for_core(place, delta):
    rows, cols = delta.shape
    part = rows // REP

    def body(place, delta_ref, out_ref):
        for j in range(REP // 2):
            source = pl.ds(pl.multiple_of((2 * j + 1 - place[4]) * part, part), part)
            out_ref[j * part : (j + 1) * part, :] = delta_ref[source, :].astype(bf16)

    return call(body, "delta_for_core", place, [delta], [((rows // 2, cols), bf16)])[0]


def delta_for_ring(place, delta, got):
    rows, cols = delta.shape
    part = rows // REP

    def body(place, delta_ref, got_ref, own_ref, s1, s2, s3):
        for hops in range(RING):
            ring = lax.rem(place[2] + hops, RING)
            for far in range(2):
                j = 2 * ring + far
                near = pl.ds(pl.multiple_of((2 * j + place[4]) * part, part), part)
                sent = pl.ds(pl.multiple_of(j * part, part), part)
                total = delta_ref[near, :] + got_ref[sent, :].astype(f32)
                block = slice(far * part, (far + 1) * part)
                if hops:
                    (s1, s2, s3)[hops - 1][block, :] = total.astype(bf16)
                else:
                    own_ref[block, :] = total

    return call(body, "delta_for_ring", place, [delta, got],
                [((2 * part, cols), f32)] + [((2 * part, cols), bf16)] * (RING - 1))


def delta_for_far(place, own, got, anchor, momentum):
    rows, cols = own.shape
    part = anchor.shape[2]

    def body(place, own_ref, g1, g2, g3, a_ref, p_ref, keep_ref, send_ref):
        total = own_ref[...]
        for ref in (g1, g2, g3):
            total = total + ref[...].astype(f32)
        keep_ref[...] = total
        send_ref[:rows, :] = total.astype(bf16)
        base = a_ref[place[5], 0] - outer_rate * outer_mu * outer_mu * p_ref[place[5], 0]
        send_ref[rows:, :] = base.astype(bf16)

    return call(body, "delta_for_far", place, [own, *got, anchor, momentum],
                [(own.shape, f32), ((rows + part, cols), bf16)])


def outer_step(place, keep, got, anchor, momentum):
    _, _, part, cols = anchor.shape

    def body(place, keep_ref, got_ref, a_ref, p_ref, a_out, p_out, new_ref):
        a_out[...] = a_ref[...]
        p_out[...] = p_ref[...]
        fragment = place[5]
        for far in range(2):
            block = slice(far * part, (far + 1) * part)
            mean = (keep_ref[block, :] + got_ref[block, :].astype(f32)) / REP

            @pl.when(place[3] == far)
            def _():
                moment = outer_mu * p_ref[fragment, 0] + mean
                fresh = a_ref[fragment, 0] - outer_rate * (mean + outer_mu * moment)
                p_out[fragment, 0] = moment
                a_out[fragment, 0] = fresh
                new_ref[block, :] = fresh.astype(bf16)

            @pl.when(place[3] != far)
            def _():
                base = got_ref[2 * part :, :].astype(f32)
                fresh = base - outer_rate * (1.0 + outer_mu) * mean
                new_ref[block, :] = fresh.astype(bf16)

    return call(body, "outer_step", place, [keep, got, anchor, momentum],
                [(anchor.shape, f32), (momentum.shape, f32), (keep.shape, bf16)])


def join_ring(place, pieces):
    part, cols = pieces[0].shape

    def body(place, p0, p1, p2, p3, out_ref):
        for hops, ref in enumerate((p0, p1, p2, p3)):
            out_ref[ring_rows(place[2], RING - hops, part), :] = ref[...]

    return call(body, "join_ring", place, pieces, [((RING * part, cols), bf16)])[0]


class InOrder:
    def __init__(self, place):
        self.place = place

    def __call__(self, kernel, *args):
        results = kernel(self.place, *args)
        single = not isinstance(results, (list, tuple))
        results = [results] if single else list(results)
        results[-1] = self.after(results[-1])
        return results[0] if single else results

    def after(self, value):
        self.place, value = lax.optimization_barrier((self.place, value))
        return value


def by_hops(values):
    return [shift_y(values[hops - 1], hops) for hops in (1, 2, 3)]


def resids_of(run, modes, parts, targets, step, chain, inv_root):
    reduce_mode, gather_mode = modes
    own, *sent = parts
    if reduce_mode == "x":
        own, *sent = run(add_far_keys, own, swap_x(sent[0]))
        got = by_hops(sent)
        yield
        resid = run(sum_keys, own, got, targets, step, chain, inv_root)
        if gather_mode == "x":
            resids = [resid, *by_hops([resid] * 3)]
            yield
            yield [*resids, swap_x(run(join_resids, resids))]
            return
        other = swap_x(resid)
        yield
        resid = run(join_pair, resid, other)
    else:
        k1, k2, k3 = sent
        if reduce_mode == "direct":
            got = by_hops(sent)
        elif reduce_mode == "up":
            relay = run(add_keys, k1, shift_y(k2, 1))
            got = [shift_y(relay, 1), shift_y(k3, 3)]
            yield
        else:
            relay = run(add_keys, k3, shift_y(k2, 3))
            got = [shift_y(relay, 3), shift_y(k1, 1)]
            yield
        half = run(sum_keys, own, got, targets, step, chain, inv_root)
        other = swap_x(half)
        yield
        resid = run(pair_resid, half, other)
    if gather_mode == "direct":
        resids = [resid, *by_hops([resid] * 3)]
    else:
        up, down = shift_y(resid, 1), shift_y(resid, 3)
        resids = [resid, up, shift_y(up, 1) if gather_mode == "up" else shift_y(down, 3), down]
    yield resids


def on_device(tokens, targets, params, moment1, moment2, stale_delta, anchor, momentum, plan):
    inv_root = 1.0 / math.sqrt(tokens.shape[3])
    here = lax.axis_index("fsdp")
    home = lax.axis_index("rep")
    run = InOrder(
        jnp.stack(
            [here // 2, here % 2, home // 4, (home // 2) % 2, home % 2, plan[0]]
        ).astype(jnp.int32)
    )
    cols = stale_delta.shape[2]
    chains = range(params.shape[2] // cols)
    delta = stale_delta[0]

    toks = run.after(regroup_tokens(tokens, 0))
    toks = lax.all_to_all(toks, "fsdp", split_axis=0, concat_axis=0, tiled=True)
    toks = toks.reshape(-1, toks.shape[-1])

    up, down, far, near, opposite = run(tokens_by_hops, tokens, 1)
    up, down, far = shift_y(up, 1), shift_y(down, 3), swap_x(far)
    got = swap_core(run(delta_for_core, delta))
    own, *sent = run(delta_for_ring, delta, got)
    got = [shift_z(sent[h - 1], h) for h in (1, 2, 3)]
    narrow = run(narrow_chains, params, cols)
    keep, send = run(delta_for_far, own, got, anchor, momentum)
    toks = run.after(toks)

    parts = {}
    for chain in chains:
        parts[chain] = run(first_keys, MODES[0][chain][0], toks, narrow[chain])
    steps = [resids_of(run, MODES[0][c], parts[c], targets, 0, c, inv_root) for c in chains]
    resids = {}

    def advance(order):
        nonlocal got, fresh, anchors, next_toks, opposite, sides
        for name in order:
            if name in ("A", "B"):
                chain = ("A", "B").index(name)
                resids[chain] = next(steps[chain])
            elif name == "pairs":
                opposite = shift_y(run(join_blocks, opposite, 0, far, 1), 2)
            elif name == "sides":
                sides = swap_x(run(join_blocks, up, 1, down, 1))
            elif name == "join":
                next_toks = run.after([near, far, up, down, opposite, sides])
            elif name == "outer":
                results.extend(run(outer_step, keep, swap_far(send), anchor, momentum))
                fresh = results.pop()
                up_z, down_z = shift_z(fresh, 1), shift_z(fresh, 3)
                got = [up_z, shift_z(up_z, 1), down_z]
            elif name == "ring":
                fresh = run(join_ring, [fresh, *got])
                anchors = (fresh, swap_core(fresh))

    results = []
    fresh = anchors = next_toks = sides = None
    advance(ORDER[0])
    state = {}
    for chain in chains:
        w, m, v, *parts[chain] = run(
            middle_step, MODES[1][chain][0], toks, next_toks, resids[chain], params, moment1,
            moment2, chain, inv_root
        )
        state[chain] = (w, m, v)
    steps = [resids_of(run, MODES[1][c], parts[c], targets, 1, c, inv_root) for c in chains]
    advance(ORDER[1])
    outs = []
    for chain in chains:
        outs = run(last_step, next_toks, resids[chain], *state[chain], anchors, chain, inv_root, outs)
    return (*outs, *results)


def solution(mesh):
    return jax.shard_map(
        on_device,
        mesh=mesh,
        in_specs=(
            P("rep", None, "fsdp", None),
            P("rep", None, "fsdp", None),
            P("rep", "fsdp", None),
            P("rep", "fsdp", None),
            P("rep", "fsdp", None),
            P("rep", "fsdp", None),
            P(None, "fsdp", "rep", None),
            P(None, "fsdp", "rep", None),
            P(),
        ),
        out_specs=(
            P("rep", "fsdp", None),
            P("rep", "fsdp", None),
            P("rep", "fsdp", None),
            P(None, "fsdp", "rep", None),
            P(None, "fsdp", "rep", None),
        ),
        check_vma=False,
    )
```

time: 599 us -> 164 us (0.27)
  waiting for transfers between devices: 445 us -> 57.1 us
  starting transfers between devices: 4.62 us -> 59.8 us
  local copies, waits for them, and re-layouts: 54.1 us -> 5.22 us
  Pallas kernels: 0 us -> 39.5 us
  matrix products: 35.9 us -> 0 us
  blocking collectives: 32.6 us -> 0 us
  between operations: 16.4 us -> 1.95 us
  other arithmetic: 8.85 us -> 0 us
    reduce_scatter x2 -> x0, waiting for transfers between devices: 183 us -> none  [on_device(): lax.psum_scatter(partial_keys(jnp.int32(0), lax.axis_size('fsdp') * tok_r...]
    psum x1 -> x0, waiting for transfers between devices: 140 us -> none  [on_device(): total = lax.psum(delta.astype(jnp.bfloat16), 'rep').astype(jnp.float32)]
    all_gather x4 -> x0, waiting for transfers between devices: 87.5 us -> none  [the longest x2 67.3 us: on_device(): lax.all_gather(resid, 'fsdp', axis=0, tiled=True)]
    ppermute x0 -> x42, starting transfers between devices: none -> 54.3 us  [the longest x27 33 us: shift_y(): lax.ppermute(value, 'fsdp', [(i, (i + 2 * hops) % FSDP) for i in range(FS...]
    ppermute x0 -> x42, waiting for transfers between devices: none -> 53.1 us  [the longest x27 36.8 us: shift_y(): lax.ppermute(value, 'fsdp', [(i, (i + 2 * hops) % FSDP) for i in range(FS...]
    pallas_call x0 -> x26, Pallas kernels: none -> 39.5 us  [call(): pl.pallas_call(body, in_specs=[pl.BlockSpec(memory_space=pltpu.SMEM)] * (...]
    dot_general x4 -> x0, matrix products: 35.9 us -> none  [the longest x2 24.2 us: add_grad(): lax.dot_general(sliced, piece, (((0,), (0,)), ((), ())), preferred_elemen...]
    unnamed x32 -> x42, local copies, waits for them, and re-layouts: 38.3 us -> 5.13 us
  transfers between devices with their start and end apart: 8 -> 43, of which waited for: 7 -> 19; matrix products, arithmetic and copies ran while one was open for 5% -> 1% of each run, Pallas kernels for 0% -> 19%
where the time goes in v2:
time: 164 us
  starting transfers between devices  59.8 us (36%)
  waiting for transfers between devices  57.1 us (35%)
  Pallas kernels  39.5 us (24%)
  local copies, waits for them, and re-layouts  5.22 us (3%)
  between operations  1.95 us (1%)
    pallas_call x26, Pallas kernels, call(): pl.pallas_call(body, in_specs=[pl.BlockSpec(memory_space=pltpu.SMEM)] * (...  39.5 us
    ppermute x27, waiting for transfers between devices, shift_y(): lax.ppermute(value, 'fsdp', [(i, (i + 2 * hops) % FSDP) for i in range(FS...  36.8 us
    ppermute x27, starting transfers between devices, shift_y(): lax.ppermute(value, 'fsdp', [(i, (i + 2 * hops) % FSDP) for i in range(FS...  33 us
    ppermute x6, starting transfers between devices, shift_z(): lax.ppermute(value, 'rep', [(i, (i + 4 * hops) % REP) for i in range(REP)])  11.5 us
    ppermute x6, waiting for transfers between devices, shift_z(): lax.ppermute(value, 'rep', [(i, (i + 4 * hops) % REP) for i in range(REP)])  11.1 us
    ppermute x6, starting transfers between devices, swap_x(): return lax.ppermute(value, 'fsdp', [(i, i ^ 1) for i in range(FSDP)])  6.91 us
    all_to_all x1, starting transfers between devices, on_device(): toks = lax.all_to_all(toks, 'fsdp', split_axis=0, concat_axis=0, tiled=True)  5.48 us
    unnamed x42, local copies, waits for them, and re-layouts  5.13 us
  transfers between devices with their start and end apart: 43, of which 19 were waited for; matrix products, arithmetic and copies ran while one was open for 1% of the time, Pallas kernels for 19%

profile of v2, /device:TPU:0, one launch (start us, length us, event | category | flops | bytes accessed | tf_op | source)
XLA Modules:
  0.0 163.6 jit_solution(8506734146414670918)
XLA Ops:
  1.3 2.4 %regroup_tokens.1 = bf16[8,128,1024]{2,1,0:T(8,128)(2,1)} custom-call(bf16[1,2,128,8192]{3,2,1,0:T(8,128)(2,1)} %src.3), custom_call_target="tpu_custom_call" | custom-call | bytes 1024 | tf_op jit(solution)/shard_map/regroup_tokens/pallas_call | solution.py:68
  3.9 5.5 %all-to-all-start = ((bf16[8,128,1024]{2,1,0:T(8,128)(2,1)}), bf16[8,128,1024]{2,1,0:T(8,128)(2,1)S(1)}, u32[]{:S(2)}, u32[]{:S(2)}) async-start(bf16[8,128,1024]{2,1,0:T(8,128)(2,1)} %regroup_tokens.1), calls=%async_computation | async-start | bytes 4194304 | tf_op jit(solution)/shard_map/all_to_all | solution.py:567
  9.3 3.0 %tokens_by_hops.1 = (bf16[2,128,1024]{2,1,0:T(8,128)(2,1)}, bf16[2,128,1024]{2,1,0:T(8,128)(2,1)}, bf16[2,128,1024]{2,1,0:T(8,128)(2,1)}, bf16[1,128,1024]{2,1,0:T(8,128)(2,1)}, bf16[1,128,1024]{2,1,0:T(8,128)(2,1)}) custom-call(s32[6]{0:T(128)S(1)} %stack.23.place._, bf16[1,2,128,8192]{3,2,1,0:T(8,128)(2,1)} %src.3), custom_call_target="tpu_custom_call" | custom-call | bytes 1024 | tf_op jit(solution)/shard_map/tokens_by_hops/pallas_call | solution.py:68
  13.1 2.1 %collective-permute-start.4 = (bf16[2,128,1024]{2,1,0:T(8,128)(2,1)}, bf16[2,128,1024]{2,1,0:T(8,128)(2,1)S(1)}, u32[]{:S(2)}, u32[]{:S(2)}) collective-permute-start(bf16[2,128,1024]{2,1,0:T(8,128)(2,1)} %get-tuple-element.133), channel_id=1, source_target_pairs={{0,2},{1,3},{2,4},{3,5},{4,6},{5,7},{6,0},{7,1},{8,10},{9,11},{10,... | collective-permute-start | bytes 1572872 | tf_op jit(solution)/shard_map/ppermute | solution.py:38
  17.1 4.1 %collective-permute-start.3 = (bf16[128,512]{1,0:T(8,128)(2,1)S(1)}, bf16[128,512]{1,0:T(8,128)(2,1)S(1)}, u32[]{:S(2)}, u32[]{:S(2)}) collective-permute-start(bf16[128,512]{1,0:T(8,128)(2,1)S(1)} %get-tuple-element.121), channel_id=1, source_target_pairs={{0,96},{8,104},{16,112},{24,120},{32,0},{40,8},{48,16},{56,24},{64... | collective-permute-start | bytes 393224 | tf_op jit(solution)/shard_map/ppermute | solution.py:50
  21.2 1.9 %collective-permute-start.2 = (bf16[128,512]{1,0:T(8,128)(2,1)S(1)}, bf16[128,512]{1,0:T(8,128)(2,1)S(1)}, u32[]{:S(2)}, u32[]{:S(2)}) collective-permute-start(bf16[128,512]{1,0:T(8,128)(2,1)S(1)} %get-tuple-element.120), channel_id=1, source_target_pairs={{0,64},{8,72},{16,80},{24,88},{32,96},{40,104},{48,112},{56,120},{... | collective-permute-start | bytes 393224 | tf_op jit(solution)/shard_map/ppermute | solution.py:50
  24.8 5.6 %collective-permute-done.1.g1 = bf16[128,512]{1,0:T(8,128)(2,1)S(1)} collective-permute-done((bf16[128,512]{1,0:T(8,128)(2,1)S(1)}, bf16[128,512]{1,0:T(8,128)(2,1)S(1)}, u32[]{:S(2)}, u32[]{:S(2)}) %collective-permute-start.1) | collective-permute-done | bytes 131104 | tf_op jit(solution)/shard_map/ppermute | solution.py:50
  32.5 4.0 %all-to-all-done = bf16[8,128,1024]{2,1,0:T(8,128)(2,1)S(1)} async-done(((bf16[8,128,1024]{2,1,0:T(8,128)(2,1)}), bf16[8,128,1024]{2,1,0:T(8,128)(2,1)S(1)}, u32[]{:S(2)}, u32[]{:S(2)}) %all-to-all-start) | async-done | bytes 2097184 | tf_op jit(solution)/shard_map/all_to_all | solution.py:567
  41.9 1.8 %first_keys.3 = (f32[256,512]{1,0:T(8,128)S(1)}, bf16[256,512]{1,0:T(8,128)(2,1)S(1)}, bf16[256,512]{1,0:T(8,128)(2,1)S(1)}, f32[256,512]{1,0:T(8,128)S(1)}) custom-call(s32[6]{0:T(128)S(1)} %stack.23.place._, bf16[1024,1024]{1,0:T(8,128)(2,1)S(1)} %bitcast.8, bf16[1024,512]{1,0:T(8,128)(2,1)S(1)} %copy-done.8), custom_call_target="tpu_custom_call" | custom-call | bytes 1024 | tf_op jit(solution)/shard_map/first_keys/pallas_call | solution.py:68
  43.8 3.2 %collective-permute-start.7 = (bf16[256,512]{1,0:T(8,128)(2,1)S(1)}, bf16[256,512]{1,0:T(8,128)(2,1)S(1)}, u32[]{:S(2)}, u32[]{:S(2)}) collective-permute-start(bf16[256,512]{1,0:T(8,128)(2,1)S(1)} %get-tuple-element.140), channel_id=1, source_target_pairs={{0,6},{1,7},{2,0},{3,1},{4,2},{5,3},{6,4},{7,5},{8,14},{9,15},{10,... | collective-permute-start | bytes 786440 | tf_op jit(solution)/shard_map/ppermute | solution.py:38
  49.5 2.7 %collective-permute-done.6.got_ref = bf16[256,512]{1,0:T(8,128)(2,1)S(1)} collective-permute-done((bf16[256,512]{1,0:T(8,128)(2,1)S(1)}, bf16[256,512]{1,0:T(8,128)(2,1)S(1)}, u32[]{:S(2)}, u32[]{:S(2)}) %collective-permute-start.6) | collective-permute-done | bytes 262176 | tf_op jit(solution)/shard_map/ppermute | solution.py:38
  52.9 2.8 %collective-permute-start.8 = (bf16[192,512]{1,0:T(8,128)(2,1)S(1)}, bf16[192,512]{1,0:T(8,128)(2,1)S(1)}, u32[]{:S(2)}, u32[]{:S(2)}) collective-permute-start(bf16[192,512]{1,0:T(8,128)(2,1)S(1)} %copy-done.18), channel_id=1, source_target_pairs={{0,16},{8,24},{16,0},{24,8},{32,48},{40,56},{48,32},{56,40},{64,80... | collective-permute-start | bytes 589832 | tf_op jit(solution)/shard_map/ppermute | solution.py:46
  57.0 3.5 %collective-permute-done.8.got_ref = bf16[192,512]{1,0:T(8,128)(2,1)S(1)} collective-permute-done((bf16[192,512]{1,0:T(8,128)(2,1)S(1)}, bf16[192,512]{1,0:T(8,128)(2,1)S(1)}, u32[]{:S(2)}, u32[]{:S(2)}) %collective-permute-start.8) | collective-permute-done | bytes 196640 | tf_op jit(solution)/shard_map/ppermute | solution.py:46
  61.3 2.9 %collective-permute-start.12 = (bf16[256,512]{1,0:T(8,128)(2,1)S(1)}, bf16[256,512]{1,0:T(8,128)(2,1)S(1)}, u32[]{:S(2)}, u32[]{:S(2)}) collective-permute-start(bf16[256,512]{1,0:T(8,128)(2,1)S(1)} %add_keys.3), channel_id=1, source_target_pairs={{0,6},{1,7},{2,0},{3,1},{4,2},{5,3},{6,4},{7,5},{8,14},{9,15},{10,... | collective-permute-start | bytes 786440 | tf_op jit(solution)/shard_map/ppermute | solution.py:38
  66.3 4.0 %collective-permute-start.17 = (bf16[128,512]{1,0:T(8,128)(2,1)S(1)}, bf16[128,512]{1,0:T(8,128)(2,1)S(1)}, u32[]{:S(2)}, u32[]{:S(2)}) collective-permute-start(bf16[128,512]{1,0:T(8,128)(2,1)S(1)} %get-tuple-element.159.p0), channel_id=1, source_target_pairs={{0,96},{8,104},{16,112},{24,120},{32,0},{40,8},{48,16},{56,24},{64... | collective-permute-start | bytes 393224 | tf_op jit(solution)/shard_map/ppermute | solution.py:50
  78.0 5.1 %collective-permute-done.16.p2 = bf16[128,512]{1,0:T(8,128)(2,1)S(1)} collective-permute-done((bf16[128,512]{1,0:T(8,128)(2,1)S(1)}, bf16[128,512]{1,0:T(8,128)(2,1)S(1)}, u32[]{:S(2)}, u32[]{:S(2)}) %collective-permute-start.16) | collective-permute-done | bytes 131104 | tf_op jit(solution)/shard_map/ppermute | solution.py:50
  86.1 4.9 %collective-permute-done.21.rest_1_ = bf16[256,512]{1,0:T(8,128)(2,1)S(1)} collective-permute-done((bf16[256,512]{1,0:T(8,128)(2,1)S(1)}, bf16[256,512]{1,0:T(8,128)(2,1)S(1)}, u32[]{:S(2)}, u32[]{:S(2)}) %collective-permute-start.21) | collective-permute-done | bytes 262176 | tf_op jit(solution)/shard_map/ppermute | solution.py:38
  92.0 2.7 %collective-permute-start.26 = (bf16[256,512]{1,0:T(8,128)(2,1)S(1)}, bf16[256,512]{1,0:T(8,128)(2,1)S(1)}, u32[]{:S(2)}, u32[]{:S(2)}) collective-permute-start(bf16[256,512]{1,0:T(8,128)(2,1)S(1)} %collective-permute-done.25.rest_3_), channel_id=1, source_target_pairs={{0,6},{1,7},{2,0},{3,1},{4,2},{5,3},{6,4},{7,5},{8,14},{9,15},{10,... | collective-permute-start | bytes 786440 | tf_op jit(solution)/shard_map/ppermute | solution.py:38
  95.9 5.4 %collective-permute-done.22.rest_2_ = bf16[256,512]{1,0:T(8,128)(2,1)S(1)} collective-permute-done((bf16[256,512]{1,0:T(8,128)(2,1)S(1)}, bf16[256,512]{1,0:T(8,128)(2,1)S(1)}, u32[]{:S(2)}, u32[]{:S(2)}) %collective-permute-start.22) | collective-permute-done | bytes 262176 | tf_op jit(solution)/shard_map/ppermute | solution.py:38
  101.4 4.4 %middle_step.2 = (f32[1024,512]{1,0:T(8,128)S(1)}, bf16[1024,512]{1,0:T(8,128)(2,1)S(1)}, bf16[1024,512]{1,0:T(8,128)(2,1)S(1)}, f32[256,512]{1,0:T(8,128)S(1)},...) custom-call(s32[6]{0:T(128)S(1)} %stack.23.place._, ...), custom_call_target="tpu_custom_call" | custom-call | bytes 1024 | tf_op jit(solution)/shard_map/middle_step/pallas_call | solution.py:68
  105.8 2.0 %collective-permute-start.27 = (bf16[256,512]{1,0:T(8,128)(2,1)S(1)}, bf16[256,512]{1,0:T(8,128)(2,1)S(1)}, u32[]{:S(2)}, u32[]{:S(2)}) collective-permute-start(bf16[256,512]{1,0:T(8,128)(2,1)S(1)} %get-tuple-element.180), channel_id=1, source_target_pairs={{0,2},{1,3},{2,4},{3,5},{4,6},{5,7},{6,0},{7,1},{8,10},{9,11},{10,... | collective-permute-start | bytes 786440 | tf_op jit(solution)/shard_map/ppermute | solution.py:38
  107.9 4.4 %middle_step.3 = (f32[1024,512]{1,0:T(8,128)S(1)}, bf16[1024,512]{1,0:T(8,128)(2,1)S(1)}, bf16[1024,512]{1,0:T(8,128)(2,1)S(1)}, f32[256,512]{1,0:T(8,128)S(1)},...) custom-call(s32[6]{0:T(128)S(1)} %stack.23.place._, ...), custom_call_target="tpu_custom_call" | custom-call | bytes 1024 | tf_op jit(solution)/shard_map/middle_step/pallas_call | solution.py:68
  112.3 2.7 %collective-permute-start.32 = (bf16[256,512]{1,0:T(8,128)(2,1)S(1)}, bf16[256,512]{1,0:T(8,128)(2,1)S(1)}, u32[]{:S(2)}, u32[]{:S(2)}) collective-permute-start(bf16[256,512]{1,0:T(8,128)(2,1)S(1)} %get-tuple-element.187), channel_id=1, source_target_pairs={{0,6},{1,7},{2,0},{3,1},{4,2},{5,3},{6,4},{7,5},{8,14},{9,15},{10,... | collective-permute-start | bytes 786440 | tf_op jit(solution)/shard_map/ppermute | solution.py:38
  115.1 2.8 %collective-permute-start.31 = (bf16[256,512]{1,0:T(8,128)(2,1)S(1)}, bf16[256,512]{1,0:T(8,128)(2,1)S(1)}, u32[]{:S(2)}, u32[]{:S(2)}) collective-permute-start(bf16[256,512]{1,0:T(8,128)(2,1)S(1)} %get-tuple-element.186), channel_id=1, source_target_pairs={{0,4},{1,5},{2,6},{3,7},{4,0},{5,1},{6,2},{7,3},{8,12},{9,13},{10,... | collective-permute-start | bytes 786440 | tf_op jit(solution)/shard_map/ppermute | solution.py:38
  117.9 2.8 %collective-permute-done.27.refs_0_ = bf16[256,512]{1,0:T(8,128)(2,1)S(1)} collective-permute-done((bf16[256,512]{1,0:T(8,128)(2,1)S(1)}, bf16[256,512]{1,0:T(8,128)(2,1)S(1)}, u32[]{:S(2)}, u32[]{:S(2)}) %collective-permute-start.27) | collective-permute-done | bytes 262176 | tf_op jit(solution)/shard_map/ppermute | solution.py:38
  122.5 3.8 %collective-permute-done.32.refs_2_ = bf16[256,512]{1,0:T(8,128)(2,1)S(1)} collective-permute-done((bf16[256,512]{1,0:T(8,128)(2,1)S(1)}, bf16[256,512]{1,0:T(8,128)(2,1)S(1)}, u32[]{:S(2)}, u32[]{:S(2)}) %collective-permute-start.32) | collective-permute-done | bytes 262176 | tf_op jit(solution)/shard_map/ppermute | solution.py:38
  126.3 4.1 %collective-permute-done.30.refs_0_ = bf16[256,512]{1,0:T(8,128)(2,1)S(1)} collective-permute-done((bf16[256,512]{1,0:T(8,128)(2,1)S(1)}, bf16[256,512]{1,0:T(8,128)(2,1)S(1)}, u32[]{:S(2)}, u32[]{:S(2)}) %collective-permute-start.30) | collective-permute-done | bytes 262176 | tf_op jit(solution)/shard_map/ppermute | solution.py:38
  140.8 3.0 %collective-permute-done.38.rest_3_ = bf16[256,512]{1,0:T(8,128)(2,1)S(1)} collective-permute-done((bf16[256,512]{1,0:T(8,128)(2,1)S(1)}, bf16[256,512]{1,0:T(8,128)(2,1)S(1)}, u32[]{:S(2)}, u32[]{:S(2)}) %collective-permute-start.38) | collective-permute-done | bytes 262176 | tf_op jit(solution)/shard_map/ppermute | solution.py:38
  145.5 5.7 %collective-permute-done.36.rest_1_ = bf16[256,512]{1,0:T(8,128)(2,1)S(1)} collective-permute-done((bf16[256,512]{1,0:T(8,128)(2,1)S(1)}, bf16[256,512]{1,0:T(8,128)(2,1)S(1)}, u32[]{:S(2)}, u32[]{:S(2)}) %collective-permute-start.36) | collective-permute-done | bytes 262176 | tf_op jit(solution)/shard_map/ppermute | solution.py:38
  151.2 5.0 %last_step.2 = (f32[1,1024,1024]{2,1,0:T(8,128)}, bf16[1,1024,1024]{2,1,0:T(8,128)(2,1)}, bf16[1,1024,1024]{2,1,0:T(8,128)(2,1)}) custom-call(s32[6]{0:T(128)S(1)} %stack.23.place._, bf16[1,128,1024]{2,1,0:T(8,128)(2,1)S(1)} %copy-done.6, bf16[2,128,1024]{2,1,0:T(8,128)(2,1)S(1)} %collective-permute-done.11.two_hbm.n1.t1, ...), custom_call_target="tpu_custom_call" | custom-call | bytes 1024 | tf_op jit(solution)/shard_map/last_step/pallas_call | solution.py:68
  156.2 1.9 %collective-permute-done.39.rest_1_ = bf16[256,512]{1,0:T(8,128)(2,1)S(1)} collective-permute-done((bf16[256,512]{1,0:T(8,128)(2,1)S(1)}, bf16[256,512]{1,0:T(8,128)(2,1)S(1)}, u32[]{:S(2)}, u32[]{:S(2)}) %collective-permute-start.39) | collective-permute-done | bytes 262176 | tf_op jit(solution)/shard_map/ppermute | solution.py:38
  158.0 5.3 %last_step.3 = (f32[1,1024,1024]{2,1,0:T(8,128)}, bf16[1,1024,1024]{2,1,0:T(8,128)(2,1)}, bf16[1,1024,1024]{2,1,0:T(8,128)(2,1)}) custom-call(s32[6]{0:T(128)S(1)} %stack.23.place._, bf16[1,128,1024]{2,1,0:T(8,128)(2,1)S(1)} %copy-done.6, ...), custom_call_target="tpu_custom_call", output_to_operand_aliasing={{0}: (16, {}), {1}: (17, {}), {2}: (18, {})} | custom-call | bytes 1024 | tf_op jit(solution)/shard_map/last_step/pallas_call | solution.py:68
  (123 shorter events, 46.2 us)
Async XLA Ops:
  3.9 32.6 %all-to-all-start = ((bf16[8,128,1024]{2,1,0:T(8,128)(2,1)}), bf16[8,128,1024]{2,1,0:T(8,128)(2,1)S(1)}, u32[]{:S(2)}, u32[]{:S(2)}) async-start(bf16[8,128,1024]{2,1,0:T(8,128)(2,1)} %regroup_tokens.1), calls=%async_computation | async-start | bytes 4194304 | tf_op jit(solution)/shard_map/all_to_all | solution.py:567
  13.1 34.4 %collective-permute-start.4 = (bf16[2,128,1024]{2,1,0:T(8,128)(2,1)}, bf16[2,128,1024]{2,1,0:T(8,128)(2,1)S(1)}, u32[]{:S(2)}, u32[]{:S(2)}) collective-permute-start(bf16[2,128,1024]{2,1,0:T(8,128)(2,1)} %get-tuple-element.133), channel_id=1, source_target_pairs={{0,2},{1,3},{2,4},{3,5},{4,6},{5,7},{6,0},{7,1},{8,10},{9,11},{10,... | collective-permute-start | bytes 1572872 | tf_op jit(solution)/shard_map/ppermute | solution.py:38
  15.2 33.7 %collective-permute-start.5 = (bf16[2,128,1024]{2,1,0:T(8,128)(2,1)}, bf16[2,128,1024]{2,1,0:T(8,128)(2,1)S(1)}, u32[]{:S(2)}, u32[]{:S(2)}) collective-permute-start(bf16[2,128,1024]{2,1,0:T(8,128)(2,1)} %get-tuple-element.134), channel_id=1, source_target_pairs={{0,6},{1,7},{2,0},{3,1},{4,2},{5,3},{6,4},{7,5},{8,14},{9,15},{10,... | collective-permute-start | bytes 1572872 | tf_op jit(solution)/shard_map/ppermute | solution.py:38
  39.7 12.6 %collective-permute-start.6 = (bf16[256,512]{1,0:T(8,128)(2,1)S(1)}, bf16[256,512]{1,0:T(8,128)(2,1)S(1)}, u32[]{:S(2)}, u32[]{:S(2)}) collective-permute-start(bf16[256,512]{1,0:T(8,128)(2,1)S(1)} %get-tuple-element.137), channel_id=1, source_target_pairs={{0,2},{1,3},{2,4},{3,5},{4,6},{5,7},{6,0},{7,1},{8,10},{9,11},{10,... | collective-permute-start | bytes 786440 | tf_op jit(solution)/shard_map/ppermute | solution.py:38
  40.9 29.4 %collective-permute-start.11 = (bf16[2,128,1024]{2,1,0:T(8,128)(2,1)S(1)}, bf16[2,128,1024]{2,1,0:T(8,128)(2,1)S(1)}, u32[]{:S(2)}, u32[]{:S(2)}) collective-permute-start(bf16[2,128,1024]{2,1,0:T(8,128)(2,1)S(1)} %copy-done.19), channel_id=1, source_target_pairs={{0,1},{1,0},{2,3},{3,2},{4,5},{5,4},{6,7},{7,6},{8,9},{9,8},{10,11... | collective-permute-start | bytes 1572872 | tf_op jit(solution)/shard_map/ppermute | solution.py:34
  43.8 11.9 %collective-permute-start.7 = (bf16[256,512]{1,0:T(8,128)(2,1)S(1)}, bf16[256,512]{1,0:T(8,128)(2,1)S(1)}, u32[]{:S(2)}, u32[]{:S(2)}) collective-permute-start(bf16[256,512]{1,0:T(8,128)(2,1)S(1)} %get-tuple-element.140), channel_id=1, source_target_pairs={{0,6},{1,7},{2,0},{3,1},{4,2},{5,3},{6,4},{7,5},{8,14},{9,15},{10,... | collective-permute-start | bytes 786440 | tf_op jit(solution)/shard_map/ppermute | solution.py:38
  47.4 16.8 %collective-permute-start.10 = (bf16[256,512]{1,0:T(8,128)(2,1)S(1)}, bf16[256,512]{1,0:T(8,128)(2,1)S(1)}, u32[]{:S(2)}, u32[]{:S(2)}) collective-permute-start(bf16[256,512]{1,0:T(8,128)(2,1)S(1)} %get-tuple-element.148), channel_id=1, source_target_pairs={{0,6},{1,7},{2,0},{3,1},{4,2},{5,3},{6,4},{7,5},{8,14},{9,15},{10,... | collective-permute-start | bytes 786440 | tf_op jit(solution)/shard_map/ppermute | solution.py:38
  52.8 11.4 %collective-permute-start.9 = (bf16[256,512]{1,0:T(8,128)(2,1)S(1)}, bf16[256,512]{1,0:T(8,128)(2,1)S(1)}, u32[]{:S(2)}, u32[]{:S(2)}) collective-permute-start(bf16[256,512]{1,0:T(8,128)(2,1)S(1)} %add_keys.2), channel_id=1, source_target_pairs={{0,2},{1,3},{2,4},{3,5},{4,6},{5,7},{6,0},{7,1},{8,10},{9,11},{10,... | collective-permute-start | bytes 786440 | tf_op jit(solution)/shard_map/ppermute | solution.py:38
  55.7 15.2 %collective-permute-start.13 = (bf16[256,512]{1,0:T(8,128)(2,1)S(1)}, bf16[256,512]{1,0:T(8,128)(2,1)S(1)}, u32[]{:S(2)}, u32[]{:S(2)}) collective-permute-start(bf16[256,512]{1,0:T(8,128)(2,1)S(1)} %get-tuple-element.155), channel_id=1, source_target_pairs={{0,2},{1,3},{2,4},{3,5},{4,6},{5,7},{6,0},{7,1},{8,10},{9,11},{10,... | collective-permute-start | bytes 786440 | tf_op jit(solution)/shard_map/ppermute | solution.py:38
  61.3 9.7 %collective-permute-start.12 = (bf16[256,512]{1,0:T(8,128)(2,1)S(1)}, bf16[256,512]{1,0:T(8,128)(2,1)S(1)}, u32[]{:S(2)}, u32[]{:S(2)}) collective-permute-start(bf16[256,512]{1,0:T(8,128)(2,1)S(1)} %add_keys.3), channel_id=1, source_target_pairs={{0,6},{1,7},{2,0},{3,1},{4,2},{5,3},{6,4},{7,5},{8,14},{9,15},{10,... | collective-permute-start | bytes 786440 | tf_op jit(solution)/shard_map/ppermute | solution.py:38
  71.7 12.0 %collective-permute-start.18 = (bf16[256,512]{1,0:T(8,128)(2,1)S(1)}, bf16[256,512]{1,0:T(8,128)(2,1)S(1)}, u32[]{:S(2)}, u32[]{:S(2)}) collective-permute-start(bf16[256,512]{1,0:T(8,128)(2,1)S(1)} %sum_keys.5.half_ref), channel_id=1, source_target_pairs={{0,1},{1,0},{2,3},{3,2},{4,5},{5,4},{6,7},{7,6},{8,9},{9,8},{10,11... | collective-permute-start | bytes 786440 | tf_op jit(solution)/shard_map/ppermute | solution.py:34
  72.5 18.5 %collective-permute-start.20 = (bf16[2,128,1024]{2,1,0:T(8,128)(2,1)S(1)}, bf16[2,128,1024]{2,1,0:T(8,128)(2,1)S(1)}, u32[]{:S(2)}, u32[]{:S(2)}) collective-permute-start(bf16[2,128,1024]{2,1,0:T(8,128)(2,1)S(1)} %join_blocks.2), channel_id=1, source_target_pairs={{0,1},{1,0},{2,3},{3,2},{4,5},{5,4},{6,7},{7,6},{8,9},{9,8},{10,11... | collective-permute-start | bytes 1572872 | tf_op jit(solution)/shard_map/ppermute | solution.py:34
  73.8 20.9 %collective-permute-start.19 = (bf16[2,128,1024]{2,1,0:T(8,128)(2,1)S(1)}, bf16[2,128,1024]{2,1,0:T(8,128)(2,1)S(1)}, u32[]{:S(2)}, u32[]{:S(2)}) collective-permute-start(bf16[2,128,1024]{2,1,0:T(8,128)(2,1)S(1)} %join_blocks.3), channel_id=1, source_target_pairs={{0,4},{1,5},{2,6},{3,7},{4,0},{5,1},{6,2},{7,3},{8,12},{9,13},{10,... | collective-permute-start | bytes 1572872 | tf_op jit(solution)/shard_map/ppermute | solution.py:38
  74.4 16.6 %collective-permute-start.21 = (bf16[256,512]{1,0:T(8,128)(2,1)S(1)}, bf16[256,512]{1,0:T(8,128)(2,1)S(1)}, u32[]{:S(2)}, u32[]{:S(2)}) collective-permute-start(bf16[256,512]{1,0:T(8,128)(2,1)S(1)} %pair_resid.4.rest_0_), channel_id=1, source_target_pairs={{0,2},{1,3},{2,4},{3,5},{4,6},{5,7},{6,0},{7,1},{8,10},{9,11},{10,... | collective-permute-start | bytes 786440 | tf_op jit(solution)/shard_map/ppermute | solution.py:38
  85.2 10.7 %collective-permute-start.23 = (bf16[256,512]{1,0:T(8,128)(2,1)S(1)}, bf16[256,512]{1,0:T(8,128)(2,1)S(1)}, u32[]{:S(2)}, u32[]{:S(2)}) collective-permute-start(bf16[256,512]{1,0:T(8,128)(2,1)S(1)} %pair_resid.4.rest_0_), channel_id=1, source_target_pairs={{0,6},{1,7},{2,0},{3,1},{4,2},{5,3},{6,4},{7,5},{8,14},{9,15},{10,... | collective-permute-start | bytes 786440 | tf_op jit(solution)/shard_map/ppermute | solution.py:38
  91.0 10.4 %collective-permute-start.22 = (bf16[256,512]{1,0:T(8,128)(2,1)S(1)}, bf16[256,512]{1,0:T(8,128)(2,1)S(1)}, u32[]{:S(2)}, u32[]{:S(2)}) collective-permute-start(bf16[256,512]{1,0:T(8,128)(2,1)S(1)} %collective-permute-done.21.rest_1_), channel_id=1, source_target_pairs={{0,2},{1,3},{2,4},{3,5},{4,6},{5,7},{6,0},{7,1},{8,10},{9,11},{10,... | collective-permute-start | bytes 786440 | tf_op jit(solution)/shard_map/ppermute | solution.py:38
  91.0 16.9 %collective-permute-start.24 = (bf16[256,512]{1,0:T(8,128)(2,1)S(1)}, bf16[256,512]{1,0:T(8,128)(2,1)S(1)}, u32[]{:S(2)}, u32[]{:S(2)}) collective-permute-start(bf16[256,512]{1,0:T(8,128)(2,1)S(1)} %pair_resid.5.rest_0_), channel_id=1, source_target_pairs={{0,2},{1,3},{2,4},{3,5},{4,6},{5,7},{6,0},{7,1},{8,10},{9,11},{10,... | collective-permute-start | bytes 786440 | tf_op jit(solution)/shard_map/ppermute | solution.py:38
  92.0 15.8 %collective-permute-start.26 = (bf16[256,512]{1,0:T(8,128)(2,1)S(1)}, bf16[256,512]{1,0:T(8,128)(2,1)S(1)}, u32[]{:S(2)}, u32[]{:S(2)}) collective-permute-start(bf16[256,512]{1,0:T(8,128)(2,1)S(1)} %collective-permute-done.25.rest_3_), channel_id=1, source_target_pairs={{0,6},{1,7},{2,0},{3,1},{4,2},{5,3},{6,4},{7,5},{8,14},{9,15},{10,... | collective-permute-start | bytes 786440 | tf_op jit(solution)/shard_map/ppermute | solution.py:38
  105.8 9.3 %collective-permute-start.29 = (bf16[256,512]{1,0:T(8,128)(2,1)S(1)}, bf16[256,512]{1,0:T(8,128)(2,1)S(1)}, u32[]{:S(2)}, u32[]{:S(2)}) collective-permute-start(bf16[256,512]{1,0:T(8,128)(2,1)S(1)} %get-tuple-element.182), channel_id=1, source_target_pairs={{0,6},{1,7},{2,0},{3,1},{4,2},{5,3},{6,4},{7,5},{8,14},{9,15},{10,... | collective-permute-start | bytes 786440 | tf_op jit(solution)/shard_map/ppermute | solution.py:38
  105.8 14.8 %collective-permute-start.27 = (bf16[256,512]{1,0:T(8,128)(2,1)S(1)}, bf16[256,512]{1,0:T(8,128)(2,1)S(1)}, u32[]{:S(2)}, u32[]{:S(2)}) collective-permute-start(bf16[256,512]{1,0:T(8,128)(2,1)S(1)} %get-tuple-element.180), channel_id=1, source_target_pairs={{0,2},{1,3},{2,4},{3,5},{4,6},{5,7},{6,0},{7,1},{8,10},{9,11},{10,... | collective-permute-start | bytes 786440 | tf_op jit(solution)/shard_map/ppermute | solution.py:38
  107.9 12.8 %collective-permute-start.28 = (bf16[256,512]{1,0:T(8,128)(2,1)S(1)}, bf16[256,512]{1,0:T(8,128)(2,1)S(1)}, u32[]{:S(2)}, u32[]{:S(2)}) collective-permute-start(bf16[256,512]{1,0:T(8,128)(2,1)S(1)} %get-tuple-element.181), channel_id=1, source_target_pairs={{0,4},{1,5},{2,6},{3,7},{4,0},{5,1},{6,2},{7,3},{8,12},{9,13},{10,... | collective-permute-start | bytes 786440 | tf_op jit(solution)/shard_map/ppermute | solution.py:38
  112.3 14.1 %collective-permute-start.32 = (bf16[256,512]{1,0:T(8,128)(2,1)S(1)}, bf16[256,512]{1,0:T(8,128)(2,1)S(1)}, u32[]{:S(2)}, u32[]{:S(2)}) collective-permute-start(bf16[256,512]{1,0:T(8,128)(2,1)S(1)} %get-tuple-element.187), channel_id=1, source_target_pairs={{0,6},{1,7},{2,0},{3,1},{4,2},{5,3},{6,4},{7,5},{8,14},{9,15},{10,... | collective-permute-start | bytes 786440 | tf_op jit(solution)/shard_map/ppermute | solution.py:38
  115.0 15.4 %collective-permute-start.30 = (bf16[256,512]{1,0:T(8,128)(2,1)S(1)}, bf16[256,512]{1,0:T(8,128)(2,1)S(1)}, u32[]{:S(2)}, u32[]{:S(2)}) collective-permute-start(bf16[256,512]{1,0:T(8,128)(2,1)S(1)} %get-tuple-element.185), channel_id=1, source_target_pairs={{0,2},{1,3},{2,4},{3,5},{4,6},{5,7},{6,0},{7,1},{8,10},{9,11},{10,... | collective-permute-start | bytes 786440 | tf_op jit(solution)/shard_map/ppermute | solution.py:38
  115.1 15.3 %collective-permute-start.31 = (bf16[256,512]{1,0:T(8,128)(2,1)S(1)}, bf16[256,512]{1,0:T(8,128)(2,1)S(1)}, u32[]{:S(2)}, u32[]{:S(2)}) collective-permute-start(bf16[256,512]{1,0:T(8,128)(2,1)S(1)} %get-tuple-element.186), channel_id=1, source_target_pairs={{0,4},{1,5},{2,6},{3,7},{4,0},{5,1},{6,2},{7,3},{8,12},{9,13},{10,... | collective-permute-start | bytes 786440 | tf_op jit(solution)/shard_map/ppermute | solution.py:38
  121.3 11.0 %collective-permute-start.33 = (bf16[256,512]{1,0:T(8,128)(2,1)S(1)}, bf16[256,512]{1,0:T(8,128)(2,1)S(1)}, u32[]{:S(2)}, u32[]{:S(2)}) collective-permute-start(bf16[256,512]{1,0:T(8,128)(2,1)S(1)} %sum_keys.6.half_ref), channel_id=1, source_target_pairs={{0,1},{1,0},{2,3},{3,2},{4,5},{5,4},{6,7},{7,6},{8,9},{9,8},{10,11... | collective-permute-start | bytes 786440 | tf_op jit(solution)/shard_map/ppermute | solution.py:34
  122.5 17.3 %collective-permute-start.35 = (bf16[512,512]{1,0:T(8,128)(2,1)S(1)}, bf16[512,512]{1,0:T(8,128)(2,1)S(1)}, u32[]{:S(2)}, u32[]{:S(2)}) collective-permute-start(bf16[512,512]{1,0:T(8,128)(2,1)S(1)} %join_ring.1.same_ref), channel_id=1, source_target_pairs={{0,8},{8,0},{16,24},{24,16},{32,40},{40,32},{48,56},{56,48},{64,72... | collective-permute-start | bytes 1572872 | tf_op jit(solution)/shard_map/ppermute | solution.py:42
  132.9 10.9 %collective-permute-start.38 = (bf16[256,512]{1,0:T(8,128)(2,1)S(1)}, bf16[256,512]{1,0:T(8,128)(2,1)S(1)}, u32[]{:S(2)}, u32[]{:S(2)}) collective-permute-start(bf16[256,512]{1,0:T(8,128)(2,1)S(1)} %pair_resid.6.rest_0_), channel_id=1, source_target_pairs={{0,6},{1,7},{2,0},{3,1},{4,2},{5,3},{6,4},{7,5},{8,14},{9,15},{10,... | collective-permute-start | bytes 786440 | tf_op jit(solution)/shard_map/ppermute | solution.py:38
  134.4 11.1 %collective-permute-start.37 = (bf16[256,512]{1,0:T(8,128)(2,1)S(1)}, bf16[256,512]{1,0:T(8,128)(2,1)S(1)}, u32[]{:S(2)}, u32[]{:S(2)}) collective-permute-start(bf16[256,512]{1,0:T(8,128)(2,1)S(1)} %pair_resid.6.rest_0_), channel_id=1, source_target_pairs={{0,4},{1,5},{2,6},{3,7},{4,0},{5,1},{6,2},{7,3},{8,12},{9,13},{10,... | collective-permute-start | bytes 786440 | tf_op jit(solution)/shard_map/ppermute | solution.py:38
  135.1 16.1 %collective-permute-start.36 = (bf16[256,512]{1,0:T(8,128)(2,1)S(1)}, bf16[256,512]{1,0:T(8,128)(2,1)S(1)}, u32[]{:S(2)}, u32[]{:S(2)}) collective-permute-start(bf16[256,512]{1,0:T(8,128)(2,1)S(1)} %pair_resid.6.rest_0_), channel_id=1, source_target_pairs={{0,2},{1,3},{2,4},{3,5},{4,6},{5,7},{6,0},{7,1},{8,10},{9,11},{10,... | collective-permute-start | bytes 786440 | tf_op jit(solution)/shard_map/ppermute | solution.py:38
  138.7 17.5 %collective-permute-start.41 = (bf16[256,512]{1,0:T(8,128)(2,1)S(1)}, bf16[256,512]{1,0:T(8,128)(2,1)S(1)}, u32[]{:S(2)}, u32[]{:S(2)}) collective-permute-start(bf16[256,512]{1,0:T(8,128)(2,1)S(1)} %pair_resid.7.rest_0_), channel_id=1, source_target_pairs={{0,6},{1,7},{2,0},{3,1},{4,2},{5,3},{6,4},{7,5},{8,14},{9,15},{10,... | collective-permute-start | bytes 786440 | tf_op jit(solution)/shard_map/ppermute | solution.py:38
  139.8 16.3 %collective-permute-start.40 = (bf16[256,512]{1,0:T(8,128)(2,1)S(1)}, bf16[256,512]{1,0:T(8,128)(2,1)S(1)}, u32[]{:S(2)}, u32[]{:S(2)}) collective-permute-start(bf16[256,512]{1,0:T(8,128)(2,1)S(1)} %pair_resid.7.rest_0_), channel_id=1, source_target_pairs={{0,4},{1,5},{2,6},{3,7},{4,0},{5,1},{6,2},{7,3},{8,12},{9,13},{10,... | collective-permute-start | bytes 786440 | tf_op jit(solution)/shard_map/ppermute | solution.py:38
  143.8 14.2 %collective-permute-start.39 = (bf16[256,512]{1,0:T(8,128)(2,1)S(1)}, bf16[256,512]{1,0:T(8,128)(2,1)S(1)}, u32[]{:S(2)}, u32[]{:S(2)}) collective-permute-start(bf16[256,512]{1,0:T(8,128)(2,1)S(1)} %pair_resid.7.rest_0_), channel_id=1, source_target_pairs={{0,2},{1,3},{2,4},{3,5},{4,6},{5,7},{6,0},{7,1},{8,10},{9,11},{10,... | collective-permute-start | bytes 786440 | tf_op jit(solution)/shard_map/ppermute | solution.py:38
  (31 other events, 363.1 us)

commit v3 on v2

--- a/solution.py
+++ b/solution.py
@@ -23,11 +23,8 @@
 FSDP = 8
 REP = 16
 TILE = 256
-ORDER = (('sides', 'A', 'B', 'outer', 'A', 'pairs', 'B', 'A', 'ring', 'B', 'join'), ('A', 'B', 'A', 'B'))
-MODES = (
-    (("up", "up"), ("down", "down")),
-    (("direct", "direct"), ("direct", "direct")),
-)
+ORDER = (('far', 'sides', 'outer', 'A', 'B', 'A', 'pairs', 'B', 'ring', 'A', 'B', 'join'), ('A', 'B', 'A', 'B'))
+MODES = ((('up', 'direct'), ('down', 'direct')), (('direct', 'direct'), ('direct', 'direct')))
 
 
 def swap_x(value):
@@ -583,13 +580,15 @@
     resids = {}
 
     def advance(order):
-        nonlocal got, fresh, anchors, next_toks, opposite, sides
+        nonlocal got, fresh, anchors, next_toks, opposite, sides, far
         for name in order:
             if name in ("A", "B"):
                 chain = ("A", "B").index(name)
                 resids[chain] = next(steps[chain])
             elif name == "pairs":
                 opposite = shift_y(run(join_blocks, opposite, 0, far, 1), 2)
+            elif name == "far":
+                far = run.after(far)
             elif name == "sides":
                 sides = swap_x(run(join_blocks, up, 1, down, 1))
             elif name == "join":

time: 164 us -> 158 us (0.963)
  waiting for transfers between devices: 57.1 us -> 44.7 us
  starting transfers between devices: 59.8 us -> 63.5 us
  Pallas kernels: 39.5 us -> 42.5 us
    ppermute x27, waiting for transfers between devices: 36.8 us -> 27.8 us  [shift_y(): lax.ppermute(value, 'fsdp', [(i, (i + 2 * hops) % FSDP) for i in range(FS...]
    pallas_call x26, Pallas kernels: 39.5 us -> 42.5 us  [call(): pl.pallas_call(body, in_specs=[pl.BlockSpec(memory_space=pltpu.SMEM)] * (...]
    ppermute x6, starting transfers between devices: 11.5 us -> 14.3 us  [shift_z(): lax.ppermute(value, 'rep', [(i, (i + 4 * hops) % REP) for i in range(REP)])]
    ppermute x1, waiting for transfers between devices: 3.54 us -> 1.13 us  [swap_far(): return lax.ppermute(value, 'rep', [(i, i ^ 2) for i in range(REP)])]
    ppermute x6, waiting for transfers between devices: 11.1 us -> 9.31 us  [shift_z(): lax.ppermute(value, 'rep', [(i, (i + 4 * hops) % REP) for i in range(REP)])]
    unnamed x42 -> x40, local copies, waits for them, and re-layouts: 5.13 us -> 5.11 us
  transfers between devices with their start and end apart: 43 -> 43, of which waited for: 19 -> 20; matrix products, arithmetic and copies ran while one was open for 1% -> 1% of each run, Pallas kernels for 19% -> 22%
where the time goes in v3:
time: 158 us
  starting transfers between devices  63.5 us (40%)
  waiting for transfers between devices  44.7 us (28%)
  Pallas kernels  42.5 us (27%)
  local copies, waits for them, and re-layouts  5.19 us (3%)
  between operations  1.91 us (1%)
    pallas_call x26, Pallas kernels, call(): pl.pallas_call(body, in_specs=[pl.BlockSpec(memory_space=pltpu.SMEM)] * (...  42.5 us
    ppermute x27, starting transfers between devices, shift_y(): lax.ppermute(value, 'fsdp', [(i, (i + 2 * hops) % FSDP) for i in range(FS...  33.4 us
    ppermute x27, waiting for transfers between devices, shift_y(): lax.ppermute(value, 'fsdp', [(i, (i + 2 * hops) % FSDP) for i in range(FS...  27.8 us
    ppermute x6, starting transfers between devices, shift_z(): lax.ppermute(value, 'rep', [(i, (i + 4 * hops) % REP) for i in range(REP)])  14.3 us
    ppermute x6, waiting for transfers between devices, shift_z(): lax.ppermute(value, 'rep', [(i, (i + 4 * hops) % REP) for i in range(REP)])  9.31 us
    ppermute x6, starting transfers between devices, swap_x(): return lax.ppermute(value, 'fsdp', [(i, i ^ 1) for i in range(FSDP)])  7.47 us
    all_to_all x1, starting transfers between devices, on_device(): toks = lax.all_to_all(toks, 'fsdp', split_axis=0, concat_axis=0, tiled=True)  5.48 us
    unnamed x40, local copies, waits for them, and re-layouts  5.11 us
  transfers between devices with their start and end apart: 43, of which 20 were waited for; matrix products, arithmetic and copies ran while one was open for 1% of the time, Pallas kernels for 22%

profile of v3, /device:TPU:0, one launch (start us, length us, event | category | flops | bytes accessed | tf_op | source)
XLA Modules:
  0.0 157.8 jit_solution(7649093812768583514)
XLA Ops:
  1.3 2.4 %regroup_tokens.1 = bf16[8,128,1024]{2,1,0:T(8,128)(2,1)} custom-call(bf16[1,2,128,8192]{3,2,1,0:T(8,128)(2,1)} %src.3), custom_call_target="tpu_custom_call" | custom-call | bytes 1024 | tf_op jit(solution)/shard_map/regroup_tokens/pallas_call | solution.py:65
  3.9 5.5 %all-to-all-start = ((bf16[8,128,1024]{2,1,0:T(8,128)(2,1)}), bf16[8,128,1024]{2,1,0:T(8,128)(2,1)S(1)}, u32[]{:S(2)}, u32[]{:S(2)}) async-start(bf16[8,128,1024]{2,1,0:T(8,128)(2,1)} %regroup_tokens.1), calls=%async_computation | async-start | bytes 4194304 | tf_op jit(solution)/shard_map/all_to_all | solution.py:564
  9.3 3.0 %tokens_by_hops.1 = (bf16[2,128,1024]{2,1,0:T(8,128)(2,1)}, bf16[2,128,1024]{2,1,0:T(8,128)(2,1)}, bf16[2,128,1024]{2,1,0:T(8,128)(2,1)}, bf16[1,128,1024]{2,1,0:T(8,128)(2,1)}, bf16[1,128,1024]{2,1,0:T(8,128)(2,1)}) custom-call(s32[6]{0:T(128)S(1)} %stack.23.place._, bf16[1,2,128,8192]{3,2,1,0:T(8,128)(2,1)} %src.3), custom_call_target="tpu_custom_call" | custom-call | bytes 1024 | tf_op jit(solution)/shard_map/tokens_by_hops/pallas_call | solution.py:65
  13.1 2.1 %collective-permute-start.4 = (bf16[2,128,1024]{2,1,0:T(8,128)(2,1)}, bf16[2,128,1024]{2,1,0:T(8,128)(2,1)S(1)}, u32[]{:S(2)}, u32[]{:S(2)}) collective-permute-start(bf16[2,128,1024]{2,1,0:T(8,128)(2,1)} %get-tuple-element.135), channel_id=1, source_target_pairs={{0,1},{1,0},{2,3},{3,2},{4,5},{5,4},{6,7},{7,6},{8,9},{9,8},{10,11... | collective-permute-start | bytes 1572872 | tf_op jit(solution)/shard_map/ppermute | solution.py:31
  17.3 4.1 %collective-permute-start.3 = (bf16[128,512]{1,0:T(8,128)(2,1)S(1)}, bf16[128,512]{1,0:T(8,128)(2,1)S(1)}, u32[]{:S(2)}, u32[]{:S(2)}) collective-permute-start(bf16[128,512]{1,0:T(8,128)(2,1)S(1)} %get-tuple-element.123), channel_id=1, source_target_pairs={{0,96},{8,104},{16,112},{24,120},{32,0},{40,8},{48,16},{56,24},{64... | collective-permute-start | bytes 393224 | tf_op jit(solution)/shard_map/ppermute | solution.py:47
  24.2 2.3 %collective-permute-start.2 = (bf16[128,512]{1,0:T(8,128)(2,1)S(1)}, bf16[128,512]{1,0:T(8,128)(2,1)S(1)}, u32[]{:S(2)}, u32[]{:S(2)}) collective-permute-start(bf16[128,512]{1,0:T(8,128)(2,1)S(1)} %get-tuple-element.122), channel_id=1, source_target_pairs={{0,64},{8,72},{16,80},{24,88},{32,96},{40,104},{48,112},{56,120},{... | collective-permute-start | bytes 393224 | tf_op jit(solution)/shard_map/ppermute | solution.py:47
  28.3 3.7 %collective-permute-done.1.g1 = bf16[128,512]{1,0:T(8,128)(2,1)S(1)} collective-permute-done((bf16[128,512]{1,0:T(8,128)(2,1)S(1)}, bf16[128,512]{1,0:T(8,128)(2,1)S(1)}, u32[]{:S(2)}, u32[]{:S(2)}) %collective-permute-start.1) | collective-permute-done | bytes 131104 | tf_op jit(solution)/shard_map/ppermute | solution.py:47
  34.0 3.9 %all-to-all-done = bf16[8,128,1024]{2,1,0:T(8,128)(2,1)S(1)} async-done(((bf16[8,128,1024]{2,1,0:T(8,128)(2,1)}), bf16[8,128,1024]{2,1,0:T(8,128)(2,1)S(1)}, u32[]{:S(2)}, u32[]{:S(2)}) %all-to-all-start) | async-done | bytes 2097184 | tf_op jit(solution)/shard_map/all_to_all | solution.py:564
  39.2 1.8 %first_keys.2 = (f32[256,512]{1,0:T(8,128)S(1)}, f32[256,512]{1,0:T(8,128)S(1)}, bf16[256,512]{1,0:T(8,128)(2,1)S(1)}, bf16[256,512]{1,0:T(8,128)(2,1)S(1)}) custom-call(s32[6]{0:T(128)S(1)} %stack.23.place._, bf16[1024,1024]{1,0:T(8,128)(2,1)S(1)} %bitcast.7, bf16[1024,512]{1,0:T(8,128)(2,1)S(1)} %copy-done.10), custom_call_target="tpu_custom_call" | custom-call | bytes 1024 | tf_op jit(solution)/shard_map/first_keys/pallas_call | solution.py:65
  41.4 1.8 %first_keys.3 = (f32[256,512]{1,0:T(8,128)S(1)}, bf16[256,512]{1,0:T(8,128)(2,1)S(1)}, bf16[256,512]{1,0:T(8,128)(2,1)S(1)}, f32[256,512]{1,0:T(8,128)S(1)}) custom-call(s32[6]{0:T(128)S(1)} %stack.23.place._, bf16[1024,1024]{1,0:T(8,128)(2,1)S(1)} %bitcast.8, bf16[1024,512]{1,0:T(8,128)(2,1)S(1)} %copy-done.8), custom_call_target="tpu_custom_call" | custom-call | bytes 1024 | tf_op jit(solution)/shard_map/first_keys/pallas_call | solution.py:65
  43.2 3.1 %collective-permute-start.9 = (bf16[256,512]{1,0:T(8,128)(2,1)S(1)}, bf16[256,512]{1,0:T(8,128)(2,1)S(1)}, u32[]{:S(2)}, u32[]{:S(2)}) collective-permute-start(bf16[256,512]{1,0:T(8,128)(2,1)S(1)} %get-tuple-element.148), channel_id=1, source_target_pairs={{0,6},{1,7},{2,0},{3,1},{4,2},{5,3},{6,4},{7,5},{8,14},{9,15},{10,... | collective-permute-start | bytes 786440 | tf_op jit(solution)/shard_map/ppermute | solution.py:35
  46.5 2.7 %collective-permute-start.7 = (bf16[192,512]{1,0:T(8,128)(2,1)S(1)}, bf16[192,512]{1,0:T(8,128)(2,1)S(1)}, u32[]{:S(2)}, u32[]{:S(2)}) collective-permute-start(bf16[192,512]{1,0:T(8,128)(2,1)S(1)} %copy-done.18), channel_id=1, source_target_pairs={{0,16},{8,24},{16,0},{24,8},{32,48},{40,56},{48,32},{56,40},{64,80... | collective-permute-start | bytes 589832 | tf_op jit(solution)/shard_map/ppermute | solution.py:43
  49.2 1.8 %collective-permute-start.11 = (bf16[256,512]{1,0:T(8,128)(2,1)S(1)}, bf16[256,512]{1,0:T(8,128)(2,1)S(1)}, u32[]{:S(2)}, u32[]{:S(2)}) collective-permute-start(bf16[256,512]{1,0:T(8,128)(2,1)S(1)} %get-tuple-element.152), channel_id=1, source_target_pairs={{0,6},{1,7},{2,0},{3,1},{4,2},{5,3},{6,4},{7,5},{8,14},{9,15},{10,... | collective-permute-start | bytes 786440 | tf_op jit(solution)/shard_map/ppermute | solution.py:35
  55.5 2.1 %collective-permute-start.13 = (bf16[256,512]{1,0:T(8,128)(2,1)S(1)}, bf16[256,512]{1,0:T(8,128)(2,1)S(1)}, u32[]{:S(2)}, u32[]{:S(2)}) collective-permute-start(bf16[256,512]{1,0:T(8,128)(2,1)S(1)} %get-tuple-element.159), channel_id=1, source_target_pairs={{0,2},{1,3},{2,4},{3,5},{4,6},{5,7},{6,0},{7,1},{8,10},{9,11},{10,... | collective-permute-start | bytes 786440 | tf_op jit(solution)/shard_map/ppermute | solution.py:35
  60.0 4.0 %collective-permute-start.16 = (bf16[128,512]{1,0:T(8,128)(2,1)S(1)}, bf16[128,512]{1,0:T(8,128)(2,1)S(1)}, u32[]{:S(2)}, u32[]{:S(2)}) collective-permute-start(bf16[128,512]{1,0:T(8,128)(2,1)S(1)} %get-tuple-element.161.p0), channel_id=1, source_target_pairs={{0,96},{8,104},{16,112},{24,120},{32,0},{40,8},{48,16},{56,24},{64... | collective-permute-start | bytes 393224 | tf_op jit(solution)/shard_map/ppermute | solution.py:47
  64.9 1.9 %collective-permute-start.14 = (bf16[128,512]{1,0:T(8,128)(2,1)S(1)}, bf16[128,512]{1,0:T(8,128)(2,1)S(1)}, u32[]{:S(2)}, u32[]{:S(2)}) collective-permute-start(bf16[128,512]{1,0:T(8,128)(2,1)S(1)} %get-tuple-element.161.p0), channel_id=1, source_target_pairs={{0,32},{8,40},{16,48},{24,56},{32,64},{40,72},{48,80},{56,88},{64,... | collective-permute-start | bytes 393224 | tf_op jit(solution)/shard_map/ppermute | solution.py:47
  70.4 2.0 %collective-permute-start.18 = (bf16[256,512]{1,0:T(8,128)(2,1)S(1)}, bf16[256,512]{1,0:T(8,128)(2,1)S(1)}, u32[]{:S(2)}, u32[]{:S(2)}) collective-permute-start(bf16[256,512]{1,0:T(8,128)(2,1)S(1)} %sum_keys.5.half_ref), channel_id=1, source_target_pairs={{0,1},{1,0},{2,3},{3,2},{4,5},{5,4},{6,7},{7,6},{8,9},{9,8},{10,11... | collective-permute-start | bytes 786440 | tf_op jit(solution)/shard_map/ppermute | solution.py:31
  72.4 1.9 %collective-permute-start.15 = (bf16[128,512]{1,0:T(8,128)(2,1)S(1)}, bf16[128,512]{1,0:T(8,128)(2,1)S(1)}, u32[]{:S(2)}, u32[]{:S(2)}) collective-permute-start(bf16[128,512]{1,0:T(8,128)(2,1)S(1)} %collective-permute-done.14.p1), channel_id=1, source_target_pairs={{0,32},{8,40},{16,48},{24,56},{32,64},{40,72},{48,80},{56,88},{64,... | collective-permute-start | bytes 393224 | tf_op jit(solution)/shard_map/ppermute | solution.py:47
  74.3 4.6 %collective-permute-done.15.p2 = bf16[128,512]{1,0:T(8,128)(2,1)S(1)} collective-permute-done((bf16[128,512]{1,0:T(8,128)(2,1)S(1)}, bf16[128,512]{1,0:T(8,128)(2,1)S(1)}, u32[]{:S(2)}, u32[]{:S(2)}) %collective-permute-start.15) | collective-permute-done | bytes 131104 | tf_op jit(solution)/shard_map/ppermute | solution.py:47
  84.3 2.2 %collective-permute-start.26 = (bf16[256,512]{1,0:T(8,128)(2,1)S(1)}, bf16[256,512]{1,0:T(8,128)(2,1)S(1)}, u32[]{:S(2)}, u32[]{:S(2)}) collective-permute-start(bf16[256,512]{1,0:T(8,128)(2,1)S(1)} %pair_resid.5.rest_0_), channel_id=1, source_target_pairs={{0,6},{1,7},{2,0},{3,1},{4,2},{5,3},{6,4},{7,5},{8,14},{9,15},{10,... | collective-permute-start | bytes 786440 | tf_op jit(solution)/shard_map/ppermute | solution.py:35
  87.3 2.1 %collective-permute-done.23.rest_3_ = bf16[256,512]{1,0:T(8,128)(2,1)S(1)} collective-permute-done((bf16[256,512]{1,0:T(8,128)(2,1)S(1)}, bf16[256,512]{1,0:T(8,128)(2,1)S(1)}, u32[]{:S(2)}, u32[]{:S(2)}) %collective-permute-start.23) | collective-permute-done | bytes 262176 | tf_op jit(solution)/shard_map/ppermute | solution.py:35
  91.5 6.4 %collective-permute-done.21.rest_1_ = bf16[256,512]{1,0:T(8,128)(2,1)S(1)} collective-permute-done((bf16[256,512]{1,0:T(8,128)(2,1)S(1)}, bf16[256,512]{1,0:T(8,128)(2,1)S(1)}, u32[]{:S(2)}, u32[]{:S(2)}) %collective-permute-start.21) | collective-permute-done | bytes 262176 | tf_op jit(solution)/shard_map/ppermute | solution.py:35
  98.0 4.9 %middle_step.2 = (f32[1024,512]{1,0:T(8,128)S(1)}, bf16[1024,512]{1,0:T(8,128)(2,1)S(1)}, bf16[1024,512]{1,0:T(8,128)(2,1)S(1)}, f32[256,512]{1,0:T(8,128)S(1)},...) custom-call(s32[6]{0:T(128)S(1)} %stack.23.place._, ...), custom_call_target="tpu_custom_call" | custom-call | bytes 1024 | tf_op jit(solution)/shard_map/middle_step/pallas_call | solution.py:65
  103.0 2.0 %collective-permute-start.27 = (bf16[256,512]{1,0:T(8,128)(2,1)S(1)}, bf16[256,512]{1,0:T(8,128)(2,1)S(1)}, u32[]{:S(2)}, u32[]{:S(2)}) collective-permute-start(bf16[256,512]{1,0:T(8,128)(2,1)S(1)} %get-tuple-element.184), channel_id=1, source_target_pairs={{0,2},{1,3},{2,4},{3,5},{4,6},{5,7},{6,0},{7,1},{8,10},{9,11},{10,... | collective-permute-start | bytes 786440 | tf_op jit(solution)/shard_map/ppermute | solution.py:35
  105.5 3.0 %collective-permute-done.24.rest_1_ = bf16[256,512]{1,0:T(8,128)(2,1)S(1)} collective-permute-done((bf16[256,512]{1,0:T(8,128)(2,1)S(1)}, bf16[256,512]{1,0:T(8,128)(2,1)S(1)}, u32[]{:S(2)}, u32[]{:S(2)}) %collective-permute-start.24) | collective-permute-done | bytes 262176 | tf_op jit(solution)/shard_map/ppermute | solution.py:35
  108.5 4.9 %middle_step.3 = (f32[1024,512]{1,0:T(8,128)S(1)}, bf16[1024,512]{1,0:T(8,128)(2,1)S(1)}, bf16[1024,512]{1,0:T(8,128)(2,1)S(1)}, f32[256,512]{1,0:T(8,128)S(1)},...) custom-call(s32[6]{0:T(128)S(1)} %stack.23.place._, ...), custom_call_target="tpu_custom_call" | custom-call | bytes 1024 | tf_op jit(solution)/shard_map/middle_step/pallas_call | solution.py:65
  116.7 2.9 %collective-permute-done.28.refs_1_ = bf16[256,512]{1,0:T(8,128)(2,1)S(1)} collective-permute-done((bf16[256,512]{1,0:T(8,128)(2,1)S(1)}, bf16[256,512]{1,0:T(8,128)(2,1)S(1)}, u32[]{:S(2)}, u32[]{:S(2)}) %collective-permute-start.28) | collective-permute-done | bytes 262176 | tf_op jit(solution)/shard_map/ppermute | solution.py:35
  122.7 2.8 %collective-permute-done.31.refs_1_ = bf16[256,512]{1,0:T(8,128)(2,1)S(1)} collective-permute-done((bf16[256,512]{1,0:T(8,128)(2,1)S(1)}, bf16[256,512]{1,0:T(8,128)(2,1)S(1)}, u32[]{:S(2)}, u32[]{:S(2)}) %collective-permute-start.31) | collective-permute-done | bytes 262176 | tf_op jit(solution)/shard_map/ppermute | solution.py:35
  136.3 2.0 %collective-permute-done.38.rest_3_ = bf16[256,512]{1,0:T(8,128)(2,1)S(1)} collective-permute-done((bf16[256,512]{1,0:T(8,128)(2,1)S(1)}, bf16[256,512]{1,0:T(8,128)(2,1)S(1)}, u32[]{:S(2)}, u32[]{:S(2)}) %collective-permute-start.38) | collective-permute-done | bytes 262176 | tf_op jit(solution)/shard_map/ppermute | solution.py:35
  140.7 5.4 %collective-permute-done.36.rest_1_ = bf16[256,512]{1,0:T(8,128)(2,1)S(1)} collective-permute-done((bf16[256,512]{1,0:T(8,128)(2,1)S(1)}, bf16[256,512]{1,0:T(8,128)(2,1)S(1)}, u32[]{:S(2)}, u32[]{:S(2)}) %collective-permute-start.36) | collective-permute-done | bytes 262176 | tf_op jit(solution)/shard_map/ppermute | solution.py:35
  146.1 5.5 %last_step.2 = (f32[1,1024,1024]{2,1,0:T(8,128)}, bf16[1,1024,1024]{2,1,0:T(8,128)(2,1)}, bf16[1,1024,1024]{2,1,0:T(8,128)(2,1)}) custom-call(s32[6]{0:T(128)S(1)} %stack.23.place._, bf16[1,128,1024]{2,1,0:T(8,128)(2,1)S(1)} %copy-done.6, bf16[2,128,1024]{2,1,0:T(8,128)(2,1)S(1)} %collective-permute-done.4.two_hbm.n1.t1, ...), custom_call_target="tpu_custom_call" | custom-call | bytes 1024 | tf_op jit(solution)/shard_map/last_step/pallas_call | solution.py:65
  151.7 5.9 %last_step.3 = (f32[1,1024,1024]{2,1,0:T(8,128)}, bf16[1,1024,1024]{2,1,0:T(8,128)(2,1)}, bf16[1,1024,1024]{2,1,0:T(8,128)(2,1)}) custom-call(s32[6]{0:T(128)S(1)} %stack.23.place._, bf16[1,128,1024]{2,1,0:T(8,128)(2,1)S(1)} %copy-done.6, ...), custom_call_target="tpu_custom_call", output_to_operand_aliasing={{0}: (16, {}), {1}: (17, {}), {2}: (18, {})} | custom-call | bytes 1024 | tf_op jit(solution)/shard_map/last_step/pallas_call | solution.py:65
  (121 shorter events, 51.0 us)
Async XLA Ops:
  3.9 34.1 %all-to-all-start = ((bf16[8,128,1024]{2,1,0:T(8,128)(2,1)}), bf16[8,128,1024]{2,1,0:T(8,128)(2,1)S(1)}, u32[]{:S(2)}, u32[]{:S(2)}) async-start(bf16[8,128,1024]{2,1,0:T(8,128)(2,1)} %regroup_tokens.1), calls=%async_computation | async-start | bytes 4194304 | tf_op jit(solution)/shard_map/all_to_all | solution.py:564
  13.1 33.4 %collective-permute-start.4 = (bf16[2,128,1024]{2,1,0:T(8,128)(2,1)}, bf16[2,128,1024]{2,1,0:T(8,128)(2,1)S(1)}, u32[]{:S(2)}, u32[]{:S(2)}) collective-permute-start(bf16[2,128,1024]{2,1,0:T(8,128)(2,1)} %get-tuple-element.135), channel_id=1, source_target_pairs={{0,1},{1,0},{2,3},{3,2},{4,5},{5,4},{6,7},{7,6},{8,9},{9,8},{10,11... | collective-permute-start | bytes 1572872 | tf_op jit(solution)/shard_map/ppermute | solution.py:31
  15.2 34.0 %collective-permute-start.5 = (bf16[2,128,1024]{2,1,0:T(8,128)(2,1)}, bf16[2,128,1024]{2,1,0:T(8,128)(2,1)S(1)}, u32[]{:S(2)}, u32[]{:S(2)}) collective-permute-start(bf16[2,128,1024]{2,1,0:T(8,128)(2,1)} %get-tuple-element.137), channel_id=1, source_target_pairs={{0,2},{1,3},{2,4},{3,5},{4,6},{5,7},{6,0},{7,1},{8,10},{9,11},{10,... | collective-permute-start | bytes 1572872 | tf_op jit(solution)/shard_map/ppermute | solution.py:35
  21.4 29.6 %collective-permute-start.6 = (bf16[2,128,1024]{2,1,0:T(8,128)(2,1)}, bf16[2,128,1024]{2,1,0:T(8,128)(2,1)}, u32[]{:S(2)}, u32[]{:S(2)}) collective-permute-start(bf16[2,128,1024]{2,1,0:T(8,128)(2,1)} %get-tuple-element.138), channel_id=1, source_target_pairs={{0,6},{1,7},{2,0},{3,1},{4,2},{5,3},{6,4},{7,5},{8,14},{9,15},{10,... | collective-permute-start | bytes 1572872 | tf_op jit(solution)/shard_map/ppermute | solution.py:35
  41.1 13.3 %collective-permute-start.8 = (bf16[256,512]{1,0:T(8,128)(2,1)S(1)}, bf16[256,512]{1,0:T(8,128)(2,1)S(1)}, u32[]{:S(2)}, u32[]{:S(2)}) collective-permute-start(bf16[256,512]{1,0:T(8,128)(2,1)S(1)} %get-tuple-element.145), channel_id=1, source_target_pairs={{0,2},{1,3},{2,4},{3,5},{4,6},{5,7},{6,0},{7,1},{8,10},{9,11},{10,... | collective-permute-start | bytes 786440 | tf_op jit(solution)/shard_map/ppermute | solution.py:35
  43.2 14.3 %collective-permute-start.9 = (bf16[256,512]{1,0:T(8,128)(2,1)S(1)}, bf16[256,512]{1,0:T(8,128)(2,1)S(1)}, u32[]{:S(2)}, u32[]{:S(2)}) collective-permute-start(bf16[256,512]{1,0:T(8,128)(2,1)S(1)} %get-tuple-element.148), channel_id=1, source_target_pairs={{0,6},{1,7},{2,0},{3,1},{4,2},{5,3},{6,4},{7,5},{8,14},{9,15},{10,... | collective-permute-start | bytes 786440 | tf_op jit(solution)/shard_map/ppermute | solution.py:35
  49.2 10.7 %collective-permute-start.11 = (bf16[256,512]{1,0:T(8,128)(2,1)S(1)}, bf16[256,512]{1,0:T(8,128)(2,1)S(1)}, u32[]{:S(2)}, u32[]{:S(2)}) collective-permute-start(bf16[256,512]{1,0:T(8,128)(2,1)S(1)} %get-tuple-element.152), channel_id=1, source_target_pairs={{0,6},{1,7},{2,0},{3,1},{4,2},{5,3},{6,4},{7,5},{8,14},{9,15},{10,... | collective-permute-start | bytes 786440 | tf_op jit(solution)/shard_map/ppermute | solution.py:35
  55.0 9.9 %collective-permute-start.10 = (bf16[256,512]{1,0:T(8,128)(2,1)S(1)}, bf16[256,512]{1,0:T(8,128)(2,1)S(1)}, u32[]{:S(2)}, u32[]{:S(2)}) collective-permute-start(bf16[256,512]{1,0:T(8,128)(2,1)S(1)} %add_keys.2), channel_id=1, source_target_pairs={{0,2},{1,3},{2,4},{3,5},{4,6},{5,7},{6,0},{7,1},{8,10},{9,11},{10,... | collective-permute-start | bytes 786440 | tf_op jit(solution)/shard_map/ppermute | solution.py:35
  55.5 12.6 %collective-permute-start.13 = (bf16[256,512]{1,0:T(8,128)(2,1)S(1)}, bf16[256,512]{1,0:T(8,128)(2,1)S(1)}, u32[]{:S(2)}, u32[]{:S(2)}) collective-permute-start(bf16[256,512]{1,0:T(8,128)(2,1)S(1)} %get-tuple-element.159), channel_id=1, source_target_pairs={{0,2},{1,3},{2,4},{3,5},{4,6},{5,7},{6,0},{7,1},{8,10},{9,11},{10,... | collective-permute-start | bytes 786440 | tf_op jit(solution)/shard_map/ppermute | solution.py:35
  58.2 10.8 %collective-permute-start.12 = (bf16[256,512]{1,0:T(8,128)(2,1)S(1)}, bf16[256,512]{1,0:T(8,128)(2,1)S(1)}, u32[]{:S(2)}, u32[]{:S(2)}) collective-permute-start(bf16[256,512]{1,0:T(8,128)(2,1)S(1)} %add_keys.3), channel_id=1, source_target_pairs={{0,6},{1,7},{2,0},{3,1},{4,2},{5,3},{6,4},{7,5},{8,14},{9,15},{10,... | collective-permute-start | bytes 786440 | tf_op jit(solution)/shard_map/ppermute | solution.py:35
  59.4 25.0 %collective-permute-start.20 = (bf16[2,128,1024]{2,1,0:T(8,128)(2,1)S(1)}, bf16[2,128,1024]{2,1,0:T(8,128)(2,1)S(1)}, u32[]{:S(2)}, u32[]{:S(2)}) collective-permute-start(bf16[2,128,1024]{2,1,0:T(8,128)(2,1)S(1)} %join_blocks.2), channel_id=1, source_target_pairs={{0,1},{1,0},{2,3},{3,2},{4,5},{5,4},{6,7},{7,6},{8,9},{9,8},{10,11... | collective-permute-start | bytes 1572872 | tf_op jit(solution)/shard_map/ppermute | solution.py:31
  60.0 10.4 %collective-permute-start.16 = (bf16[128,512]{1,0:T(8,128)(2,1)S(1)}, bf16[128,512]{1,0:T(8,128)(2,1)S(1)}, u32[]{:S(2)}, u32[]{:S(2)}) collective-permute-start(bf16[128,512]{1,0:T(8,128)(2,1)S(1)} %get-tuple-element.161.p0), channel_id=1, source_target_pairs={{0,96},{8,104},{16,112},{24,120},{32,0},{40,8},{48,16},{56,24},{64... | collective-permute-start | bytes 393224 | tf_op jit(solution)/shard_map/ppermute | solution.py:47
  68.1 11.4 %collective-permute-start.17 = (bf16[256,512]{1,0:T(8,128)(2,1)S(1)}, bf16[256,512]{1,0:T(8,128)(2,1)S(1)}, u32[]{:S(2)}, u32[]{:S(2)}) collective-permute-start(bf16[256,512]{1,0:T(8,128)(2,1)S(1)} %sum_keys.4.half_ref), channel_id=1, source_target_pairs={{0,1},{1,0},{2,3},{3,2},{4,5},{5,4},{6,7},{7,6},{8,9},{9,8},{10,11... | collective-permute-start | bytes 786440 | tf_op jit(solution)/shard_map/ppermute | solution.py:31
  69.0 17.5 %collective-permute-start.19 = (bf16[2,128,1024]{2,1,0:T(8,128)(2,1)S(1)}, bf16[2,128,1024]{2,1,0:T(8,128)(2,1)S(1)}, u32[]{:S(2)}, u32[]{:S(2)}) collective-permute-start(bf16[2,128,1024]{2,1,0:T(8,128)(2,1)S(1)} %join_blocks.3), channel_id=1, source_target_pairs={{0,4},{1,5},{2,6},{3,7},{4,0},{5,1},{6,2},{7,3},{8,12},{9,13},{10,... | collective-permute-start | bytes 1572872 | tf_op jit(solution)/shard_map/ppermute | solution.py:35
  70.4 12.0 %collective-permute-start.18 = (bf16[256,512]{1,0:T(8,128)(2,1)S(1)}, bf16[256,512]{1,0:T(8,128)(2,1)S(1)}, u32[]{:S(2)}, u32[]{:S(2)}) collective-permute-start(bf16[256,512]{1,0:T(8,128)(2,1)S(1)} %sum_keys.5.half_ref), channel_id=1, source_target_pairs={{0,1},{1,0},{2,3},{3,2},{4,5},{5,4},{6,7},{7,6},{8,9},{9,8},{10,11... | collective-permute-start | bytes 786440 | tf_op jit(solution)/shard_map/ppermute | solution.py:31
  80.1 9.3 %collective-permute-start.23 = (bf16[256,512]{1,0:T(8,128)(2,1)S(1)}, bf16[256,512]{1,0:T(8,128)(2,1)S(1)}, u32[]{:S(2)}, u32[]{:S(2)}) collective-permute-start(bf16[256,512]{1,0:T(8,128)(2,1)S(1)} %pair_resid.4.rest_0_), channel_id=1, source_target_pairs={{0,6},{1,7},{2,0},{3,1},{4,2},{5,3},{6,4},{7,5},{8,14},{9,15},{10,... | collective-permute-start | bytes 786440 | tf_op jit(solution)/shard_map/ppermute | solution.py:35
  80.7 10.8 %collective-permute-start.22 = (bf16[256,512]{1,0:T(8,128)(2,1)S(1)}, bf16[256,512]{1,0:T(8,128)(2,1)S(1)}, u32[]{:S(2)}, u32[]{:S(2)}) collective-permute-start(bf16[256,512]{1,0:T(8,128)(2,1)S(1)} %pair_resid.4.rest_0_), channel_id=1, source_target_pairs={{0,4},{1,5},{2,6},{3,7},{4,0},{5,1},{6,2},{7,3},{8,12},{9,13},{10,... | collective-permute-start | bytes 786440 | tf_op jit(solution)/shard_map/ppermute | solution.py:35
  82.4 15.6 %collective-permute-start.21 = (bf16[256,512]{1,0:T(8,128)(2,1)S(1)}, bf16[256,512]{1,0:T(8,128)(2,1)S(1)}, u32[]{:S(2)}, u32[]{:S(2)}) collective-permute-start(bf16[256,512]{1,0:T(8,128)(2,1)S(1)} %pair_resid.4.rest_0_), channel_id=1, source_target_pairs={{0,2},{1,3},{2,4},{3,5},{4,6},{5,7},{6,0},{7,1},{8,10},{9,11},{10,... | collective-permute-start | bytes 786440 | tf_op jit(solution)/shard_map/ppermute | solution.py:35
  84.3 20.7 %collective-permute-start.26 = (bf16[256,512]{1,0:T(8,128)(2,1)S(1)}, bf16[256,512]{1,0:T(8,128)(2,1)S(1)}, u32[]{:S(2)}, u32[]{:S(2)}) collective-permute-start(bf16[256,512]{1,0:T(8,128)(2,1)S(1)} %pair_resid.5.rest_0_), channel_id=1, source_target_pairs={{0,6},{1,7},{2,0},{3,1},{4,2},{5,3},{6,4},{7,5},{8,14},{9,15},{10,... | collective-permute-start | bytes 786440 | tf_op jit(solution)/shard_map/ppermute | solution.py:35
  86.5 19.0 %collective-permute-start.25 = (bf16[256,512]{1,0:T(8,128)(2,1)S(1)}, bf16[256,512]{1,0:T(8,128)(2,1)S(1)}, u32[]{:S(2)}, u32[]{:S(2)}) collective-permute-start(bf16[256,512]{1,0:T(8,128)(2,1)S(1)} %pair_resid.5.rest_0_), channel_id=1, source_target_pairs={{0,4},{1,5},{2,6},{3,7},{4,0},{5,1},{6,2},{7,3},{8,12},{9,13},{10,... | collective-permute-start | bytes 786440 | tf_op jit(solution)/shard_map/ppermute | solution.py:35
  89.4 19.1 %collective-permute-start.24 = (bf16[256,512]{1,0:T(8,128)(2,1)S(1)}, bf16[256,512]{1,0:T(8,128)(2,1)S(1)}, u32[]{:S(2)}, u32[]{:S(2)}) collective-permute-start(bf16[256,512]{1,0:T(8,128)(2,1)S(1)} %pair_resid.5.rest_0_), channel_id=1, source_target_pairs={{0,2},{1,3},{2,4},{3,5},{4,6},{5,7},{6,0},{7,1},{8,10},{9,11},{10,... | collective-permute-start | bytes 786440 | tf_op jit(solution)/shard_map/ppermute | solution.py:35
  102.9 12.7 %collective-permute-start.29 = (bf16[256,512]{1,0:T(8,128)(2,1)S(1)}, bf16[256,512]{1,0:T(8,128)(2,1)S(1)}, u32[]{:S(2)}, u32[]{:S(2)}) collective-permute-start(bf16[256,512]{1,0:T(8,128)(2,1)S(1)} %get-tuple-element.186), channel_id=1, source_target_pairs={{0,6},{1,7},{2,0},{3,1},{4,2},{5,3},{6,4},{7,5},{8,14},{9,15},{10,... | collective-permute-start | bytes 786440 | tf_op jit(solution)/shard_map/ppermute | solution.py:35
  103.0 13.7 %collective-permute-start.27 = (bf16[256,512]{1,0:T(8,128)(2,1)S(1)}, bf16[256,512]{1,0:T(8,128)(2,1)S(1)}, u32[]{:S(2)}, u32[]{:S(2)}) collective-permute-start(bf16[256,512]{1,0:T(8,128)(2,1)S(1)} %get-tuple-element.184), channel_id=1, source_target_pairs={{0,2},{1,3},{2,4},{3,5},{4,6},{5,7},{6,0},{7,1},{8,10},{9,11},{10,... | collective-permute-start | bytes 786440 | tf_op jit(solution)/shard_map/ppermute | solution.py:35
  105.0 14.6 %collective-permute-start.28 = (bf16[256,512]{1,0:T(8,128)(2,1)S(1)}, bf16[256,512]{1,0:T(8,128)(2,1)S(1)}, u32[]{:S(2)}, u32[]{:S(2)}) collective-permute-start(bf16[256,512]{1,0:T(8,128)(2,1)S(1)} %get-tuple-element.185), channel_id=1, source_target_pairs={{0,4},{1,5},{2,6},{3,7},{4,0},{5,1},{6,2},{7,3},{8,12},{9,13},{10,... | collective-permute-start | bytes 786440 | tf_op jit(solution)/shard_map/ppermute | solution.py:35
  115.5 9.9 %collective-permute-start.31 = (bf16[256,512]{1,0:T(8,128)(2,1)S(1)}, bf16[256,512]{1,0:T(8,128)(2,1)S(1)}, u32[]{:S(2)}, u32[]{:S(2)}) collective-permute-start(bf16[256,512]{1,0:T(8,128)(2,1)S(1)} %get-tuple-element.190), channel_id=1, source_target_pairs={{0,4},{1,5},{2,6},{3,7},{4,0},{5,1},{6,2},{7,3},{8,12},{9,13},{10,... | collective-permute-start | bytes 786440 | tf_op jit(solution)/shard_map/ppermute | solution.py:35
  121.2 13.5 %collective-permute-start.35 = (bf16[512,512]{1,0:T(8,128)(2,1)S(1)}, bf16[512,512]{1,0:T(8,128)(2,1)S(1)}, u32[]{:S(2)}, u32[]{:S(2)}) collective-permute-start(bf16[512,512]{1,0:T(8,128)(2,1)S(1)} %join_ring.1.same_ref), channel_id=1, source_target_pairs={{0,8},{8,0},{16,24},{24,16},{32,40},{40,32},{48,56},{56,48},{64,72... | collective-permute-start | bytes 1572872 | tf_op jit(solution)/shard_map/ppermute | solution.py:39
  129.0 9.2 %collective-permute-start.38 = (bf16[256,512]{1,0:T(8,128)(2,1)S(1)}, bf16[256,512]{1,0:T(8,128)(2,1)S(1)}, u32[]{:S(2)}, u32[]{:S(2)}) collective-permute-start(bf16[256,512]{1,0:T(8,128)(2,1)S(1)} %pair_resid.6.rest_0_), channel_id=1, source_target_pairs={{0,6},{1,7},{2,0},{3,1},{4,2},{5,3},{6,4},{7,5},{8,14},{9,15},{10,... | collective-permute-start | bytes 786440 | tf_op jit(solution)/shard_map/ppermute | solution.py:35
  130.0 10.7 %collective-permute-start.37 = (bf16[256,512]{1,0:T(8,128)(2,1)S(1)}, bf16[256,512]{1,0:T(8,128)(2,1)S(1)}, u32[]{:S(2)}, u32[]{:S(2)}) collective-permute-start(bf16[256,512]{1,0:T(8,128)(2,1)S(1)} %pair_resid.6.rest_0_), channel_id=1, source_target_pairs={{0,4},{1,5},{2,6},{3,7},{4,0},{5,1},{6,2},{7,3},{8,12},{9,13},{10,... | collective-permute-start | bytes 786440 | tf_op jit(solution)/shard_map/ppermute | solution.py:35
  130.8 15.4 %collective-permute-start.36 = (bf16[256,512]{1,0:T(8,128)(2,1)S(1)}, bf16[256,512]{1,0:T(8,128)(2,1)S(1)}, u32[]{:S(2)}, u32[]{:S(2)}) collective-permute-start(bf16[256,512]{1,0:T(8,128)(2,1)S(1)} %pair_resid.6.rest_0_), channel_id=1, source_target_pairs={{0,2},{1,3},{2,4},{3,5},{4,6},{5,7},{6,0},{7,1},{8,10},{9,11},{10,... | collective-permute-start | bytes 786440 | tf_op jit(solution)/shard_map/ppermute | solution.py:35
  133.3 18.3 %collective-permute-start.41 = (bf16[256,512]{1,0:T(8,128)(2,1)S(1)}, bf16[256,512]{1,0:T(8,128)(2,1)S(1)}, u32[]{:S(2)}, u32[]{:S(2)}) collective-permute-start(bf16[256,512]{1,0:T(8,128)(2,1)S(1)} %pair_resid.7.rest_0_), channel_id=1, source_target_pairs={{0,6},{1,7},{2,0},{3,1},{4,2},{5,3},{6,4},{7,5},{8,14},{9,15},{10,... | collective-permute-start | bytes 786440 | tf_op jit(solution)/shard_map/ppermute | solution.py:35
  134.7 16.9 %collective-permute-start.40 = (bf16[256,512]{1,0:T(8,128)(2,1)S(1)}, bf16[256,512]{1,0:T(8,128)(2,1)S(1)}, u32[]{:S(2)}, u32[]{:S(2)}) collective-permute-start(bf16[256,512]{1,0:T(8,128)(2,1)S(1)} %pair_resid.7.rest_0_), channel_id=1, source_target_pairs={{0,4},{1,5},{2,6},{3,7},{4,0},{5,1},{6,2},{7,3},{8,12},{9,13},{10,... | collective-permute-start | bytes 786440 | tf_op jit(solution)/shard_map/ppermute | solution.py:35
  138.3 13.4 %collective-permute-start.39 = (bf16[256,512]{1,0:T(8,128)(2,1)S(1)}, bf16[256,512]{1,0:T(8,128)(2,1)S(1)}, u32[]{:S(2)}, u32[]{:S(2)}) collective-permute-start(bf16[256,512]{1,0:T(8,128)(2,1)S(1)} %pair_resid.7.rest_0_), channel_id=1, source_target_pairs={{0,2},{1,3},{2,4},{3,5},{4,6},{5,7},{6,0},{7,1},{8,10},{9,11},{10,... | collective-permute-start | bytes 786440 | tf_op jit(solution)/shard_map/ppermute | solution.py:35
  (30 other events, 310.4 us)

commit v4 on v3

--- a/solution.py
+++ b/solution.py
@@ -213,10 +213,15 @@
     rows, width = toks.shape
     cols = narrow.shape[1]
 
-    def body(place, tok_ref, narrow_ref, *out_refs):
-        partial_keys(place, mode, (tok_ref,), narrow_ref, out_refs)
-
-    return call(body, "first_keys", place, [toks, narrow], keys_outs(mode, rows, cols),
+    def body(place, tok_ref, narrow_hbm, *rest):
+        *out_refs, held, sem = rest
+        copy = pltpu.make_async_copy(narrow_hbm, held, sem)
+        copy.start()
+        copy.wait()
+        partial_keys(place, mode, (tok_ref,), held, out_refs)
+
+    return call(body, "first_keys", place, [toks], keys_outs(mode, rows, cols), apart=[narrow],
+                scratch=[pltpu.VMEM((width, cols), bf16), pltpu.SemaphoreType.DMA(())],
                 flops=2 * rows * width * cols)
 
 
@@ -553,7 +558,7 @@
     home = lax.axis_index("rep")
     run = InOrder(
         jnp.stack(
-            [here // 2, here % 2, home // 4, (home // 2) % 2, home % 2, plan[0]]
+            [here >> 1, here & 1, home >> 2, (home >> 1) & 1, home & 1, plan[0]]
         ).astype(jnp.int32)
     )
     cols = stale_delta.shape[2]

time: 158 us -> 158 us (level)
  transfers between devices with their start and end apart: 43 -> 43, of which waited for: 20 -> 18; matrix products, arithmetic and copies ran while one was open for 1% -> 1% of each run, Pallas kernels for 22% -> 22%
where the time goes in v4:
time: 158 us
  starting transfers between devices  64 us (41%)
  waiting for transfers between devices  43.7 us (28%)
  Pallas kernels  42.7 us (27%)
  local copies, waits for them, and re-layouts  5.2 us (3%)
  between operations  1.85 us (1%)
    pallas_call x26, Pallas kernels, call(): pl.pallas_call(body, in_specs=[pl.BlockSpec(memory_space=pltpu.SMEM)] * (...  42.7 us
    ppermute x27, starting transfers between devices, shift_y(): lax.ppermute(value, 'fsdp', [(i, (i + 2 * hops) % FSDP) for i in range(FS...  33.8 us
    ppermute x27, waiting for transfers between devices, shift_y(): lax.ppermute(value, 'fsdp', [(i, (i + 2 * hops) % FSDP) for i in range(FS...  27 us
    ppermute x6, starting transfers between devices, shift_z(): lax.ppermute(value, 'rep', [(i, (i + 4 * hops) % REP) for i in range(REP)])  14.3 us
    ppermute x6, waiting for transfers between devices, shift_z(): lax.ppermute(value, 'rep', [(i, (i + 4 * hops) % REP) for i in range(REP)])  9.32 us
    ppermute x6, starting transfers between devices, swap_x(): return lax.ppermute(value, 'fsdp', [(i, i ^ 1) for i in range(FSDP)])  7.58 us
    all_to_all x1, starting transfers between devices, on_device(): toks = lax.all_to_all(toks, 'fsdp', split_axis=0, concat_axis=0, tiled=True)  5.48 us
    unnamed x40, local copies, waits for them, and re-layouts  5.11 us
  transfers between devices with their start and end apart: 43, of which 18 were waited for; matrix products, arithmetic and copies ran while one was open for 1% of the time, Pallas kernels for 22%

profile of v4, /device:TPU:0, one launch (start us, length us, event | category | flops | bytes accessed | tf_op | source)
XLA Modules:
  0.0 157.5 jit_solution(5815107571106697544)
XLA Ops:
  1.3 2.4 %regroup_tokens.1 = bf16[8,128,1024]{2,1,0:T(8,128)(2,1)} custom-call(bf16[1,2,128,8192]{3,2,1,0:T(8,128)(2,1)} %src.3), custom_call_target="tpu_custom_call" | custom-call | bytes 1024 | tf_op jit(solution)/shard_map/regroup_tokens/pallas_call | solution.py:65
  3.8 5.5 %all-to-all-start = ((bf16[8,128,1024]{2,1,0:T(8,128)(2,1)}), bf16[8,128,1024]{2,1,0:T(8,128)(2,1)S(1)}, u32[]{:S(2)}, u32[]{:S(2)}) async-start(bf16[8,128,1024]{2,1,0:T(8,128)(2,1)} %regroup_tokens.1), calls=%async_computation | async-start | bytes 4194304 | tf_op jit(solution)/shard_map/all_to_all | solution.py:569
  9.3 3.0 %tokens_by_hops.1 = (bf16[2,128,1024]{2,1,0:T(8,128)(2,1)}, bf16[2,128,1024]{2,1,0:T(8,128)(2,1)}, bf16[2,128,1024]{2,1,0:T(8,128)(2,1)}, bf16[1,128,1024]{2,1,0:T(8,128)(2,1)}, bf16[1,128,1024]{2,1,0:T(8,128)(2,1)}) custom-call(s32[6]{0:T(128)S(1)} %stack.23.place._, bf16[1,2,128,8192]{3,2,1,0:T(8,128)(2,1)} %src.3), custom_call_target="tpu_custom_call" | custom-call | bytes 1024 | tf_op jit(solution)/shard_map/tokens_by_hops/pallas_call | solution.py:65
  13.0 2.1 %collective-permute-start.4 = (bf16[2,128,1024]{2,1,0:T(8,128)(2,1)}, bf16[2,128,1024]{2,1,0:T(8,128)(2,1)S(1)}, u32[]{:S(2)}, u32[]{:S(2)}) collective-permute-start(bf16[2,128,1024]{2,1,0:T(8,128)(2,1)} %get-tuple-element.135), channel_id=1, source_target_pairs={{0,1},{1,0},{2,3},{3,2},{4,5},{5,4},{6,7},{7,6},{8,9},{9,8},{10,11... | collective-permute-start | bytes 1572872 | tf_op jit(solution)/shard_map/ppermute | solution.py:31
  17.2 4.1 %collective-permute-start.3 = (bf16[128,512]{1,0:T(8,128)(2,1)S(1)}, bf16[128,512]{1,0:T(8,128)(2,1)S(1)}, u32[]{:S(2)}, u32[]{:S(2)}) collective-permute-start(bf16[128,512]{1,0:T(8,128)(2,1)S(1)} %get-tuple-element.123), channel_id=1, source_target_pairs={{0,96},{8,104},{16,112},{24,120},{32,0},{40,8},{48,16},{56,24},{64... | collective-permute-start | bytes 393224 | tf_op jit(solution)/shard_map/ppermute | solution.py:47
  24.1 2.3 %collective-permute-start.2 = (bf16[128,512]{1,0:T(8,128)(2,1)S(1)}, bf16[128,512]{1,0:T(8,128)(2,1)S(1)}, u32[]{:S(2)}, u32[]{:S(2)}) collective-permute-start(bf16[128,512]{1,0:T(8,128)(2,1)S(1)} %get-tuple-element.122), channel_id=1, source_target_pairs={{0,64},{8,72},{16,80},{24,88},{32,96},{40,104},{48,112},{56,120},{... | collective-permute-start | bytes 393224 | tf_op jit(solution)/shard_map/ppermute | solution.py:47
  28.2 3.7 %collective-permute-done.1.g1 = bf16[128,512]{1,0:T(8,128)(2,1)S(1)} collective-permute-done((bf16[128,512]{1,0:T(8,128)(2,1)S(1)}, bf16[128,512]{1,0:T(8,128)(2,1)S(1)}, u32[]{:S(2)}, u32[]{:S(2)}) %collective-permute-start.1) | collective-permute-done | bytes 131104 | tf_op jit(solution)/shard_map/ppermute | solution.py:47
  33.9 3.9 %all-to-all-done = bf16[8,128,1024]{2,1,0:T(8,128)(2,1)S(1)} async-done(((bf16[8,128,1024]{2,1,0:T(8,128)(2,1)}), bf16[8,128,1024]{2,1,0:T(8,128)(2,1)S(1)}, u32[]{:S(2)}, u32[]{:S(2)}) %all-to-all-start) | async-done | bytes 2097184 | tf_op jit(solution)/shard_map/all_to_all | solution.py:569
  39.2 1.9 %first_keys.2 = (f32[256,512]{1,0:T(8,128)S(1)}, f32[256,512]{1,0:T(8,128)S(1)}, bf16[256,512]{1,0:T(8,128)(2,1)S(1)}, bf16[256,512]{1,0:T(8,128)(2,1)S(1)}) custom-call(s32[6]{0:T(128)S(1)} %stack.23.place._, bf16[1024,1024]{1,0:T(8,128)(2,1)S(1)} %bitcast.7, bf16[1024,512]{1,0:T(8,128)(2,1)S(1)} %copy-done.10), custom_call_target="tpu_custom_call" | custom-call | bytes 1024 | tf_op jit(solution)/shard_map/first_keys/pallas_call | solution.py:65
  41.4 1.9 %first_keys.3 = (f32[256,512]{1,0:T(8,128)S(1)}, bf16[256,512]{1,0:T(8,128)(2,1)S(1)}, bf16[256,512]{1,0:T(8,128)(2,1)S(1)}, f32[256,512]{1,0:T(8,128)S(1)}) custom-call(s32[6]{0:T(128)S(1)} %stack.23.place._, bf16[1024,1024]{1,0:T(8,128)(2,1)S(1)} %bitcast.8, bf16[1024,512]{1,0:T(8,128)(2,1)S(1)} %copy-done.8), custom_call_target="tpu_custom_call" | custom-call | bytes 1024 | tf_op jit(solution)/shard_map/first_keys/pallas_call | solution.py:65
  43.3 3.1 %collective-permute-start.9 = (bf16[256,512]{1,0:T(8,128)(2,1)S(1)}, bf16[256,512]{1,0:T(8,128)(2,1)S(1)}, u32[]{:S(2)}, u32[]{:S(2)}) collective-permute-start(bf16[256,512]{1,0:T(8,128)(2,1)S(1)} %get-tuple-element.148), channel_id=1, source_target_pairs={{0,6},{1,7},{2,0},{3,1},{4,2},{5,3},{6,4},{7,5},{8,14},{9,15},{10,... | collective-permute-start | bytes 786440 | tf_op jit(solution)/shard_map/ppermute | solution.py:35
  46.4 2.7 %collective-permute-start.7 = (bf16[192,512]{1,0:T(8,128)(2,1)S(1)}, bf16[192,512]{1,0:T(8,128)(2,1)S(1)}, u32[]{:S(2)}, u32[]{:S(2)}) collective-permute-start(bf16[192,512]{1,0:T(8,128)(2,1)S(1)} %copy-done.18), channel_id=1, source_target_pairs={{0,16},{8,24},{16,0},{24,8},{32,48},{40,56},{48,32},{56,40},{64,80... | collective-permute-start | bytes 589832 | tf_op jit(solution)/shard_map/ppermute | solution.py:43
  49.1 1.8 %collective-permute-start.11 = (bf16[256,512]{1,0:T(8,128)(2,1)S(1)}, bf16[256,512]{1,0:T(8,128)(2,1)S(1)}, u32[]{:S(2)}, u32[]{:S(2)}) collective-permute-start(bf16[256,512]{1,0:T(8,128)(2,1)S(1)} %get-tuple-element.152), channel_id=1, source_target_pairs={{0,6},{1,7},{2,0},{3,1},{4,2},{5,3},{6,4},{7,5},{8,14},{9,15},{10,... | collective-permute-start | bytes 786440 | tf_op jit(solution)/shard_map/ppermute | solution.py:35
  55.4 2.1 %collective-permute-start.13 = (bf16[256,512]{1,0:T(8,128)(2,1)S(1)}, bf16[256,512]{1,0:T(8,128)(2,1)S(1)}, u32[]{:S(2)}, u32[]{:S(2)}) collective-permute-start(bf16[256,512]{1,0:T(8,128)(2,1)S(1)} %get-tuple-element.159), channel_id=1, source_target_pairs={{0,2},{1,3},{2,4},{3,5},{4,6},{5,7},{6,0},{7,1},{8,10},{9,11},{10,... | collective-permute-start | bytes 786440 | tf_op jit(solution)/shard_map/ppermute | solution.py:35
  59.9 4.0 %collective-permute-start.16 = (bf16[128,512]{1,0:T(8,128)(2,1)S(1)}, bf16[128,512]{1,0:T(8,128)(2,1)S(1)}, u32[]{:S(2)}, u32[]{:S(2)}) collective-permute-start(bf16[128,512]{1,0:T(8,128)(2,1)S(1)} %get-tuple-element.161.p0), channel_id=1, source_target_pairs={{0,96},{8,104},{16,112},{24,120},{32,0},{40,8},{48,16},{56,24},{64... | collective-permute-start | bytes 393224 | tf_op jit(solution)/shard_map/ppermute | solution.py:47
  64.8 1.9 %collective-permute-start.14 = (bf16[128,512]{1,0:T(8,128)(2,1)S(1)}, bf16[128,512]{1,0:T(8,128)(2,1)S(1)}, u32[]{:S(2)}, u32[]{:S(2)}) collective-permute-start(bf16[128,512]{1,0:T(8,128)(2,1)S(1)} %get-tuple-element.161.p0), channel_id=1, source_target_pairs={{0,32},{8,40},{16,48},{24,56},{32,64},{40,72},{48,80},{56,88},{64,... | collective-permute-start | bytes 393224 | tf_op jit(solution)/shard_map/ppermute | solution.py:47
  70.3 2.0 %collective-permute-start.18 = (bf16[256,512]{1,0:T(8,128)(2,1)S(1)}, bf16[256,512]{1,0:T(8,128)(2,1)S(1)}, u32[]{:S(2)}, u32[]{:S(2)}) collective-permute-start(bf16[256,512]{1,0:T(8,128)(2,1)S(1)} %sum_keys.5.half_ref), channel_id=1, source_target_pairs={{0,1},{1,0},{2,3},{3,2},{4,5},{5,4},{6,7},{7,6},{8,9},{9,8},{10,11... | collective-permute-start | bytes 786440 | tf_op jit(solution)/shard_map/ppermute | solution.py:31
  72.3 1.9 %collective-permute-start.15 = (bf16[128,512]{1,0:T(8,128)(2,1)S(1)}, bf16[128,512]{1,0:T(8,128)(2,1)S(1)}, u32[]{:S(2)}, u32[]{:S(2)}) collective-permute-start(bf16[128,512]{1,0:T(8,128)(2,1)S(1)} %collective-permute-done.14.p1), channel_id=1, source_target_pairs={{0,32},{8,40},{16,48},{24,56},{32,64},{40,72},{48,80},{56,88},{64,... | collective-permute-start | bytes 393224 | tf_op jit(solution)/shard_map/ppermute | solution.py:47
  74.2 4.6 %collective-permute-done.15.p2 = bf16[128,512]{1,0:T(8,128)(2,1)S(1)} collective-permute-done((bf16[128,512]{1,0:T(8,128)(2,1)S(1)}, bf16[128,512]{1,0:T(8,128)(2,1)S(1)}, u32[]{:S(2)}, u32[]{:S(2)}) %collective-permute-start.15) | collective-permute-done | bytes 131104 | tf_op jit(solution)/shard_map/ppermute | solution.py:47
  84.2 2.2 %collective-permute-start.26 = (bf16[256,512]{1,0:T(8,128)(2,1)S(1)}, bf16[256,512]{1,0:T(8,128)(2,1)S(1)}, u32[]{:S(2)}, u32[]{:S(2)}) collective-permute-start(bf16[256,512]{1,0:T(8,128)(2,1)S(1)} %pair_resid.5.rest_0_), channel_id=1, source_target_pairs={{0,6},{1,7},{2,0},{3,1},{4,2},{5,3},{6,4},{7,5},{8,14},{9,15},{10,... | collective-permute-start | bytes 786440 | tf_op jit(solution)/shard_map/ppermute | solution.py:35
  87.2 2.1 %collective-permute-done.23.rest_3_ = bf16[256,512]{1,0:T(8,128)(2,1)S(1)} collective-permute-done((bf16[256,512]{1,0:T(8,128)(2,1)S(1)}, bf16[256,512]{1,0:T(8,128)(2,1)S(1)}, u32[]{:S(2)}, u32[]{:S(2)}) %collective-permute-start.23) | collective-permute-done | bytes 262176 | tf_op jit(solution)/shard_map/ppermute | solution.py:35
  91.4 6.3 %collective-permute-done.21.rest_1_ = bf16[256,512]{1,0:T(8,128)(2,1)S(1)} collective-permute-done((bf16[256,512]{1,0:T(8,128)(2,1)S(1)}, bf16[256,512]{1,0:T(8,128)(2,1)S(1)}, u32[]{:S(2)}, u32[]{:S(2)}) %collective-permute-start.21) | collective-permute-done | bytes 262176 | tf_op jit(solution)/shard_map/ppermute | solution.py:35
  97.7 5.0 %middle_step.2 = (f32[1024,512]{1,0:T(8,128)S(1)}, bf16[1024,512]{1,0:T(8,128)(2,1)S(1)}, bf16[1024,512]{1,0:T(8,128)(2,1)S(1)}, f32[256,512]{1,0:T(8,128)S(1)},...) custom-call(s32[6]{0:T(128)S(1)} %stack.23.place._, ...), custom_call_target="tpu_custom_call" | custom-call | bytes 1024 | tf_op jit(solution)/shard_map/middle_step/pallas_call | solution.py:65
  102.8 2.0 %collective-permute-start.27 = (bf16[256,512]{1,0:T(8,128)(2,1)S(1)}, bf16[256,512]{1,0:T(8,128)(2,1)S(1)}, u32[]{:S(2)}, u32[]{:S(2)}) collective-permute-start(bf16[256,512]{1,0:T(8,128)(2,1)S(1)} %get-tuple-element.184), channel_id=1, source_target_pairs={{0,2},{1,3},{2,4},{3,5},{4,6},{5,7},{6,0},{7,1},{8,10},{9,11},{10,... | collective-permute-start | bytes 786440 | tf_op jit(solution)/shard_map/ppermute | solution.py:35
  105.5 3.0 %collective-permute-done.24.rest_1_ = bf16[256,512]{1,0:T(8,128)(2,1)S(1)} collective-permute-done((bf16[256,512]{1,0:T(8,128)(2,1)S(1)}, bf16[256,512]{1,0:T(8,128)(2,1)S(1)}, u32[]{:S(2)}, u32[]{:S(2)}) %collective-permute-start.24) | collective-permute-done | bytes 262176 | tf_op jit(solution)/shard_map/ppermute | solution.py:35
  108.5 4.9 %middle_step.3 = (f32[1024,512]{1,0:T(8,128)S(1)}, bf16[1024,512]{1,0:T(8,128)(2,1)S(1)}, bf16[1024,512]{1,0:T(8,128)(2,1)S(1)}, f32[256,512]{1,0:T(8,128)S(1)},...) custom-call(s32[6]{0:T(128)S(1)} %stack.23.place._, ...), custom_call_target="tpu_custom_call" | custom-call | bytes 1024 | tf_op jit(solution)/shard_map/middle_step/pallas_call | solution.py:65
  116.6 2.9 %collective-permute-done.28.refs_1_ = bf16[256,512]{1,0:T(8,128)(2,1)S(1)} collective-permute-done((bf16[256,512]{1,0:T(8,128)(2,1)S(1)}, bf16[256,512]{1,0:T(8,128)(2,1)S(1)}, u32[]{:S(2)}, u32[]{:S(2)}) %collective-permute-start.28) | collective-permute-done | bytes 262176 | tf_op jit(solution)/shard_map/ppermute | solution.py:35
  122.5 2.8 %collective-permute-done.31.refs_1_ = bf16[256,512]{1,0:T(8,128)(2,1)S(1)} collective-permute-done((bf16[256,512]{1,0:T(8,128)(2,1)S(1)}, bf16[256,512]{1,0:T(8,128)(2,1)S(1)}, u32[]{:S(2)}, u32[]{:S(2)}) %collective-permute-start.31) | collective-permute-done | bytes 262176 | tf_op jit(solution)/shard_map/ppermute | solution.py:35
  136.2 2.0 %collective-permute-done.38.rest_3_ = bf16[256,512]{1,0:T(8,128)(2,1)S(1)} collective-permute-done((bf16[256,512]{1,0:T(8,128)(2,1)S(1)}, bf16[256,512]{1,0:T(8,128)(2,1)S(1)}, u32[]{:S(2)}, u32[]{:S(2)}) %collective-permute-start.38) | collective-permute-done | bytes 262176 | tf_op jit(solution)/shard_map/ppermute | solution.py:35
  140.6 5.2 %collective-permute-done.36.rest_1_ = bf16[256,512]{1,0:T(8,128)(2,1)S(1)} collective-permute-done((bf16[256,512]{1,0:T(8,128)(2,1)S(1)}, bf16[256,512]{1,0:T(8,128)(2,1)S(1)}, u32[]{:S(2)}, u32[]{:S(2)}) %collective-permute-start.36) | collective-permute-done | bytes 262176 | tf_op jit(solution)/shard_map/ppermute | solution.py:35
  145.9 5.9 %last_step.2 = (f32[1,1024,1024]{2,1,0:T(8,128)}, bf16[1,1024,1024]{2,1,0:T(8,128)(2,1)}, bf16[1,1024,1024]{2,1,0:T(8,128)(2,1)}) custom-call(s32[6]{0:T(128)S(1)} %stack.23.place._, bf16[1,128,1024]{2,1,0:T(8,128)(2,1)S(1)} %copy-done.6, bf16[2,128,1024]{2,1,0:T(8,128)(2,1)S(1)} %collective-permute-done.4.two_hbm.n1.t1, ...), custom_call_target="tpu_custom_call" | custom-call | bytes 1024 | tf_op jit(solution)/shard_map/last_step/pallas_call | solution.py:65
  151.8 5.5 %last_step.3 = (f32[1,1024,1024]{2,1,0:T(8,128)}, bf16[1,1024,1024]{2,1,0:T(8,128)(2,1)}, bf16[1,1024,1024]{2,1,0:T(8,128)(2,1)}) custom-call(s32[6]{0:T(128)S(1)} %stack.23.place._, bf16[1,128,1024]{2,1,0:T(8,128)(2,1)S(1)} %copy-done.6, ...), custom_call_target="tpu_custom_call", output_to_operand_aliasing={{0}: (16, {}), {1}: (17, {}), {2}: (18, {})} | custom-call | bytes 1024 | tf_op jit(solution)/shard_map/last_step/pallas_call | solution.py:65
  (121 shorter events, 50.9 us)
Async XLA Ops:
  3.8 34.1 %all-to-all-start = ((bf16[8,128,1024]{2,1,0:T(8,128)(2,1)}), bf16[8,128,1024]{2,1,0:T(8,128)(2,1)S(1)}, u32[]{:S(2)}, u32[]{:S(2)}) async-start(bf16[8,128,1024]{2,1,0:T(8,128)(2,1)} %regroup_tokens.1), calls=%async_computation | async-start | bytes 4194304 | tf_op jit(solution)/shard_map/all_to_all | solution.py:569
  13.0 33.4 %collective-permute-start.4 = (bf16[2,128,1024]{2,1,0:T(8,128)(2,1)}, bf16[2,128,1024]{2,1,0:T(8,128)(2,1)S(1)}, u32[]{:S(2)}, u32[]{:S(2)}) collective-permute-start(bf16[2,128,1024]{2,1,0:T(8,128)(2,1)} %get-tuple-element.135), channel_id=1, source_target_pairs={{0,1},{1,0},{2,3},{3,2},{4,5},{5,4},{6,7},{7,6},{8,9},{9,8},{10,11... | collective-permute-start | bytes 1572872 | tf_op jit(solution)/shard_map/ppermute | solution.py:31
  15.1 34.0 %collective-permute-start.5 = (bf16[2,128,1024]{2,1,0:T(8,128)(2,1)}, bf16[2,128,1024]{2,1,0:T(8,128)(2,1)S(1)}, u32[]{:S(2)}, u32[]{:S(2)}) collective-permute-start(bf16[2,128,1024]{2,1,0:T(8,128)(2,1)} %get-tuple-element.137), channel_id=1, source_target_pairs={{0,2},{1,3},{2,4},{3,5},{4,6},{5,7},{6,0},{7,1},{8,10},{9,11},{10,... | collective-permute-start | bytes 1572872 | tf_op jit(solution)/shard_map/ppermute | solution.py:35
  21.3 29.6 %collective-permute-start.6 = (bf16[2,128,1024]{2,1,0:T(8,128)(2,1)}, bf16[2,128,1024]{2,1,0:T(8,128)(2,1)}, u32[]{:S(2)}, u32[]{:S(2)}) collective-permute-start(bf16[2,128,1024]{2,1,0:T(8,128)(2,1)} %get-tuple-element.138), channel_id=1, source_target_pairs={{0,6},{1,7},{2,0},{3,1},{4,2},{5,3},{6,4},{7,5},{8,14},{9,15},{10,... | collective-permute-start | bytes 1572872 | tf_op jit(solution)/shard_map/ppermute | solution.py:35
  41.1 13.2 %collective-permute-start.8 = (bf16[256,512]{1,0:T(8,128)(2,1)S(1)}, bf16[256,512]{1,0:T(8,128)(2,1)S(1)}, u32[]{:S(2)}, u32[]{:S(2)}) collective-permute-start(bf16[256,512]{1,0:T(8,128)(2,1)S(1)} %get-tuple-element.145), channel_id=1, source_target_pairs={{0,2},{1,3},{2,4},{3,5},{4,6},{5,7},{6,0},{7,1},{8,10},{9,11},{10,... | collective-permute-start | bytes 786440 | tf_op jit(solution)/shard_map/ppermute | solution.py:35
  43.3 14.2 %collective-permute-start.9 = (bf16[256,512]{1,0:T(8,128)(2,1)S(1)}, bf16[256,512]{1,0:T(8,128)(2,1)S(1)}, u32[]{:S(2)}, u32[]{:S(2)}) collective-permute-start(bf16[256,512]{1,0:T(8,128)(2,1)S(1)} %get-tuple-element.148), channel_id=1, source_target_pairs={{0,6},{1,7},{2,0},{3,1},{4,2},{5,3},{6,4},{7,5},{8,14},{9,15},{10,... | collective-permute-start | bytes 786440 | tf_op jit(solution)/shard_map/ppermute | solution.py:35
  49.1 10.7 %collective-permute-start.11 = (bf16[256,512]{1,0:T(8,128)(2,1)S(1)}, bf16[256,512]{1,0:T(8,128)(2,1)S(1)}, u32[]{:S(2)}, u32[]{:S(2)}) collective-permute-start(bf16[256,512]{1,0:T(8,128)(2,1)S(1)} %get-tuple-element.152), channel_id=1, source_target_pairs={{0,6},{1,7},{2,0},{3,1},{4,2},{5,3},{6,4},{7,5},{8,14},{9,15},{10,... | collective-permute-start | bytes 786440 | tf_op jit(solution)/shard_map/ppermute | solution.py:35
  54.9 9.9 %collective-permute-start.10 = (bf16[256,512]{1,0:T(8,128)(2,1)S(1)}, bf16[256,512]{1,0:T(8,128)(2,1)S(1)}, u32[]{:S(2)}, u32[]{:S(2)}) collective-permute-start(bf16[256,512]{1,0:T(8,128)(2,1)S(1)} %add_keys.2), channel_id=1, source_target_pairs={{0,2},{1,3},{2,4},{3,5},{4,6},{5,7},{6,0},{7,1},{8,10},{9,11},{10,... | collective-permute-start | bytes 786440 | tf_op jit(solution)/shard_map/ppermute | solution.py:35
  55.4 12.6 %collective-permute-start.13 = (bf16[256,512]{1,0:T(8,128)(2,1)S(1)}, bf16[256,512]{1,0:T(8,128)(2,1)S(1)}, u32[]{:S(2)}, u32[]{:S(2)}) collective-permute-start(bf16[256,512]{1,0:T(8,128)(2,1)S(1)} %get-tuple-element.159), channel_id=1, source_target_pairs={{0,2},{1,3},{2,4},{3,5},{4,6},{5,7},{6,0},{7,1},{8,10},{9,11},{10,... | collective-permute-start | bytes 786440 | tf_op jit(solution)/shard_map/ppermute | solution.py:35
  58.1 10.8 %collective-permute-start.12 = (bf16[256,512]{1,0:T(8,128)(2,1)S(1)}, bf16[256,512]{1,0:T(8,128)(2,1)S(1)}, u32[]{:S(2)}, u32[]{:S(2)}) collective-permute-start(bf16[256,512]{1,0:T(8,128)(2,1)S(1)} %add_keys.3), channel_id=1, source_target_pairs={{0,6},{1,7},{2,0},{3,1},{4,2},{5,3},{6,4},{7,5},{8,14},{9,15},{10,... | collective-permute-start | bytes 786440 | tf_op jit(solution)/shard_map/ppermute | solution.py:35
  59.3 24.9 %collective-permute-start.20 = (bf16[2,128,1024]{2,1,0:T(8,128)(2,1)S(1)}, bf16[2,128,1024]{2,1,0:T(8,128)(2,1)S(1)}, u32[]{:S(2)}, u32[]{:S(2)}) collective-permute-start(bf16[2,128,1024]{2,1,0:T(8,128)(2,1)S(1)} %join_blocks.2), channel_id=1, source_target_pairs={{0,1},{1,0},{2,3},{3,2},{4,5},{5,4},{6,7},{7,6},{8,9},{9,8},{10,11... | collective-permute-start | bytes 1572872 | tf_op jit(solution)/shard_map/ppermute | solution.py:31
  59.9 10.4 %collective-permute-start.16 = (bf16[128,512]{1,0:T(8,128)(2,1)S(1)}, bf16[128,512]{1,0:T(8,128)(2,1)S(1)}, u32[]{:S(2)}, u32[]{:S(2)}) collective-permute-start(bf16[128,512]{1,0:T(8,128)(2,1)S(1)} %get-tuple-element.161.p0), channel_id=1, source_target_pairs={{0,96},{8,104},{16,112},{24,120},{32,0},{40,8},{48,16},{56,24},{64... | collective-permute-start | bytes 393224 | tf_op jit(solution)/shard_map/ppermute | solution.py:47
  68.0 11.4 %collective-permute-start.17 = (bf16[256,512]{1,0:T(8,128)(2,1)S(1)}, bf16[256,512]{1,0:T(8,128)(2,1)S(1)}, u32[]{:S(2)}, u32[]{:S(2)}) collective-permute-start(bf16[256,512]{1,0:T(8,128)(2,1)S(1)} %sum_keys.4.half_ref), channel_id=1, source_target_pairs={{0,1},{1,0},{2,3},{3,2},{4,5},{5,4},{6,7},{7,6},{8,9},{9,8},{10,11... | collective-permute-start | bytes 786440 | tf_op jit(solution)/shard_map/ppermute | solution.py:31
  68.9 17.5 %collective-permute-start.19 = (bf16[2,128,1024]{2,1,0:T(8,128)(2,1)S(1)}, bf16[2,128,1024]{2,1,0:T(8,128)(2,1)S(1)}, u32[]{:S(2)}, u32[]{:S(2)}) collective-permute-start(bf16[2,128,1024]{2,1,0:T(8,128)(2,1)S(1)} %join_blocks.3), channel_id=1, source_target_pairs={{0,4},{1,5},{2,6},{3,7},{4,0},{5,1},{6,2},{7,3},{8,12},{9,13},{10,... | collective-permute-start | bytes 1572872 | tf_op jit(solution)/shard_map/ppermute | solution.py:35
  70.3 12.0 %collective-permute-start.18 = (bf16[256,512]{1,0:T(8,128)(2,1)S(1)}, bf16[256,512]{1,0:T(8,128)(2,1)S(1)}, u32[]{:S(2)}, u32[]{:S(2)}) collective-permute-start(bf16[256,512]{1,0:T(8,128)(2,1)S(1)} %sum_keys.5.half_ref), channel_id=1, source_target_pairs={{0,1},{1,0},{2,3},{3,2},{4,5},{5,4},{6,7},{7,6},{8,9},{9,8},{10,11... | collective-permute-start | bytes 786440 | tf_op jit(solution)/shard_map/ppermute | solution.py:31
  80.0 9.3 %collective-permute-start.23 = (bf16[256,512]{1,0:T(8,128)(2,1)S(1)}, bf16[256,512]{1,0:T(8,128)(2,1)S(1)}, u32[]{:S(2)}, u32[]{:S(2)}) collective-permute-start(bf16[256,512]{1,0:T(8,128)(2,1)S(1)} %pair_resid.4.rest_0_), channel_id=1, source_target_pairs={{0,6},{1,7},{2,0},{3,1},{4,2},{5,3},{6,4},{7,5},{8,14},{9,15},{10,... | collective-permute-start | bytes 786440 | tf_op jit(solution)/shard_map/ppermute | solution.py:35
  80.6 10.8 %collective-permute-start.22 = (bf16[256,512]{1,0:T(8,128)(2,1)S(1)}, bf16[256,512]{1,0:T(8,128)(2,1)S(1)}, u32[]{:S(2)}, u32[]{:S(2)}) collective-permute-start(bf16[256,512]{1,0:T(8,128)(2,1)S(1)} %pair_resid.4.rest_0_), channel_id=1, source_target_pairs={{0,4},{1,5},{2,6},{3,7},{4,0},{5,1},{6,2},{7,3},{8,12},{9,13},{10,... | collective-permute-start | bytes 786440 | tf_op jit(solution)/shard_map/ppermute | solution.py:35
  82.3 15.4 %collective-permute-start.21 = (bf16[256,512]{1,0:T(8,128)(2,1)S(1)}, bf16[256,512]{1,0:T(8,128)(2,1)S(1)}, u32[]{:S(2)}, u32[]{:S(2)}) collective-permute-start(bf16[256,512]{1,0:T(8,128)(2,1)S(1)} %pair_resid.4.rest_0_), channel_id=1, source_target_pairs={{0,2},{1,3},{2,4},{3,5},{4,6},{5,7},{6,0},{7,1},{8,10},{9,11},{10,... | collective-permute-start | bytes 786440 | tf_op jit(solution)/shard_map/ppermute | solution.py:35
  84.2 20.6 %collective-permute-start.26 = (bf16[256,512]{1,0:T(8,128)(2,1)S(1)}, bf16[256,512]{1,0:T(8,128)(2,1)S(1)}, u32[]{:S(2)}, u32[]{:S(2)}) collective-permute-start(bf16[256,512]{1,0:T(8,128)(2,1)S(1)} %pair_resid.5.rest_0_), channel_id=1, source_target_pairs={{0,6},{1,7},{2,0},{3,1},{4,2},{5,3},{6,4},{7,5},{8,14},{9,15},{10,... | collective-permute-start | bytes 786440 | tf_op jit(solution)/shard_map/ppermute | solution.py:35
  86.4 19.1 %collective-permute-start.25 = (bf16[256,512]{1,0:T(8,128)(2,1)S(1)}, bf16[256,512]{1,0:T(8,128)(2,1)S(1)}, u32[]{:S(2)}, u32[]{:S(2)}) collective-permute-start(bf16[256,512]{1,0:T(8,128)(2,1)S(1)} %pair_resid.5.rest_0_), channel_id=1, source_target_pairs={{0,4},{1,5},{2,6},{3,7},{4,0},{5,1},{6,2},{7,3},{8,12},{9,13},{10,... | collective-permute-start | bytes 786440 | tf_op jit(solution)/shard_map/ppermute | solution.py:35
  89.3 19.1 %collective-permute-start.24 = (bf16[256,512]{1,0:T(8,128)(2,1)S(1)}, bf16[256,512]{1,0:T(8,128)(2,1)S(1)}, u32[]{:S(2)}, u32[]{:S(2)}) collective-permute-start(bf16[256,512]{1,0:T(8,128)(2,1)S(1)} %pair_resid.5.rest_0_), channel_id=1, source_target_pairs={{0,2},{1,3},{2,4},{3,5},{4,6},{5,7},{6,0},{7,1},{8,10},{9,11},{10,... | collective-permute-start | bytes 786440 | tf_op jit(solution)/shard_map/ppermute | solution.py:35
  102.7 12.8 %collective-permute-start.29 = (bf16[256,512]{1,0:T(8,128)(2,1)S(1)}, bf16[256,512]{1,0:T(8,128)(2,1)S(1)}, u32[]{:S(2)}, u32[]{:S(2)}) collective-permute-start(bf16[256,512]{1,0:T(8,128)(2,1)S(1)} %get-tuple-element.186), channel_id=1, source_target_pairs={{0,6},{1,7},{2,0},{3,1},{4,2},{5,3},{6,4},{7,5},{8,14},{9,15},{10,... | collective-permute-start | bytes 786440 | tf_op jit(solution)/shard_map/ppermute | solution.py:35
  102.8 13.8 %collective-permute-start.27 = (bf16[256,512]{1,0:T(8,128)(2,1)S(1)}, bf16[256,512]{1,0:T(8,128)(2,1)S(1)}, u32[]{:S(2)}, u32[]{:S(2)}) collective-permute-start(bf16[256,512]{1,0:T(8,128)(2,1)S(1)} %get-tuple-element.184), channel_id=1, source_target_pairs={{0,2},{1,3},{2,4},{3,5},{4,6},{5,7},{6,0},{7,1},{8,10},{9,11},{10,... | collective-permute-start | bytes 786440 | tf_op jit(solution)/shard_map/ppermute | solution.py:35
  104.8 14.7 %collective-permute-start.28 = (bf16[256,512]{1,0:T(8,128)(2,1)S(1)}, bf16[256,512]{1,0:T(8,128)(2,1)S(1)}, u32[]{:S(2)}, u32[]{:S(2)}) collective-permute-start(bf16[256,512]{1,0:T(8,128)(2,1)S(1)} %get-tuple-element.185), channel_id=1, source_target_pairs={{0,4},{1,5},{2,6},{3,7},{4,0},{5,1},{6,2},{7,3},{8,12},{9,13},{10,... | collective-permute-start | bytes 786440 | tf_op jit(solution)/shard_map/ppermute | solution.py:35
  115.5 9.8 %collective-permute-start.31 = (bf16[256,512]{1,0:T(8,128)(2,1)S(1)}, bf16[256,512]{1,0:T(8,128)(2,1)S(1)}, u32[]{:S(2)}, u32[]{:S(2)}) collective-permute-start(bf16[256,512]{1,0:T(8,128)(2,1)S(1)} %get-tuple-element.190), channel_id=1, source_target_pairs={{0,4},{1,5},{2,6},{3,7},{4,0},{5,1},{6,2},{7,3},{8,12},{9,13},{10,... | collective-permute-start | bytes 786440 | tf_op jit(solution)/shard_map/ppermute | solution.py:35
  121.1 13.4 %collective-permute-start.35 = (bf16[512,512]{1,0:T(8,128)(2,1)S(1)}, bf16[512,512]{1,0:T(8,128)(2,1)S(1)}, u32[]{:S(2)}, u32[]{:S(2)}) collective-permute-start(bf16[512,512]{1,0:T(8,128)(2,1)S(1)} %join_ring.1.same_ref), channel_id=1, source_target_pairs={{0,8},{8,0},{16,24},{24,16},{32,40},{40,32},{48,56},{56,48},{64,72... | collective-permute-start | bytes 1572872 | tf_op jit(solution)/shard_map/ppermute | solution.py:39
  128.9 9.2 %collective-permute-start.38 = (bf16[256,512]{1,0:T(8,128)(2,1)S(1)}, bf16[256,512]{1,0:T(8,128)(2,1)S(1)}, u32[]{:S(2)}, u32[]{:S(2)}) collective-permute-start(bf16[256,512]{1,0:T(8,128)(2,1)S(1)} %pair_resid.6.rest_0_), channel_id=1, source_target_pairs={{0,6},{1,7},{2,0},{3,1},{4,2},{5,3},{6,4},{7,5},{8,14},{9,15},{10,... | collective-permute-start | bytes 786440 | tf_op jit(solution)/shard_map/ppermute | solution.py:35
  129.7 11.0 %collective-permute-start.37 = (bf16[256,512]{1,0:T(8,128)(2,1)S(1)}, bf16[256,512]{1,0:T(8,128)(2,1)S(1)}, u32[]{:S(2)}, u32[]{:S(2)}) collective-permute-start(bf16[256,512]{1,0:T(8,128)(2,1)S(1)} %pair_resid.6.rest_0_), channel_id=1, source_target_pairs={{0,4},{1,5},{2,6},{3,7},{4,0},{5,1},{6,2},{7,3},{8,12},{9,13},{10,... | collective-permute-start | bytes 786440 | tf_op jit(solution)/shard_map/ppermute | solution.py:35
  130.7 15.2 %collective-permute-start.36 = (bf16[256,512]{1,0:T(8,128)(2,1)S(1)}, bf16[256,512]{1,0:T(8,128)(2,1)S(1)}, u32[]{:S(2)}, u32[]{:S(2)}) collective-permute-start(bf16[256,512]{1,0:T(8,128)(2,1)S(1)} %pair_resid.6.rest_0_), channel_id=1, source_target_pairs={{0,2},{1,3},{2,4},{3,5},{4,6},{5,7},{6,0},{7,1},{8,10},{9,11},{10,... | collective-permute-start | bytes 786440 | tf_op jit(solution)/shard_map/ppermute | solution.py:35
  133.1 18.7 %collective-permute-start.41 = (bf16[256,512]{1,0:T(8,128)(2,1)S(1)}, bf16[256,512]{1,0:T(8,128)(2,1)S(1)}, u32[]{:S(2)}, u32[]{:S(2)}) collective-permute-start(bf16[256,512]{1,0:T(8,128)(2,1)S(1)} %pair_resid.7.rest_0_), channel_id=1, source_target_pairs={{0,6},{1,7},{2,0},{3,1},{4,2},{5,3},{6,4},{7,5},{8,14},{9,15},{10,... | collective-permute-start | bytes 786440 | tf_op jit(solution)/shard_map/ppermute | solution.py:35
  134.6 17.2 %collective-permute-start.40 = (bf16[256,512]{1,0:T(8,128)(2,1)S(1)}, bf16[256,512]{1,0:T(8,128)(2,1)S(1)}, u32[]{:S(2)}, u32[]{:S(2)}) collective-permute-start(bf16[256,512]{1,0:T(8,128)(2,1)S(1)} %pair_resid.7.rest_0_), channel_id=1, source_target_pairs={{0,4},{1,5},{2,6},{3,7},{4,0},{5,1},{6,2},{7,3},{8,12},{9,13},{10,... | collective-permute-start | bytes 786440 | tf_op jit(solution)/shard_map/ppermute | solution.py:35
  138.1 13.7 %collective-permute-start.39 = (bf16[256,512]{1,0:T(8,128)(2,1)S(1)}, bf16[256,512]{1,0:T(8,128)(2,1)S(1)}, u32[]{:S(2)}, u32[]{:S(2)}) collective-permute-start(bf16[256,512]{1,0:T(8,128)(2,1)S(1)} %pair_resid.7.rest_0_), channel_id=1, source_target_pairs={{0,2},{1,3},{2,4},{3,5},{4,6},{5,7},{6,0},{7,1},{8,10},{9,11},{10,... | collective-permute-start | bytes 786440 | tf_op jit(solution)/shard_map/ppermute | solution.py:35
  (30 other events, 309.5 us)
